TPU v7x, 256 devices: a whole 4x4x8 slice. The times are simulated.
256 devices in a mesh: row: 32 (over x_hi, z, core), blk: 8 (over y, x_lo).
Axes of the slice: x: 4 (x_hi: 2, x_lo: 2; x = x_hi * 2 + x_lo), y: 4, z: 8, core: 2. Of those that a mesh axis runs over, the one named last changes fastest.
Arguments:
- features: bfloat16 [98304, 256], P(('row', 'blk')), may hold values from -6 to 6
- adj_tiles: bfloat16 [32, 2304, 128, 128], P('row', 'blk'), may hold values from -0.15625 to 0.15625
- tile_row: int32 [32, 2304], P('row', 'blk'), may hold values from 0 to 23, as said below
- tile_col: int32 [32, 2304], P('row', 'blk'), may hold values from 0 to 96, as said below
- weight: bfloat16 [256, 256], replicated, may hold values from -0.375 to 0.375
- bias_vec: float32 [256], replicated, may hold values from -3 to 3
- cotangent: bfloat16 [98304, 256], P(('row', 'blk')), may hold values from -6 to 6
Outputs:
- activated: bfloat16 [98304, 256], P(('row', 'blk'))
- grad_x: bfloat16 [98304, 256], P(('row', 'blk'))
- grad_w: float32 [256, 256], replicated
- grad_b: float32 [256], replicated
Inputs may be any that keep to these rules, and one draw needn't show every extreme that they name: On each device the 288 slots of tile_col are non-decreasing; live slots hold 0 to 95 and come first, dead slots hold 96; live (tile_row, tile_col) pairs on one device are distinct; a device has 72 to 288 live slots, and at least one device has 288. `tile_row`: dead slots hold 0.
All inputs are finite; a program needn't handle non-finite values.
Results may differ from a plain program's by a relative error of at most 0.0075.
Values may be sent and summed in bfloat16 or wider, within the bound.
No kernel may reach another device: no remote copies, remote signals or barrier semaphores. Data moves between devices by JAX's collectives and lax.ppermute only.
A program may use at most 128 MiB of HBM per device.

v0:
```python
import math

import jax
import jax.numpy as jnp
from jax import lax
from jax.sharding import PartitionSpec as P

turn_tiles = 24


def gather_rows(summed, tile_vals, rows_in, cols_in, source, first_col, low_end, high_end):
    piece_len = source.shape[0]
    slot_count = summed.shape[0]

    def gather_turn(turn_index, running):
        offset = turn_index * turn_tiles
        tile_block = lax.dynamic_slice_in_dim(tile_vals, offset, turn_tiles, 0)
        blk_rows = lax.dynamic_slice_in_dim(rows_in, offset, turn_tiles, 0)
        blk_cols = lax.dynamic_slice_in_dim(cols_in, offset, turn_tiles, 0)
        positions = offset + jnp.arange(turn_tiles, dtype=jnp.int32)
        active = (positions >= low_end) & (positions < high_end)
        local_col = jnp.clip(blk_cols - first_col, 0, piece_len - 1)
        picked = source[local_col]
        contrib = jnp.einsum("kij,kjf->kif", tile_block, picked, preferred_element_type=jnp.float32)
        target = jnp.where(active, blk_rows, slot_count)
        return running.at[target].add(contrib, mode="drop")

    return lax.fori_loop(
        low_end // turn_tiles, (high_end + turn_tiles - 1) // turn_tiles, gather_turn, summed
    )


def scatter_cols(summed, tile_vals, rows_in, cols_in, err_slab, first_col, low_end, high_end):
    slot_count = summed.shape[0]

    def scatter_turn(turn_index, running):
        offset = turn_index * turn_tiles
        tile_block = lax.dynamic_slice_in_dim(tile_vals, offset, turn_tiles, 0)
        blk_rows = lax.dynamic_slice_in_dim(rows_in, offset, turn_tiles, 0)
        blk_cols = lax.dynamic_slice_in_dim(cols_in, offset, turn_tiles, 0)
        positions = offset + jnp.arange(turn_tiles, dtype=jnp.int32)
        active = (positions >= low_end) & (positions < high_end)
        picked = err_slab[blk_rows]
        contrib = jnp.einsum("kji,kjf->kif", tile_block, picked, preferred_element_type=jnp.float32)
        target = jnp.where(active, blk_cols - first_col, slot_count)
        return running.at[target].add(contrib, mode="drop")

    return lax.fori_loop(
        low_end // turn_tiles, (high_end + turn_tiles - 1) // turn_tiles, scatter_turn, summed
    )


def below(cols_in, limit):
    return jnp.sum((cols_in < limit).astype(jnp.int32))


def shards(features, adj_tiles, tile_row, tile_col, weight, bias_vec, cotangent):
    tile_vals = adj_tiles[0]
    rows_in = tile_row[0]
    cols_in = tile_col[0]
    tile_size = tile_vals.shape[-1]
    node_rows = features.shape[0]
    hidden = features.shape[1]
    row_devices = lax.axis_size("row")
    blk_devices = lax.axis_size("blk")
    row_tiles = blk_devices * node_rows // tile_size
    col_tiles = row_devices * node_rows // tile_size
    live_end = below(cols_in, col_tiles)
    own_blocks = features.reshape(node_rows // tile_size, tile_size, hidden)
    zeroed = jnp.zeros((row_tiles, tile_size, hidden), jnp.float32)
    col_slab = lax.all_gather(own_blocks, "row", axis=0, tiled=True)
    partial_fwd = gather_rows(zeroed, tile_vals, rows_in, cols_in, col_slab, 0, 0, live_end)
    aggregated = lax.psum_scatter(
        partial_fwd.reshape(row_tiles * tile_size, hidden), "blk", scatter_dimension=0, tiled=True
    ).astype(jnp.bfloat16)
    pre_act = jnp.dot(aggregated, weight, preferred_element_type=jnp.float32) + bias_vec
    value_out, pullback = jax.vjp(lambda v: jax.nn.gelu(v, approximate=True), pre_act)
    activated = value_out.astype(jnp.bfloat16)
    delta_grad = pullback(cotangent.astype(jnp.float32))[0].astype(jnp.bfloat16)
    grad_scale = 1.0 / math.sqrt(node_rows * row_devices * blk_devices)
    weight_terms = lax.psum(
        (
            jnp.einsum("nf,ng->fg", aggregated, delta_grad, preferred_element_type=jnp.float32)
            * grad_scale,
            jnp.sum(delta_grad.astype(jnp.float32), axis=0) * grad_scale,
        ),
        ("row", "blk"),
    )
    back_feat = jnp.einsum(
        "ng,fg->nf", delta_grad, weight, preferred_element_type=jnp.float32
    ).astype(jnp.bfloat16)
    err_slab = lax.all_gather(
        back_feat.reshape(node_rows // tile_size, tile_size, hidden), "blk", axis=0, tiled=True
    )
    start_zero = jnp.zeros((col_tiles, tile_size, hidden), jnp.float32)
    partial_back = scatter_cols(start_zero, tile_vals, rows_in, cols_in, err_slab, 0, 0, live_end)
    grad_x = lax.psum_scatter(
        partial_back.reshape(col_tiles * tile_size, hidden), "row", scatter_dimension=0, tiled=True
    )
    return (activated, grad_x.astype(jnp.bfloat16), weight_terms[0], weight_terms[1])


def solution(mesh):
    return jax.shard_map(
        shards,
        mesh=mesh,
        in_specs=(
            P(("row", "blk"), None),
            P("row", "blk", None, None),
            P("row", "blk"),
            P("row", "blk"),
            P(),
            P(),
            P(("row", "blk"), None),
        ),
        out_specs=(P(("row", "blk"), None), P(("row", "blk"), None), P(), P()),
        check_vma=False,
    )
```

profile of v0, /device:TPU:2, one launch (start us, length us, event | category | flops | bytes accessed | tf_op | source)
XLA Modules:
  0.0 1032.8 jit_solution(4332578193671647481)
XLA Ops:
  7.2 0.7 all-gather.3.cloned.1.call-update
  8.0 0.7 reduce
  8.7 0.6 convert_reduce_fusion.1
  10.0 0.7 reduce.1
  10.7 96.7 %all-gather.3.cloned.1.call-done = bf16[96,128,256]{2,1,0:T(8,128)(2,1)} async-done(((bf16[3,128,256]{2,1,0:T(8,128)(2,1)}), bf16[96,128,256]{2,1,0:T(8,128)(2,1)}) %all-gather.3.cloned.1.call-update) | async-done | bytes 6291472 | tf_op jit(solution)/shard_map/all_gather | solution.py:71
  107.4 2.1 broadcast_in_dim.26
  109.4 79.5 %while.20 = (s32[]{:T(128)}, f32[24,128,256]{2,1,0:T(8,128)}, s32[]{:T(128)}, s32[]{:T(128)}, s32[288]{0:T(512)S(1)}, /*index=5*/bf16[288,128,128]{2,1,0:T(8,128...) while((s32[]{:T(128)}, f32[24,128,256]{2,1,0:T(8,128)}, ...), condition=%wide.region_3.4_spmd, body=%wide.region_1.3_spmd.sunk | while | flops 202114336 | bytes 18092884 | solution.py:28
  109.4 0.7 compare_select_fusion.6
  110.2 4.7 gather_fusion
  114.8 2.2 fusion.33
  117.0 8.1 scatter_fusion
  125.2 0.7 compare_select_fusion.6
  125.9 4.7 gather_fusion
  130.6 2.2 fusion.33
  132.8 8.0 scatter_fusion
  140.8 0.7 compare_select_fusion.6
  141.5 4.7 gather_fusion
  146.2 2.2 fusion.33
  148.4 8.0 scatter_fusion
  156.4 0.7 compare_select_fusion.6
  157.1 4.7 gather_fusion
  161.8 2.2 fusion.33
  164.0 8.2 scatter_fusion
  172.1 0.7 compare_select_fusion.6
  172.9 4.7 gather_fusion
  177.5 2.2 fusion.33
  179.7 9.2 scatter_fusion
  189.0 0.0 all-gather.5.cloned.1.call-start
  189.0 180.6 %reduce-scatter.3.cloned.1.call-done = f32[384,256]{1,0:T(8,128)} async-done(((f32[3072,256]{1,0:T(8,128)}), f32[384,256]{1,0:T(8,128)}) %reduce-scatter.3.cloned.1.call-update) | async-done | bytes 393232 | tf_op jit(solution)/shard_map/reduce_scatter | solution.py:73
  369.7 2.2 convert_reduce_fusion
  371.8 0.9 convolution_convert_fusion
  372.8 0.0 reduce-scatter.5.cloned.1.call-start
  372.8 12.7 %copy.13 = bf16[1,288,128,128]{2,3,1,0:T(8,128)(2,1)} copy(bf16[1,288,128,128]{3,2,1,0:T(8,128)(2,1)} %bitcast.19) | data formatting | bytes 18874368 | tf_op args[1]
  385.5 33.0 %all-gather.5.cloned.1.call-done = bf16[24,128,256]{2,1,0:T(8,128)(2,1)} async-done(((bf16[3,128,256]{2,1,0:T(8,128)(2,1)}), bf16[24,128,256]{2,1,0:T(8,128)(2,1)}) %all-gather.5.cloned.1.call-update) | async-done | bytes 1572880 | tf_op jit(solution)/shard_map/all_gather | solution.py:92
  418.5 6.1 broadcast_in_dim.27
  424.6 72.1 %while.21 = (s32[]{:T(128)}, f32[96,128,256]{2,1,0:T(8,128)}, s32[]{:T(128)}, s32[]{:T(128)}, s32[288]{0:T(512)S(1)}, /*index=5*/bf16[288,128,128]{1,2,0:T(8,128...) while((s32[]{:T(128)}, f32[96,128,256]{2,1,0:T(8,128)}, ...), condition=%wide.region_7.8_spmd, body=%wide.region_5.7_spmd.sunk | while | flops 202114320 | bytes 18092884 | solution.py:48
  424.6 0.7 compare_select_fusion.7
  425.4 3.3 gather_fusion.1
  428.6 2.2 fusion.36
  430.8 8.1 scatter_fusion.1
  438.9 0.7 compare_select_fusion.7
  439.6 3.3 gather_fusion.1
  442.9 2.2 fusion.36
  445.1 8.0 scatter_fusion.1
  453.1 0.7 compare_select_fusion.7
  453.8 3.3 gather_fusion.1
  457.0 2.2 fusion.36
  459.2 8.2 scatter_fusion.1
  467.4 0.7 compare_select_fusion.7
  468.1 3.3 gather_fusion.1
  471.4 2.2 fusion.36
  473.6 7.9 scatter_fusion.1
  481.5 0.7 compare_select_fusion.7
  482.2 3.3 gather_fusion.1
  485.5 2.2 fusion.36
  487.7 9.0 scatter_fusion.1
  496.8 0.0 all-reduce.2.cloned.1.call-start
  496.8 0.9 copy-done.1
  497.7 1.0 convolution_multiply_fusion
  498.7 178.6 %psum.15 = f32[256]{0:T(256)} all-reduce(f32[256]{0:T(256)S(1)} %broadcast_multiply_fusion), channel_id=1, replica_groups=mesh['row'=32,'blk'=8] {'row','blk'}, use_global_device_ids=true, to_apply=%region_11.12 | all-reduce | flops 256 | bytes 2048 | tf_op jit(solution)/shard_map/psum | solution.py:81
  677.3 91.8 %reduce-scatter.5.cloned.1.call-done = f32[384,256]{1,0:T(8,128)} async-done(((f32[12288,256]{1,0:T(8,128)}), f32[384,256]{1,0:T(8,128)}) %reduce-scatter.5.cloned.1.call-update) | async-done | bytes 393232 | tf_op jit(solution)/shard_map/reduce_scatter | solution.py:97
  769.1 1.7 convert_element_type.30
  770.8 253.8 %all-reduce.2.cloned.1.call-done = f32[256,256]{1,0:T(8,128)} async-done(((f32[256,256]{1,0:T(8,128)}), f32[256,256]{1,0:T(8,128)}) %all-reduce.2.cloned.1.call-update) | async-done | bytes 262160 | tf_op jit(solution)/shard_map/psum | solution.py:81
  1024.6 1.7 copy.31
  (24 shorter events, 0.2 us)
Async XLA Ops:
  7.2 362.5 %copy-start = (bf16[256,256]{1,0:T(8,128)(2,1)S(1)}, bf16[256,256]{1,0:T(8,128)(2,1)}, u32[]{:S(2)}) copy-start(bf16[256,256]{1,0:T(8,128)(2,1)} %param.15) | copy-start | bytes 393220
  7.2 100.2 %all-gather.3.cloned.1.call-start = ((), (), s32[]{:S(2)}) async-start(), calls=%async_computation.2 | async-start | bytes 6488064 | tf_op jit(solution)/shard_map/all_gather | solution.py:71
  7.9 361.7 %reduce-scatter.3.cloned.1.call-start = ((), (), s32[]{:S(2)}) async-start(), calls=%async_computation.3 | async-start | bytes 3538944 | tf_op jit(solution)/shard_map/reduce_scatter | solution.py:73
  188.9 180.7 %copy-start.2 = (bf16[384,256]{1,0:T(8,128)(2,1)S(1)}, bf16[384,256]{1,0:T(8,128)(2,1)}, u32[]{:S(2)}) copy-start(bf16[384,256]{1,0:T(8,128)(2,1)} %param.17) | copy-start | bytes 589828
  188.9 180.7 %copy-start.3 = (f32[256]{0:T(256)S(1)}, f32[256]{0:T(256)}, u32[]{:S(2)}) copy-start(f32[256]{0:T(256)} %param.16) | copy-start | bytes 3076
  189.0 229.5 %all-gather.5.cloned.1.call-start = ((), (), s32[]{:S(2)}) async-start(), calls=%async_computation.4 | async-start | bytes 1769472 | tf_op jit(solution)/shard_map/all_gather | solution.py:92
  372.8 396.3 %reduce-scatter.5.cloned.1.call-start = ((), (), s32[]{:S(2)}) async-start(), calls=%async_computation.5 | async-start | bytes 12976128 | tf_op jit(solution)/shard_map/reduce_scatter | solution.py:97
  496.7 1.0 copy-start.1
  496.8 527.9 %all-reduce.2.cloned.1.call-start = ((), (), s32[]{:S(2)}) async-start(), calls=%async_computation.6 | async-start | bytes 524288 | tf_op jit(solution)/shard_map/psum | solution.py:81
Sparse Core Ops, SparseCore 0:
  10.8 96.5 all-gather.2
  189.1 180.5 reduce-scatter.2
  372.9 45.5 all-gather.4
  496.9 272.1 reduce-scatter.4
  775.0 249.6 all-reduce.1
where the time goes:
time: 1040 us; the launch traced here: 1030 us
  waiting for transfers between devices  657 us (63%)
  blocking collectives  179 us (17%)
  other arithmetic  93.6 us (9%)
  local copies, waits for them, and re-layouts  63 us (6%)
  matrix products  26.1 us (3%)
  between operations  14.5 us (1%)
    psum x1, waiting for transfers between devices, shards(): lax.psum((jnp.einsum('nf,ng->fg', aggregated, delta_grad, preferred_eleme...  254 us
    reduce_scatter x1, waiting for transfers between devices, shards(): lax.psum_scatter(partial_fwd.reshape(row_tiles * tile_size, hidden), 'blk...  181 us
    psum x1, blocking collectives, shards(): lax.psum((jnp.einsum('nf,ng->fg', aggregated, delta_grad, preferred_eleme...  179 us
    all_gather x1, waiting for transfers between devices, shards(): col_slab = lax.all_gather(own_blocks, 'row', axis=0, tiled=True)  96.7 us
    reduce_scatter x1, waiting for transfers between devices, shards(): lax.psum_scatter(partial_back.reshape(col_tiles * tile_size, hidden), 'ro...  91.8 us
    scatter-add x5, other arithmetic, gather_turn(): return running.at[target].add(contrib, mode='drop')  41.5 us
    scatter-add x5, other arithmetic, scatter_turn(): return running.at[target].add(contrib, mode='drop')  41.1 us
    all_gather x1, waiting for transfers between devices, shards(): lax.all_gather(back_feat.reshape(node_rows // tile_size, tile_size, hidde...  33 us
  transfers between devices with their start and end apart: 5, of which 5 were waited for; matrix products, arithmetic and copies ran while one was open for 2% of the time, Pallas kernels for 0%

commit v1 on v0

v1 whole, which is shorter than its diff:
```python
import functools
import math

import jax
import jax.numpy as jnp
from jax import lax
from jax.experimental import pallas as pl
from jax.experimental.pallas import tpu as pltpu
from jax.sharding import Mesh, PartitionSpec as P

XH, Z, CORE, Y, XL = 2, 8, 2, 4, 2
AXES = ("xh", "z", "core", "y", "xl")
BLK = ("y", "xl")
N_BLK = Y * XL
TILE = 128
HIDDEN = 256
PER = 3
NB = PER * TILE
TR = N_BLK * PER
TC = XH * Z * CORE * PER
K = 288
GROUP = 16
GROUPS = K // GROUP
VMEM_BYTES = 56 * 2**20
bf16 = jnp.bfloat16
f32 = jnp.float32

ANY = pl.BlockSpec(memory_space=pl.ANY)
VMEM = pl.BlockSpec(memory_space=pltpu.VMEM)


def swap(axis):
    return lambda v: lax.ppermute(v, axis, [(0, 1), (1, 0)])


def turn(v, step):
    return lax.ppermute(v, "z", [(i, (i + step) % Z) for i in range(Z)])


def fetch_group(live, adj_hbm, adj, sem, g):
    first = jnp.minimum(g * GROUP, K - GROUP)
    return pltpu.make_async_copy(adj_hbm.at[pl.ds(first, GROUP)], adj.at[g], sem.at[g])


def start_groups(live_ref, adj_hbm, adj, sem):
    live = live_ref[0]
    groups = (live + GROUP - 1) // GROUP

    def begin(g, carry):
        fetch_group(live, adj_hbm, adj, sem, g).start()
        return carry

    lax.fori_loop(0, groups, begin, 0)
    return live, groups


def forward_kernel(live_ref, row_ref, pos_ref, adj_hbm, *refs):
    pieces = refs[:-6]
    out_ref, adj, slab, acc, adj_sem, piece_sem = refs[-6:]
    copies = []
    at = 0
    for n, piece in enumerate(pieces):
        size = piece.shape[0]
        copies.append(pltpu.make_async_copy(piece, slab.at[pl.ds(at, size)], piece_sem.at[n]))
        at += size
    for copy in copies:
        copy.start()
    live, groups = start_groups(live_ref, adj_hbm, adj, adj_sem)
    acc[...] = jnp.zeros_like(acc)
    for copy in copies:
        copy.wait()

    def step(g, carry):
        fetch_group(live, adj_hbm, adj, adj_sem, g).wait()
        for u in range(GROUP):
            k = g * GROUP + u
            row = jnp.where(k < live, row_ref[k], TR)
            acc[row] += jnp.dot(adj[g, u], slab[pos_ref[k]], preferred_element_type=f32)
        return carry

    lax.fori_loop(0, groups, step, 0)
    out_ref[...] = acc[:TR].astype(bf16)


def forward_tiles(live, rows, pos, adj, pieces):
    return pl.pallas_call(
        forward_kernel,
        out_shape=jax.ShapeDtypeStruct((TR, TILE, HIDDEN), bf16),
        grid_spec=pltpu.PrefetchScalarGridSpec(
            num_scalar_prefetch=3,
            grid=(),
            in_specs=[ANY] * (1 + len(pieces)),
            out_specs=VMEM,
            scratch_shapes=[
                pltpu.VMEM((GROUPS, GROUP, TILE, TILE), bf16),
                pltpu.VMEM((TC, TILE, HIDDEN), bf16),
                pltpu.VMEM((TR + 1, TILE, HIDDEN), f32),
                pltpu.SemaphoreType.DMA((GROUPS,)),
                pltpu.SemaphoreType.DMA((len(pieces),)),
            ],
        ),
        compiler_params=pltpu.CompilerParams(vmem_limit_bytes=VMEM_BYTES),
        name="forward_tiles",
    )(live, rows, pos, adj, *pieces)


def backward_kernel(live_ref, row_ref, pos_ref, adj_hbm, err_hbm, *refs):
    outs = refs[:-5]
    adj, err, acc, adj_sem, err_sem = refs[-5:]
    err_copy = pltpu.make_async_copy(err_hbm, err, err_sem)
    err_copy.start()
    live, groups = start_groups(live_ref, adj_hbm, adj, adj_sem)
    acc[...] = jnp.zeros_like(acc)
    err_copy.wait()

    def step(g, carry):
        fetch_group(live, adj_hbm, adj, adj_sem, g).wait()
        for u in range(GROUP):
            k = g * GROUP + u
            pos = jnp.where(k < live, pos_ref[k], TC)
            acc[pos] += lax.dot_general(
                adj[g, u], err[row_ref[k]], (((0,), (0,)), ((), ())), preferred_element_type=f32
            )
        return carry

    lax.fori_loop(0, groups, step, 0)
    at = 0
    for out in outs:
        out[...] = acc[at : at + out.shape[0]].astype(bf16)
        at += out.shape[0]


def backward_tiles(live, rows, pos, adj, err, sizes):
    return pl.pallas_call(
        backward_kernel,
        out_shape=[jax.ShapeDtypeStruct((size, TILE, HIDDEN), bf16) for size in sizes],
        grid_spec=pltpu.PrefetchScalarGridSpec(
            num_scalar_prefetch=3,
            grid=(),
            in_specs=[ANY, ANY],
            out_specs=[VMEM] * len(sizes),
            scratch_shapes=[
                pltpu.VMEM((GROUPS, GROUP, TILE, TILE), bf16),
                pltpu.VMEM((TR, TILE, HIDDEN), bf16),
                pltpu.VMEM((TC + 1, TILE, HIDDEN), f32),
                pltpu.SemaphoreType.DMA((GROUPS,)),
                pltpu.SemaphoreType.DMA,
            ],
        ),
        compiler_params=pltpu.CompilerParams(vmem_limit_bytes=VMEM_BYTES),
        name="backward_tiles",
    )(live, rows, pos, adj, err)


def dense_kernel(scale, parts_ref, weight_ref, bias_ref, cot_ref, act_ref, back_ref, grad_ref):
    summed = parts_ref[0].astype(f32)
    for b in range(1, N_BLK):
        summed = summed + parts_ref[b].astype(f32)
    agg = summed.astype(bf16)
    weight = weight_ref[...]
    v = jnp.dot(agg, weight, preferred_element_type=f32) + bias_ref[...]
    c = math.sqrt(2.0 / math.pi)
    t = jnp.tanh(c * (v + 0.044715 * (v * v * v)))
    act_ref[...] = (0.5 * v * (1.0 + t)).astype(bf16)
    slope = 0.5 * (1.0 + t) + 0.5 * v * (1.0 - t * t) * (c * (1.0 + 3.0 * 0.044715 * (v * v)))
    delta = (cot_ref[...].astype(f32) * slope).astype(bf16)
    back = lax.dot_general(
        delta, weight, (((1,), (1,)), ((), ())), preferred_element_type=f32
    ).astype(bf16)
    for b in range(N_BLK):
        back_ref[b] = back
    over_nodes = (((0,), (0,)), ((), ()))
    grad_ref[:, :HIDDEN] = (
        lax.dot_general(agg, delta, over_nodes, preferred_element_type=f32) * scale
    )
    ones = jnp.ones((NB, TILE), bf16)
    grad_ref[:, HIDDEN:] = (
        lax.dot_general(delta, ones, over_nodes, preferred_element_type=f32) * scale
    )


def dense_block(parts, weight, bias, cot, scale):
    return pl.pallas_call(
        functools.partial(dense_kernel, scale),
        out_shape=[
            jax.ShapeDtypeStruct((NB, HIDDEN), bf16),
            jax.ShapeDtypeStruct((N_BLK, NB, HIDDEN), bf16),
            jax.ShapeDtypeStruct((HIDDEN, HIDDEN + TILE), f32),
        ],
        in_specs=[VMEM] * 4,
        out_specs=[VMEM] * 3,
        compiler_params=pltpu.CompilerParams(vmem_limit_bytes=VMEM_BYTES),
        name="dense_block",
    )(parts, weight, bias, cot)


def gather_pieces(own):
    both = jnp.concatenate([own, swap("xh")(own)], axis=0)
    pieces = [both]
    right = left = both
    for _ in range(3):
        right = turn(right, 1)
        left = turn(left, -1)
        pieces += [right, left]
    pieces += [turn(right[:PER], 1), turn(left[PER:], -1)]
    ordered = []
    for piece in pieces[:-2]:
        ordered += [piece, swap("core")(piece)]
    last = pieces[-2:]
    ordered += last + [swap("core")(piece) for piece in last]
    return ordered


def place_of(cols, xh, z, core):
    owner = cols // PER
    away = ((owner // CORE) % Z - z) % Z
    near = jnp.where(away <= 3, 2 * away, 15 - 2 * away)
    return near, (owner % CORE) ^ core, (owner // (CORE * Z)) ^ xh, cols % PER


def scatter_sum(sends, keep):
    received = [swap("core")(part) for part in sends]
    size = XH * PER

    def mine(near):
        here = keep[near * size : (near + 1) * size].astype(f32)
        return here + received[near].astype(f32)

    far = mine(7).astype(bf16)
    right = turn(far[:PER], 1)
    left = turn(far[PER:], -1)
    onto_right, onto_left = mine(6), mine(5)
    right = jnp.concatenate([onto_right[:PER] + right.astype(f32), onto_right[PER:]], axis=0)
    left = jnp.concatenate([onto_left[:PER], onto_left[PER:] + left.astype(f32)], axis=0)
    right = turn(right.astype(bf16), 1)
    left = turn(left.astype(bf16), -1)
    for near in (4, 2):
        right = turn((mine(near) + right.astype(f32)).astype(bf16), 1)
        left = turn((mine(near - 1) + left.astype(f32)).astype(bf16), -1)
    here = mine(0) + right.astype(f32) + left.astype(f32)
    across = swap("xh")(here[PER:].astype(bf16))
    return (here[:PER] + across.astype(f32)).astype(bf16)


def shards(features, adj_tiles, tile_row, tile_col, weight, bias_vec, cotangent):
    adj = adj_tiles[0]
    rows = tile_row[0]
    cols = tile_col[0]
    xh, z, core = (lax.axis_index(axis) for axis in ("xh", "z", "core"))
    live = jnp.sum((cols < TC).astype(jnp.int32)).reshape(1)
    near, other, across, part = place_of(jnp.minimum(cols, TC - 1), xh, z, core)
    slab_pos = ((near * CORE + other) * XH + across) * PER + part
    sum_pos = ((other * Z + near) * XH + across) * PER + part

    pieces = gather_pieces(features.reshape(PER, TILE, HIDDEN))
    partial = forward_tiles(live, rows, slab_pos, adj, pieces)
    parts = lax.all_to_all(
        partial.reshape(N_BLK, NB, HIDDEN), BLK, split_axis=0, concat_axis=0, tiled=True
    )
    scale = 1.0 / math.sqrt(NB * XH * Z * CORE * N_BLK)
    activated, back, grads = dense_block(parts, weight, bias_vec.reshape(1, HIDDEN), cotangent, scale)
    err = lax.all_to_all(back, BLK, split_axis=0, concat_axis=0, tiled=True)

    grad_rows = lax.all_to_all(grads, AXES, split_axis=0, concat_axis=0, tiled=True)
    grad_row = jnp.sum(grad_rows, axis=0, keepdims=True)
    grads = lax.all_to_all(
        jnp.broadcast_to(grad_row, grads.shape), AXES, split_axis=0, concat_axis=0, tiled=True
    )

    half = TC // CORE
    step = half // Z
    outs = backward_tiles(
        live, rows, sum_pos, adj, err.reshape(TR, TILE, HIDDEN), [half] + [step] * Z
    )
    grad_x = scatter_sum(outs[1:], outs[0])
    return (activated, grad_x.reshape(NB, HIDDEN), grads[:, :HIDDEN], grads[:, HIDDEN])


def solution(mesh):
    cut = Mesh(mesh.devices.reshape(XH, Z, CORE, Y, XL), AXES)
    row = ("xh", "z", "core")
    return jax.shard_map(
        shards,
        mesh=cut,
        in_specs=(
            P(AXES, None),
            P(row, BLK, None, None),
            P(row, BLK),
            P(row, BLK),
            P(),
            P(),
            P(AXES, None),
        ),
        out_specs=(P(AXES, None), P(AXES, None), P(), P()),
        check_vma=False,
    )
```

time: 1040 us -> 245 us (0.24)
  waiting for transfers between devices: 657 us -> 94.5 us
  blocking collectives: 179 us -> 53.6 us
  other arithmetic: 93.6 us -> 14.4 us
  local copies, waits for them, and re-layouts: 63 us -> 5.3 us
  starting transfers between devices: 0.2 us -> 53.3 us
  matrix products: 26.1 us -> 0 us
  Pallas kernels: 0 us -> 23.3 us
  between operations: 14.5 us -> 1.07 us
    reduce_scatter x2 -> x0, waiting for transfers between devices: 272 us -> none  [the longest x1 181 us: shards(): lax.psum_scatter(partial_fwd.reshape(row_tiles * tile_size, hidden), 'blk...]
    psum x1 -> x0, waiting for transfers between devices: 254 us -> none  [shards(): lax.psum((jnp.einsum('nf,ng->fg', aggregated, delta_grad, preferred_eleme...]
    psum x1 -> x0, blocking collectives: 179 us -> none  [shards(): lax.psum((jnp.einsum('nf,ng->fg', aggregated, delta_grad, preferred_eleme...]
    all_gather x2 -> x0, waiting for transfers between devices: 130 us -> none  [the longest x1 96.7 us: shards(): col_slab = lax.all_gather(own_blocks, 'row', axis=0, tiled=True)]
    ppermute x0 -> x35, waiting for transfers between devices: none -> 84.1 us  [the longest x16 70.7 us: turn(): return lax.ppermute(v, 'z', [(i, (i + step) % Z) for i in range(Z)])]
    scatter-add x10 -> x0, other arithmetic: 82.6 us -> none  [the longest x5 41.5 us: gather_turn(): return running.at[target].add(contrib, mode='drop')]
    all_to_all x0 -> x2, blocking collectives: none -> 53.6 us  [the longest x1 29.5 us: shards(): lax.all_to_all(partial.reshape(N_BLK, NB, HIDDEN), BLK, split_axis=0, con...]
    gather x10 -> x0, local copies, waits for them, and re-layouts: 39.6 us -> none  [the longest x5 23.3 us: gather_turn(): picked = source[local_col]]
  transfers between devices with their start and end apart: 5 -> 37, of which waited for: 5 -> 16; matrix products, arithmetic and copies ran while one was open for 2% -> 6% of each run, Pallas kernels for 0% -> 0%
where the time goes in v1:
time: 245 us
  waiting for transfers between devices  94.5 us (39%)
  blocking collectives  53.6 us (22%)
  starting transfers between devices  53.3 us (22%)
  Pallas kernels  23.3 us (10%)
  other arithmetic  14.4 us (6%)
  local copies, waits for them, and re-layouts  5.3 us (2%)
    ppermute x16, waiting for transfers between devices, turn(): return lax.ppermute(v, 'z', [(i, (i + step) % Z) for i in range(Z)])  70.7 us
    all_to_all x1, blocking collectives, shards(): lax.all_to_all(partial.reshape(N_BLK, NB, HIDDEN), BLK, split_axis=0, con...  29.5 us
    ppermute x16, starting transfers between devices, turn(): return lax.ppermute(v, 'z', [(i, (i + step) % Z) for i in range(Z)])  29.4 us
    all_to_all x1, blocking collectives, shards(): err = lax.all_to_all(back, BLK, split_axis=0, concat_axis=0, tiled=True)  24.1 us
    ppermute x19, waiting for transfers between devices, swap(): return lambda v: lax.ppermute(v, axis, [(0, 1), (1, 0)])  13.4 us
    all_to_all x1, waiting for transfers between devices, shards(): lax.all_to_all(grads, AXES, split_axis=0, concat_axis=0, tiled=True)  10.4 us
    pallas_call x1, Pallas kernels, backward_tiles(): pl.pallas_call(backward_kernel, out_shape=[jax.ShapeDtypeStruct((size, TI...  9.99 us
    pallas_call x1, Pallas kernels, forward_tiles(): pl.pallas_call(forward_kernel, out_shape=jax.ShapeDtypeStruct((TR, TILE,...  9.89 us
  transfers between devices with their start and end apart: 37, of which 16 were waited for; matrix products, arithmetic and copies ran while one was open for 6% of the time, Pallas kernels for 0%

profile of v1, /device:TPU:2, one launch (start us, length us, event | category | flops | bytes accessed | tf_op | source)
XLA Modules:
  0.0 245.3 jit_solution(4264599498565820369)
XLA Ops:
  0.6 2.2 collective-permute-start
  2.8 6.2 %collective-permute-done = bf16[3,128,256]{2,1,0:T(8,128)(2,1)S(1)} collective-permute-done((bf16[3,128,256]{2,1,0:T(8,128)(2,1)}, bf16[3,128,256]{2,1,0:T(8,128)(2,1)S(1)}, u32[]{:S(2)}, u32[]{:S(2)}) %collective-permute-start) | collective-permute-done | bytes 196640 | tf_op jit(solution)/shard_map/ppermute | solution.py:33
  9.1 1.0 pad_maximum_fusion.refs_0_
  10.0 5.9 %collective-permute-start.4 = (bf16[6,128,256]{2,1,0:T(8,128)(2,1)S(1)}, bf16[6,128,256]{2,1,0:T(8,128)(2,1)S(1)}, u32[]{:S(2)}, u32[]{:S(2)}) collective-permute-start(bf16[6,128,256]{2,1,0:T(8,128)(2,1)S(1)} %pad_maximum_fusion.refs_0_), channel_id=1, source_target_pairs={{0,112},{16,0},{32,16},{48,32},{64,48},{80,64},{96,80},{112,96},{1... | collective-permute-start | bytes 1179656 | tf_op jit(solution)/shard_map/ppermute | solution.py:37
  16.0 7.5 %collective-permute-done.4.refs_4_ = bf16[6,128,256]{2,1,0:T(8,128)(2,1)S(1)} collective-permute-done((bf16[6,128,256]{2,1,0:T(8,128)(2,1)S(1)}, bf16[6,128,256]{2,1,0:T(8,128)(2,1)S(1)}, u32[]{:S(2)}, u32[]{:S(2)}) %collective-permute-start.4) | collective-permute-done | bytes 393248 | tf_op jit(solution)/shard_map/ppermute | solution.py:37
  23.5 3.7 %collective-permute-start.8 = (bf16[6,128,256]{2,1,0:T(8,128)(2,1)S(1)}, bf16[6,128,256]{2,1,0:T(8,128)(2,1)S(1)}, u32[]{:S(2)}, u32[]{:S(2)}) collective-permute-start(bf16[6,128,256]{2,1,0:T(8,128)(2,1)S(1)} %collective-permute-done.4.refs_4_), channel_id=1, source_target_pairs={{0,112},{16,0},{32,16},{48,32},{64,48},{80,64},{96,80},{112,96},{1... | collective-permute-start | bytes 1179656 | tf_op jit(solution)/shard_map/ppermute | solution.py:37
  27.2 6.6 %collective-permute-done.8.refs_8_ = bf16[6,128,256]{2,1,0:T(8,128)(2,1)S(1)} collective-permute-done((bf16[6,128,256]{2,1,0:T(8,128)(2,1)S(1)}, bf16[6,128,256]{2,1,0:T(8,128)(2,1)S(1)}, u32[]{:S(2)}, u32[]{:S(2)}) %collective-permute-start.8) | collective-permute-done | bytes 393248 | tf_op jit(solution)/shard_map/ppermute | solution.py:37
  33.8 3.7 %collective-permute-start.12 = (bf16[6,128,256]{2,1,0:T(8,128)(2,1)S(1)}, bf16[6,128,256]{2,1,0:T(8,128)(2,1)S(1)}, u32[]{:S(2)}, u32[]{:S(2)}) collective-permute-start(bf16[6,128,256]{2,1,0:T(8,128)(2,1)S(1)} %collective-permute-done.8.refs_8_), channel_id=1, source_target_pairs={{0,112},{16,0},{32,16},{48,32},{64,48},{80,64},{96,80},{112,96},{1... | collective-permute-start | bytes 1179656 | tf_op jit(solution)/shard_map/ppermute | solution.py:37
  37.6 0.5 collective-permute-start.5
  38.1 0.1 collective-permute-start.3
  38.2 4.9 %collective-permute-done.12.refs_12_ = bf16[6,128,256]{2,1,0:T(8,128)(2,1)S(1)} collective-permute-done((bf16[6,128,256]{2,1,0:T(8,128)(2,1)S(1)}, bf16[6,128,256]{2,1,0:T(8,128)(2,1)S(1)}, u32[]{:S(2)}, u32[]{:S(2)}) %collective-permute-start.12) | collective-permute-done | bytes 393248 | tf_op jit(solution)/shard_map/ppermute | solution.py:37
  43.1 1.3 reduce.2.row_ref
  44.4 0.7 compare_reduce_fusion
  45.1 1.3 remainder_reduce_fusion
  46.4 0.1 collective-permute-done.10.refs_10_
  46.5 0.5 collective-permute-start.7
  47.1 3.8 %collective-permute-start.15 = (bf16[3,128,256]{2,1,0:T(8,128)(2,1)S(1)}, bf16[3,128,256]{2,1,0:T(8,128)(2,1)S(1)}, u32[]{:S(2)}, u32[]{:S(2)}) collective-permute-start(bf16[3,128,256]{2,1,0:T(8,128)(2,1)S(1)} %slice.84), channel_id=1, source_target_pairs={{0,112},{16,0},{32,16},{48,32},{64,48},{80,64},{96,80},{112,96},{1... | collective-permute-start | bytes 589832 | tf_op jit(solution)/shard_map/ppermute | solution.py:37
  51.0 0.5 collective-permute-start.11
  51.4 0.6 multiply_add_fusion
  52.1 3.1 %collective-permute-done.15.refs_15_ = bf16[3,128,256]{2,1,0:T(8,128)(2,1)S(1)} collective-permute-done((bf16[3,128,256]{2,1,0:T(8,128)(2,1)S(1)}, bf16[3,128,256]{2,1,0:T(8,128)(2,1)S(1)}, u32[]{:S(2)}, u32[]{:S(2)}) %collective-permute-start.15) | collective-permute-done | bytes 196640 | tf_op jit(solution)/shard_map/ppermute | solution.py:37
  55.2 3.4 %collective-permute-done.14.refs_14_ = bf16[3,128,256]{2,1,0:T(8,128)(2,1)S(1)} collective-permute-done((bf16[3,128,256]{2,1,0:T(8,128)(2,1)S(1)}, bf16[3,128,256]{2,1,0:T(8,128)(2,1)S(1)}, u32[]{:S(2)}, u32[]{:S(2)}) %collective-permute-start.14) | collective-permute-done | bytes 196640 | tf_op jit(solution)/shard_map/ppermute | solution.py:37
  58.6 0.6 multiply_add_fusion.1.pos_ref
  59.3 0.8 collective-permute-done.16.refs_16_
  60.2 0.5 copy-done.18
  60.7 0.1 copy-done.14
  60.9 9.9 %forward_tiles.1 = bf16[24,128,256]{2,1,0:T(8,128)(2,1)} custom-call(s32[1]{0:T(128)} %bitcast.live_ref, s32[288]{0:T(512)} %reduce.2.row_ref, s32[288]{0:T(512)} %multiply_add_fusion.1.pos_ref, bf16[288,128,128]{2,1,0:T(8,128)(2,1)} %bitcast.11, bf16[6,128,256]{2,1,0:T(8,128)(2,1)} %copy-done.2, bf16[6,128,256]{2,1,0:T(8,128)(2,1)} %copy-done.10, ...), custom_call_target="tpu_custom_call" | custom-call | tf_op jit(solution)/shard_map/forward_tiles/pallas_call | solution.py:86
  70.8 29.5 %all_to_all.28.parts_ref = bf16[8,384,256]{2,1,0:T(8,128)(2,1)} all-to-all(bf16[8,384,256]{2,1,0:T(8,128)(2,1)} %bitcast.13), channel_id=1, replica_groups=mesh['xh'=2,'z'=8,'core'=2,'y'=4,'xl'=2] {'y','xl'}, dimensions={0} | all-to-all | bytes 3145728 | tf_op jit(solution)/shard_map/all_to_all | solution.py:257
  100.2 3.4 %dense_block.1 = (bf16[384,256]{1,0:T(8,128)(2,1)}, bf16[8,384,256]{2,1,0:T(8,128)(2,1)}, f32[256,384]{1,0:T(8,128)}) custom-call(bf16[8,384,256]{2,1,0:T(8,128)(2,1)} %all_to_all.28.parts_ref, bf16[256,256]{1,0:T(8,128)(2,1)} %weight_ref.1, f32[1,256]{1,0:T(1,128)} %bitcast.21, bf16[384,256]{1,0:T(8,128)(2,1)} %cot_ref.1), custom_call_target="tpu_custom_call" | custom-call | tf_op jit(solution)/shard_map/dense_block/pallas_call | solution.py:183
  103.7 24.1 %all_to_all.29 = bf16[8,384,256]{2,1,0:T(8,128)(2,1)} all-to-all(bf16[8,384,256]{2,1,0:T(8,128)(2,1)} %get-tuple-element.17), channel_id=1, replica_groups=mesh['xh'=2,'z'=8,'core'=2,'y'=4,'xl'=2] {'y','xl'}, dimensions={0} | all-to-all | bytes 3145728 | tf_op jit(solution)/shard_map/all_to_all | solution.py:262
  127.7 10.0 %backward_tiles.1 = (bf16[48,128,256]{2,1,0:T(8,128)(2,1)}, bf16[6,128,256]{2,1,0:T(8,128)(2,1)}, bf16[6,128,256]{2,1,0:T(8,128)(2,1)}, bf16[6,128,256]{2,1,0:T(...) custom-call(s32[1]{0:T(128)} %bitcast.live_ref, ...), custom_call_target="tpu_custom_call" | custom-call | tf_op jit(solution)/shard_map/backward_tiles/pallas_call | solution.py:134
  137.9 0.5 collective-permute-start.22
  138.3 1.4 collective-permute-done.21
  139.8 0.6 collective-permute-done.22
  140.3 1.3 convert_add_fusion.2
  141.8 0.2 collective-permute-start.20
  142.0 11.5 %collective-permute-done.23 = bf16[3,128,256]{2,1,0:T(8,128)(2,1)S(1)} collective-permute-done((bf16[3,128,256]{2,1,0:T(8,128)(2,1)S(1)}, bf16[3,128,256]{2,1,0:T(8,128)(2,1)S(1)}, u32[]{:S(2)}, u32[]{:S(2)}) %collective-permute-start.23) | collective-permute-done | bytes 196640 | tf_op jit(solution)/shard_map/ppermute | solution.py:37
  153.8 0.5 collective-permute-start.29
  154.3 11.2 %collective-permute-done.24 = bf16[6,128,256]{2,1,0:T(8,128)(2,1)S(1)} collective-permute-done((bf16[6,128,256]{2,1,0:T(8,128)(2,1)S(1)}, bf16[6,128,256]{2,1,0:T(8,128)(2,1)S(1)}, u32[]{:S(2)}, u32[]{:S(2)}) %collective-permute-start.24) | collective-permute-done | bytes 393248 | tf_op jit(solution)/shard_map/ppermute | solution.py:37
  165.5 0.2 add_convert_fusion.3
  165.9 3.1 %collective-permute-start.30 = (bf16[3,128,256]{2,1,0:T(8,128)(2,1)S(1)}, bf16[3,128,256]{2,1,0:T(8,128)(2,1)S(1)}, u32[]{:S(2)}, u32[]{:S(2)}) collective-permute-start(bf16[3,128,256]{2,1,0:T(8,128)(2,1)S(1)} %get-tuple-element.38), channel_id=1, source_target_pairs={{0,112},{16,0},{32,16},{48,32},{64,48},{80,64},{96,80},{112,96},{1... | collective-permute-start | bytes 589832 | tf_op jit(solution)/shard_map/ppermute | solution.py:37
  169.0 7.7 %collective-permute-done.25 = bf16[6,128,256]{2,1,0:T(8,128)(2,1)S(1)} collective-permute-done((bf16[6,128,256]{2,1,0:T(8,128)(2,1)S(1)}, bf16[6,128,256]{2,1,0:T(8,128)(2,1)S(1)}, u32[]{:S(2)}, u32[]{:S(2)}) %collective-permute-start.25) | collective-permute-done | bytes 393248 | tf_op jit(solution)/shard_map/ppermute | solution.py:37
  176.7 1.0 add_convert_fusion.2
  177.8 0.8 pad_maximum_fusion.2
  178.6 1.2 copy.11
  179.8 9.0 %all-to-all-start.2 = ((f32[256,1,384]{2,1,0:T(1,128)}), f32[256,1,384]{2,1,0:T(1,128)S(1)}, u32[]{:S(2)}, u32[]{:S(2)}) async-start(f32[256,1,384]{2,1,0:T(1,128)} %copy.11), calls=%async_computation.2 | async-start | bytes 786432 | tf_op jit(solution)/shard_map/all_to_all | solution.py:264
  188.8 0.2 collective-permute-start.27
  189.0 2.0 add_convert_fusion.1
  191.1 4.4 %collective-permute-start.32 = (bf16[6,128,256]{2,1,0:T(8,128)(2,1)}, bf16[6,128,256]{2,1,0:T(8,128)(2,1)}, u32[]{:S(2)}, u32[]{:S(2)}) collective-permute-start(bf16[6,128,256]{2,1,0:T(8,128)(2,1)} %add_convert_fusion.1), channel_id=1, source_target_pairs={{0,112},{16,0},{32,16},{48,32},{64,48},{80,64},{96,80},{112,96},{1... | collective-permute-start | bytes 1179656 | tf_op jit(solution)/shard_map/ppermute | solution.py:37
  195.5 10.4 %all-to-all-done.2 = f32[256,1,384]{2,1,0:T(1,128)S(1)} async-done(((f32[256,1,384]{2,1,0:T(1,128)}), f32[256,1,384]{2,1,0:T(1,128)S(1)}, u32[]{:S(2)}, u32[]{:S(2)}) %all-to-all-start.2) | async-done | bytes 393248 | tf_op jit(solution)/shard_map/all_to_all | solution.py:264
  205.9 0.3 reduce_sum.19
  206.2 0.9 broadcast_in_dim.2
  207.2 6.7 %all-to-all-start.3 = ((f32[256,1,384]{2,1,0:T(1,128)}), f32[256,1,384]{2,1,0:T(1,128)S(1)}, u32[]{:S(2)}, u32[]{:S(2)}) async-start(f32[256,1,384]{2,1,0:T(1,128)} %broadcast_in_dim.2), calls=%async_computation.3 | async-start | bytes 786432 | tf_op jit(solution)/shard_map/all_to_all | solution.py:266
  213.8 0.2 collective-permute-start.18
  214.1 1.6 collective-permute-start.26
  215.7 1.3 add_convert_fusion
  217.0 2.9 %collective-permute-start.33 = (bf16[6,128,256]{2,1,0:T(8,128)(2,1)S(1)}, bf16[6,128,256]{2,1,0:T(8,128)(2,1)S(1)}, u32[]{:S(2)}, u32[]{:S(2)}) collective-permute-start(bf16[6,128,256]{2,1,0:T(8,128)(2,1)S(1)} %add_convert_fusion), channel_id=1, source_target_pairs={{0,112},{16,0},{32,16},{48,32},{64,48},{80,64},{96,80},{112,96},{1... | collective-permute-start | bytes 1179656 | tf_op jit(solution)/shard_map/ppermute | solution.py:37
  219.9 14.6 %collective-permute-done.26 = bf16[6,128,256]{2,1,0:T(8,128)(2,1)S(1)} collective-permute-done((bf16[6,128,256]{2,1,0:T(8,128)(2,1)}, bf16[6,128,256]{2,1,0:T(8,128)(2,1)S(1)}, u32[]{:S(2)}, u32[]{:S(2)}) %collective-permute-start.26) | collective-permute-done | bytes 393248 | tf_op jit(solution)/shard_map/ppermute | solution.py:37
  234.5 0.2 convert_add_fusion
  234.7 0.9 copy-done.1
  235.6 2.2 collective-permute-start.34
  237.8 0.7 slice.93
  238.5 0.7 slice_reduce_fusion
  239.2 4.4 %collective-permute-done.34 = bf16[3,128,256]{2,1,0:T(8,128)(2,1)S(1)} collective-permute-done((bf16[3,128,256]{2,1,0:T(8,128)(2,1)S(1)}, bf16[3,128,256]{2,1,0:T(8,128)(2,1)S(1)}, u32[]{:S(2)}, u32[]{:S(2)}) %collective-permute-start.34) | collective-permute-done | bytes 196640 | tf_op jit(solution)/shard_map/ppermute | solution.py:33
  243.6 1.7 fusion
  (86 shorter events, 1.2 us)
Async XLA Ops:
  0.6 8.4 %collective-permute-start = (bf16[3,128,256]{2,1,0:T(8,128)(2,1)}, bf16[3,128,256]{2,1,0:T(8,128)(2,1)S(1)}, u32[]{:S(2)}, u32[]{:S(2)}) collective-permute-start(bf16[3,128,256]{2,1,0:T(8,128)(2,1)} %bitcast.18), channel_id=1, source_target_pairs={{0,128},{128,0},{1,129},{129,1},{2,130},{130,2},{3,131},{131,3},{4... | collective-permute-start | bytes 589832 | tf_op jit(solution)/shard_map/ppermute | solution.py:33
  10.0 50.0 %copy-start.2 = (bf16[6,128,256]{2,1,0:T(8,128)(2,1)}, bf16[6,128,256]{2,1,0:T(8,128)(2,1)S(1)}, u32[]{:S(2)}) copy-start(bf16[6,128,256]{2,1,0:T(8,128)(2,1)S(1)} %pad_maximum_fusion.refs_0_) | copy-start | bytes 1179652
  10.0 13.4 %collective-permute-start.4 = (bf16[6,128,256]{2,1,0:T(8,128)(2,1)S(1)}, bf16[6,128,256]{2,1,0:T(8,128)(2,1)S(1)}, u32[]{:S(2)}, u32[]{:S(2)}) collective-permute-start(bf16[6,128,256]{2,1,0:T(8,128)(2,1)S(1)} %pad_maximum_fusion.refs_0_), channel_id=1, source_target_pairs={{0,112},{16,0},{32,16},{48,32},{64,48},{80,64},{96,80},{112,96},{1... | collective-permute-start | bytes 1179656 | tf_op jit(solution)/shard_map/ppermute | solution.py:37
  16.0 11.2 %collective-permute-start.2 = (bf16[6,128,256]{2,1,0:T(8,128)(2,1)S(1)}, bf16[6,128,256]{2,1,0:T(8,128)(2,1)S(1)}, u32[]{:S(2)}, u32[]{:S(2)}) collective-permute-start(bf16[6,128,256]{2,1,0:T(8,128)(2,1)S(1)} %pad_maximum_fusion.refs_0_), channel_id=1, source_target_pairs={{0,16},{16,32},{32,48},{48,64},{64,80},{80,96},{96,112},{112,0},{1... | collective-permute-start | bytes 1179656 | tf_op jit(solution)/shard_map/ppermute | solution.py:37
  23.5 36.6 %copy-start.6 = (bf16[6,128,256]{2,1,0:T(8,128)(2,1)}, bf16[6,128,256]{2,1,0:T(8,128)(2,1)S(1)}, u32[]{:S(2)}) copy-start(bf16[6,128,256]{2,1,0:T(8,128)(2,1)S(1)} %collective-permute-done.4.refs_4_) | copy-start | bytes 1179652
  23.5 10.3 %collective-permute-start.8 = (bf16[6,128,256]{2,1,0:T(8,128)(2,1)S(1)}, bf16[6,128,256]{2,1,0:T(8,128)(2,1)S(1)}, u32[]{:S(2)}, u32[]{:S(2)}) collective-permute-start(bf16[6,128,256]{2,1,0:T(8,128)(2,1)S(1)} %collective-permute-done.4.refs_4_), channel_id=1, source_target_pairs={{0,112},{16,0},{32,16},{48,32},{64,48},{80,64},{96,80},{112,96},{1... | collective-permute-start | bytes 1179656 | tf_op jit(solution)/shard_map/ppermute | solution.py:37
  27.2 32.9 %copy-start.7 = (bf16[6,128,256]{2,1,0:T(8,128)(2,1)}, bf16[6,128,256]{2,1,0:T(8,128)(2,1)S(1)}, u32[]{:S(2)}) copy-start(bf16[6,128,256]{2,1,0:T(8,128)(2,1)S(1)} %collective-permute-done.2.refs_2_) | copy-start | bytes 1179652
  27.2 10.3 %collective-permute-start.6 = (bf16[6,128,256]{2,1,0:T(8,128)(2,1)S(1)}, bf16[6,128,256]{2,1,0:T(8,128)(2,1)S(1)}, u32[]{:S(2)}, u32[]{:S(2)}) collective-permute-start(bf16[6,128,256]{2,1,0:T(8,128)(2,1)S(1)} %collective-permute-done.2.refs_2_), channel_id=1, source_target_pairs={{0,16},{16,32},{32,48},{48,64},{64,80},{80,96},{96,112},{112,0},{1... | collective-permute-start | bytes 1179656 | tf_op jit(solution)/shard_map/ppermute | solution.py:37
  33.8 26.3 %copy-start.8 = (bf16[6,128,256]{2,1,0:T(8,128)(2,1)}, bf16[6,128,256]{2,1,0:T(8,128)(2,1)S(1)}, u32[]{:S(2)}) copy-start(bf16[6,128,256]{2,1,0:T(8,128)(2,1)S(1)} %collective-permute-done.8.refs_8_) | copy-start | bytes 1179652
  33.8 9.4 %collective-permute-start.12 = (bf16[6,128,256]{2,1,0:T(8,128)(2,1)S(1)}, bf16[6,128,256]{2,1,0:T(8,128)(2,1)S(1)}, u32[]{:S(2)}, u32[]{:S(2)}) collective-permute-start(bf16[6,128,256]{2,1,0:T(8,128)(2,1)S(1)} %collective-permute-done.8.refs_8_), channel_id=1, source_target_pairs={{0,112},{16,0},{32,16},{48,32},{64,48},{80,64},{96,80},{112,96},{1... | collective-permute-start | bytes 1179656 | tf_op jit(solution)/shard_map/ppermute | solution.py:37
  37.5 22.6 %copy-start.9 = (bf16[6,128,256]{2,1,0:T(8,128)(2,1)}, bf16[6,128,256]{2,1,0:T(8,128)(2,1)S(1)}, u32[]{:S(2)}) copy-start(bf16[6,128,256]{2,1,0:T(8,128)(2,1)S(1)} %collective-permute-done.6.refs_6_) | copy-start | bytes 1179652
  37.5 9.1 %collective-permute-start.10 = (bf16[6,128,256]{2,1,0:T(8,128)(2,1)S(1)}, bf16[6,128,256]{2,1,0:T(8,128)(2,1)S(1)}, u32[]{:S(2)}, u32[]{:S(2)}) collective-permute-start(bf16[6,128,256]{2,1,0:T(8,128)(2,1)S(1)} %collective-permute-done.6.refs_6_), channel_id=1, source_target_pairs={{0,16},{16,32},{32,48},{48,64},{64,80},{80,96},{96,112},{112,0},{1... | collective-permute-start | bytes 1179656 | tf_op jit(solution)/shard_map/ppermute | solution.py:37
  37.5 9.6 %collective-permute-start.1 = (bf16[6,128,256]{2,1,0:T(8,128)(2,1)S(1)}, bf16[6,128,256]{2,1,0:T(8,128)(2,1)S(1)}, u32[]{:S(2)}, u32[]{:S(2)}) collective-permute-start(bf16[6,128,256]{2,1,0:T(8,128)(2,1)S(1)} %pad_maximum_fusion.refs_0_), channel_id=1, source_target_pairs={{0,8},{8,0},{1,9},{9,1},{2,10},{10,2},{3,11},{11,3},{4,12},{12,4},... | collective-permute-start | bytes 1179656 | tf_op jit(solution)/shard_map/ppermute | solution.py:33
  37.6 13.3 %collective-permute-start.5 = (bf16[6,128,256]{2,1,0:T(8,128)(2,1)S(1)}, bf16[6,128,256]{2,1,0:T(8,128)(2,1)S(1)}, u32[]{:S(2)}, u32[]{:S(2)}) collective-permute-start(bf16[6,128,256]{2,1,0:T(8,128)(2,1)S(1)} %collective-permute-done.4.refs_4_), channel_id=1, source_target_pairs={{0,8},{8,0},{1,9},{9,1},{2,10},{10,2},{3,11},{11,3},{4,12},{12,4},... | collective-permute-start | bytes 1179656 | tf_op jit(solution)/shard_map/ppermute | solution.py:33
  38.1 12.8 %collective-permute-start.3 = (bf16[6,128,256]{2,1,0:T(8,128)(2,1)S(1)}, bf16[6,128,256]{2,1,0:T(8,128)(2,1)}, u32[]{:S(2)}, u32[]{:S(2)}) collective-permute-start(bf16[6,128,256]{2,1,0:T(8,128)(2,1)S(1)} %collective-permute-done.2.refs_2_), channel_id=1, source_target_pairs={{0,8},{8,0},{1,9},{9,1},{2,10},{10,2},{3,11},{11,3},{4,12},{12,4},... | collective-permute-start | bytes 1179656 | tf_op jit(solution)/shard_map/ppermute | solution.py:33
  43.1 17.0 %copy-start.3 = (bf16[6,128,256]{2,1,0:T(8,128)(2,1)}, bf16[6,128,256]{2,1,0:T(8,128)(2,1)S(1)}, u32[]{:S(2)}) copy-start(bf16[6,128,256]{2,1,0:T(8,128)(2,1)S(1)} %collective-permute-done.12.refs_12_) | copy-start | bytes 1179652
  43.1 7.8 %collective-permute-start.9 = (bf16[6,128,256]{2,1,0:T(8,128)(2,1)S(1)}, bf16[6,128,256]{2,1,0:T(8,128)(2,1)}, u32[]{:S(2)}, u32[]{:S(2)}) collective-permute-start(bf16[6,128,256]{2,1,0:T(8,128)(2,1)S(1)} %collective-permute-done.8.refs_8_), channel_id=1, source_target_pairs={{0,8},{8,0},{1,9},{9,1},{2,10},{10,2},{3,11},{11,3},{4,12},{12,4},... | collective-permute-start | bytes 1179656 | tf_op jit(solution)/shard_map/ppermute | solution.py:33
  46.5 13.6 %copy-start.4 = (bf16[6,128,256]{2,1,0:T(8,128)(2,1)}, bf16[6,128,256]{2,1,0:T(8,128)(2,1)S(1)}, u32[]{:S(2)}) copy-start(bf16[6,128,256]{2,1,0:T(8,128)(2,1)S(1)} %collective-permute-done.10.refs_10_) | copy-start | bytes 1179652
  46.5 12.7 %collective-permute-start.7 = (bf16[6,128,256]{2,1,0:T(8,128)(2,1)S(1)}, bf16[6,128,256]{2,1,0:T(8,128)(2,1)S(1)}, u32[]{:S(2)}, u32[]{:S(2)}) collective-permute-start(bf16[6,128,256]{2,1,0:T(8,128)(2,1)S(1)} %collective-permute-done.6.refs_6_), channel_id=1, source_target_pairs={{0,8},{8,0},{1,9},{9,1},{2,10},{10,2},{3,11},{11,3},{4,12},{12,4},... | collective-permute-start | bytes 1179656 | tf_op jit(solution)/shard_map/ppermute | solution.py:33
  47.0 13.1 %copy-start.10 = (bf16[6,128,256]{2,1,0:T(8,128)(2,1)}, bf16[6,128,256]{2,1,0:T(8,128)(2,1)S(1)}, u32[]{:S(2)}) copy-start(bf16[6,128,256]{2,1,0:T(8,128)(2,1)S(1)} %collective-permute-done.1.refs_1_) | copy-start | bytes 1179652
  47.1 8.1 %collective-permute-start.15 = (bf16[3,128,256]{2,1,0:T(8,128)(2,1)S(1)}, bf16[3,128,256]{2,1,0:T(8,128)(2,1)S(1)}, u32[]{:S(2)}, u32[]{:S(2)}) collective-permute-start(bf16[3,128,256]{2,1,0:T(8,128)(2,1)S(1)} %slice.84), channel_id=1, source_target_pairs={{0,112},{16,0},{32,16},{48,32},{64,48},{80,64},{96,80},{112,96},{1... | collective-permute-start | bytes 589832 | tf_op jit(solution)/shard_map/ppermute | solution.py:37
  50.8 9.3 %copy-start.11 = (bf16[6,128,256]{2,1,0:T(8,128)(2,1)}, bf16[6,128,256]{2,1,0:T(8,128)(2,1)S(1)}, u32[]{:S(2)}) copy-start(bf16[6,128,256]{2,1,0:T(8,128)(2,1)S(1)} %collective-permute-done.5.refs_5_) | copy-start | bytes 1179652
  50.8 7.8 %collective-permute-start.14 = (bf16[3,128,256]{2,1,0:T(8,128)(2,1)S(1)}, bf16[3,128,256]{2,1,0:T(8,128)(2,1)S(1)}, u32[]{:S(2)}, u32[]{:S(2)}) collective-permute-start(bf16[3,128,256]{2,1,0:T(8,128)(2,1)S(1)} %slice.83), channel_id=1, source_target_pairs={{0,16},{16,32},{32,48},{48,64},{64,80},{80,96},{96,112},{112,0},{1... | collective-permute-start | bytes 589832 | tf_op jit(solution)/shard_map/ppermute | solution.py:37
  50.8 8.4 %collective-permute-start.13 = (bf16[6,128,256]{2,1,0:T(8,128)(2,1)S(1)}, bf16[6,128,256]{2,1,0:T(8,128)(2,1)S(1)}, u32[]{:S(2)}, u32[]{:S(2)}) collective-permute-start(bf16[6,128,256]{2,1,0:T(8,128)(2,1)S(1)} %collective-permute-done.12.refs_12_), channel_id=1, source_target_pairs={{0,8},{8,0},{1,9},{9,1},{2,10},{10,2},{3,11},{11,3},{4,12},{12,4},... | collective-permute-start | bytes 1179656 | tf_op jit(solution)/shard_map/ppermute | solution.py:33
  51.0 9.1 %collective-permute-start.11 = (bf16[6,128,256]{2,1,0:T(8,128)(2,1)S(1)}, bf16[6,128,256]{2,1,0:T(8,128)(2,1)S(1)}, u32[]{:S(2)}, u32[]{:S(2)}) collective-permute-start(bf16[6,128,256]{2,1,0:T(8,128)(2,1)S(1)} %collective-permute-done.10.refs_10_), channel_id=1, source_target_pairs={{0,8},{8,0},{1,9},{9,1},{2,10},{10,2},{3,11},{11,3},{4,12},{12,4},... | collective-permute-start | bytes 1179656 | tf_op jit(solution)/shard_map/ppermute | solution.py:33
  55.2 5.0 %copy-start.15 = (bf16[3,128,256]{2,1,0:T(8,128)(2,1)}, bf16[3,128,256]{2,1,0:T(8,128)(2,1)S(1)}, u32[]{:S(2)}) copy-start(bf16[3,128,256]{2,1,0:T(8,128)(2,1)S(1)} %collective-permute-done.15.refs_15_) | copy-start | bytes 589828
  55.2 4.1 %collective-permute-start.17 = (bf16[3,128,256]{2,1,0:T(8,128)(2,1)S(1)}, bf16[3,128,256]{2,1,0:T(8,128)(2,1)S(1)}, u32[]{:S(2)}, u32[]{:S(2)}) collective-permute-start(bf16[3,128,256]{2,1,0:T(8,128)(2,1)S(1)} %collective-permute-done.15.refs_15_), channel_id=1, source_target_pairs={{0,8},{8,0},{1,9},{9,1},{2,10},{10,2},{3,11},{11,3},{4,12},{12,4},... | collective-permute-start | bytes 589832 | tf_op jit(solution)/shard_map/ppermute | solution.py:33
  58.6 1.6 copy-start.16
  58.6 1.4 collective-permute-start.16
  59.2 0.9 copy-start.12
  59.2 0.9 copy-start.17
  59.3 0.9 copy-start.13
  60.0 0.7 copy-start.18
  60.0 0.8 copy-start.14
  137.7 16.0 %copy-start.20 = (bf16[6,128,256]{2,1,0:T(8,128)(2,1)S(1)}, bf16[6,128,256]{2,1,0:T(8,128)(2,1)}, u32[]{:S(2)}) copy-start(bf16[6,128,256]{2,1,0:T(8,128)(2,1)} %get-tuple-element.20) | copy-start | bytes 1179652
  137.7 16.1 %copy-start.19 = (bf16[6,128,256]{2,1,0:T(8,128)(2,1)S(1)}, bf16[6,128,256]{2,1,0:T(8,128)(2,1)}, u32[]{:S(2)}) copy-start(bf16[6,128,256]{2,1,0:T(8,128)(2,1)} %get-tuple-element.26) | copy-start | bytes 1179652
  137.7 27.8 %copy-start = (bf16[48,128,256]{2,1,0:T(8,128)(2,1)S(1)}, bf16[48,128,256]{2,1,0:T(8,128)(2,1)}, u32[]{:S(2)}) copy-start(bf16[48,128,256]{2,1,0:T(8,128)(2,1)} %get-tuple-element.18) | copy-start | bytes 9437188
  137.8 2.0 collective-permute-start.21
  137.9 2.5 %collective-permute-start.22 = (bf16[6,128,256]{2,1,0:T(8,128)(2,1)}, bf16[6,128,256]{2,1,0:T(8,128)(2,1)S(1)}, u32[]{:S(2)}, u32[]{:S(2)}) collective-permute-start(bf16[6,128,256]{2,1,0:T(8,128)(2,1)} %get-tuple-element.23), channel_id=1, source_target_pairs={{0,8},{8,0},{1,9},{9,1},{2,10},{10,2},{3,11},{11,3},{4,12},{12,4},... | collective-permute-start | bytes 1179656 | tf_op jit(solution)/shard_map/ppermute | solution.py:33
  141.7 11.8 %collective-permute-start.23 = (bf16[3,128,256]{2,1,0:T(8,128)(2,1)S(1)}, bf16[3,128,256]{2,1,0:T(8,128)(2,1)S(1)}, u32[]{:S(2)}, u32[]{:S(2)}) collective-permute-start(bf16[3,128,256]{2,1,0:T(8,128)(2,1)S(1)} %get-tuple-element.37), channel_id=1, source_target_pairs={{0,16},{16,32},{32,48},{48,64},{64,80},{80,96},{96,112},{112,0},{1... | collective-permute-start | bytes 589832 | tf_op jit(solution)/shard_map/ppermute | solution.py:37
  141.8 12.5 %collective-permute-start.20 = (bf16[6,128,256]{2,1,0:T(8,128)(2,1)}, bf16[6,128,256]{2,1,0:T(8,128)(2,1)S(1)}, u32[]{:S(2)}, u32[]{:S(2)}) collective-permute-start(bf16[6,128,256]{2,1,0:T(8,128)(2,1)} %get-tuple-element.21), channel_id=1, source_target_pairs={{0,8},{8,0},{1,9},{9,1},{2,10},{10,2},{3,11},{11,3},{4,12},{12,4},... | collective-permute-start | bytes 1179656 | tf_op jit(solution)/shard_map/ppermute | solution.py:33
  153.6 11.9 %collective-permute-start.24 = (bf16[6,128,256]{2,1,0:T(8,128)(2,1)S(1)}, bf16[6,128,256]{2,1,0:T(8,128)(2,1)S(1)}, u32[]{:S(2)}, u32[]{:S(2)}) collective-permute-start(bf16[6,128,256]{2,1,0:T(8,128)(2,1)S(1)} %pad_maximum_fusion.1), channel_id=1, source_target_pairs={{0,16},{16,32},{32,48},{48,64},{64,80},{80,96},{96,112},{112,0},{1... | collective-permute-start | bytes 1179656 | tf_op jit(solution)/shard_map/ppermute | solution.py:37
  153.7 15.3 %collective-permute-start.19 = (bf16[6,128,256]{2,1,0:T(8,128)(2,1)S(1)}, bf16[6,128,256]{2,1,0:T(8,128)(2,1)S(1)}, u32[]{:S(2)}, u32[]{:S(2)}) collective-permute-start(bf16[6,128,256]{2,1,0:T(8,128)(2,1)S(1)} %copy-done.20), channel_id=1, source_target_pairs={{0,8},{8,0},{1,9},{9,1},{2,10},{10,2},{3,11},{11,3},{4,12},{12,4},... | collective-permute-start | bytes 1179656 | tf_op jit(solution)/shard_map/ppermute | solution.py:33
  153.8 24.8 %copy-start.5 = (f32[256,384]{1,0:T(8,128)S(1)}, f32[256,384]{1,0:T(8,128)}, u32[]{:S(2)}) copy-start(f32[256,384]{1,0:T(8,128)} %get-tuple-element.27) | copy-start | bytes 1179652
  153.8 15.2 %collective-permute-start.29 = (bf16[6,128,256]{2,1,0:T(8,128)(2,1)S(1)}, bf16[6,128,256]{2,1,0:T(8,128)(2,1)S(1)}, u32[]{:S(2)}, u32[]{:S(2)}) collective-permute-start(bf16[6,128,256]{2,1,0:T(8,128)(2,1)S(1)} %copy-done.19), channel_id=1, source_target_pairs={{0,8},{8,0},{1,9},{9,1},{2,10},{10,2},{3,11},{11,3},{4,12},{12,4},... | collective-permute-start | bytes 1179656 | tf_op jit(solution)/shard_map/ppermute | solution.py:33
  165.7 11.0 %collective-permute-start.25 = (bf16[6,128,256]{2,1,0:T(8,128)(2,1)S(1)}, bf16[6,128,256]{2,1,0:T(8,128)(2,1)S(1)}, u32[]{:S(2)}, u32[]{:S(2)}) collective-permute-start(bf16[6,128,256]{2,1,0:T(8,128)(2,1)S(1)} %add_convert_fusion.3), channel_id=1, source_target_pairs={{0,16},{16,32},{32,48},{48,64},{64,80},{80,96},{96,112},{112,0},{1... | collective-permute-start | bytes 1179656 | tf_op jit(solution)/shard_map/ppermute | solution.py:37
  165.8 23.3 %collective-permute-start.28 = (bf16[6,128,256]{2,1,0:T(8,128)(2,1)}, bf16[6,128,256]{2,1,0:T(8,128)(2,1)}, u32[]{:S(2)}, u32[]{:S(2)}) collective-permute-start(bf16[6,128,256]{2,1,0:T(8,128)(2,1)} %get-tuple-element.25), channel_id=1, source_target_pairs={{0,8},{8,0},{1,9},{9,1},{2,10},{10,2},{3,11},{11,3},{4,12},{12,4},... | collective-permute-start | bytes 1179656 | tf_op jit(solution)/shard_map/ppermute | solution.py:33
  165.9 11.9 %collective-permute-start.30 = (bf16[3,128,256]{2,1,0:T(8,128)(2,1)S(1)}, bf16[3,128,256]{2,1,0:T(8,128)(2,1)S(1)}, u32[]{:S(2)}, u32[]{:S(2)}) collective-permute-start(bf16[3,128,256]{2,1,0:T(8,128)(2,1)S(1)} %get-tuple-element.38), channel_id=1, source_target_pairs={{0,112},{16,0},{32,16},{48,32},{64,48},{80,64},{96,80},{112,96},{1... | collective-permute-start | bytes 589832 | tf_op jit(solution)/shard_map/ppermute | solution.py:37
  178.6 10.5 %collective-permute-start.31 = (bf16[6,128,256]{2,1,0:T(8,128)(2,1)}, bf16[6,128,256]{2,1,0:T(8,128)(2,1)}, u32[]{:S(2)}, u32[]{:S(2)}) collective-permute-start(bf16[6,128,256]{2,1,0:T(8,128)(2,1)} %pad_maximum_fusion.2), channel_id=1, source_target_pairs={{0,112},{16,0},{32,16},{48,32},{64,48},{80,64},{96,80},{112,96},{1... | collective-permute-start | bytes 1179656 | tf_op jit(solution)/shard_map/ppermute | solution.py:37
  179.8 26.1 %all-to-all-start.2 = ((f32[256,1,384]{2,1,0:T(1,128)}), f32[256,1,384]{2,1,0:T(1,128)S(1)}, u32[]{:S(2)}, u32[]{:S(2)}) async-start(f32[256,1,384]{2,1,0:T(1,128)} %copy.11), calls=%async_computation.2 | async-start | bytes 786432 | tf_op jit(solution)/shard_map/all_to_all | solution.py:264
  188.8 26.9 %collective-permute-start.27 = (bf16[6,128,256]{2,1,0:T(8,128)(2,1)}, bf16[6,128,256]{2,1,0:T(8,128)(2,1)}, u32[]{:S(2)}, u32[]{:S(2)}) collective-permute-start(bf16[6,128,256]{2,1,0:T(8,128)(2,1)} %get-tuple-element.24), channel_id=1, source_target_pairs={{0,8},{8,0},{1,9},{9,1},{2,10},{10,2},{3,11},{11,3},{4,12},{12,4},... | collective-permute-start | bytes 1179656 | tf_op jit(solution)/shard_map/ppermute | solution.py:33
  191.1 24.6 %collective-permute-start.32 = (bf16[6,128,256]{2,1,0:T(8,128)(2,1)}, bf16[6,128,256]{2,1,0:T(8,128)(2,1)}, u32[]{:S(2)}, u32[]{:S(2)}) collective-permute-start(bf16[6,128,256]{2,1,0:T(8,128)(2,1)} %add_convert_fusion.1), channel_id=1, source_target_pairs={{0,112},{16,0},{32,16},{48,32},{64,48},{80,64},{96,80},{112,96},{1... | collective-permute-start | bytes 1179656 | tf_op jit(solution)/shard_map/ppermute | solution.py:37
  207.2 30.6 %all-to-all-start.3 = ((f32[256,1,384]{2,1,0:T(1,128)}), f32[256,1,384]{2,1,0:T(1,128)S(1)}, u32[]{:S(2)}, u32[]{:S(2)}) async-start(f32[256,1,384]{2,1,0:T(1,128)} %broadcast_in_dim.2), calls=%async_computation.3 | async-start | bytes 786432 | tf_op jit(solution)/shard_map/all_to_all | solution.py:266
  213.8 6.0 %collective-permute-start.18 = (bf16[6,128,256]{2,1,0:T(8,128)(2,1)}, bf16[6,128,256]{2,1,0:T(8,128)(2,1)S(1)}, u32[]{:S(2)}, u32[]{:S(2)}) collective-permute-start(bf16[6,128,256]{2,1,0:T(8,128)(2,1)} %get-tuple-element.19), channel_id=1, source_target_pairs={{0,8},{8,0},{1,9},{9,1},{2,10},{10,2},{3,11},{11,3},{4,12},{12,4},... | collective-permute-start | bytes 1179656 | tf_op jit(solution)/shard_map/ppermute | solution.py:33
  214.1 20.4 %collective-permute-start.26 = (bf16[6,128,256]{2,1,0:T(8,128)(2,1)}, bf16[6,128,256]{2,1,0:T(8,128)(2,1)S(1)}, u32[]{:S(2)}, u32[]{:S(2)}) collective-permute-start(bf16[6,128,256]{2,1,0:T(8,128)(2,1)} %get-tuple-element.33), channel_id=1, source_target_pairs={{0,16},{16,32},{32,48},{48,64},{64,80},{80,96},{96,112},{112,0},{1... | collective-permute-start | bytes 1179656 | tf_op jit(solution)/shard_map/ppermute | solution.py:37
  217.0 17.5 %collective-permute-start.33 = (bf16[6,128,256]{2,1,0:T(8,128)(2,1)S(1)}, bf16[6,128,256]{2,1,0:T(8,128)(2,1)S(1)}, u32[]{:S(2)}, u32[]{:S(2)}) collective-permute-start(bf16[6,128,256]{2,1,0:T(8,128)(2,1)S(1)} %add_convert_fusion), channel_id=1, source_target_pairs={{0,112},{16,0},{32,16},{48,32},{64,48},{80,64},{96,80},{112,96},{1... | collective-permute-start | bytes 1179656 | tf_op jit(solution)/shard_map/ppermute | solution.py:37
  234.7 0.9 copy-start.1
  235.6 8.0 %collective-permute-start.34 = (bf16[3,128,256]{2,1,0:T(8,128)(2,1)S(1)}, bf16[3,128,256]{2,1,0:T(8,128)(2,1)S(1)}, u32[]{:S(2)}, u32[]{:S(2)}) collective-permute-start(bf16[3,128,256]{2,1,0:T(8,128)(2,1)S(1)} %slice.116), channel_id=1, source_target_pairs={{0,128},{128,0},{1,129},{129,1},{2,130},{130,2},{3,131},{131,3},{4... | collective-permute-start | bytes 589832 | tf_op jit(solution)/shard_map/ppermute | solution.py:33

commit v2 on v1

v2 whole, which is shorter than its diff:
```python
import functools
import math

import jax
import jax.numpy as jnp
from jax import lax
from jax.experimental import pallas as pl
from jax.experimental.pallas import tpu as pltpu
from jax.sharding import Mesh, PartitionSpec as P

XH, Z, CORE, Y, XL = 2, 8, 2, 4, 2
AXES = ("xh", "z", "core", "y", "xl")
BLK = ("y", "xl")
N_BLK = Y * XL
TILE = 128
HIDDEN = 256
PER = 3
NB = PER * TILE
TR = N_BLK * PER
TC = XH * Z * CORE * PER
K = 288
SPAN = CORE * PER
SPANS = XH * Z
NEAR_TILES = CORE * XH * PER
GROUP = 8
EXTRA = 48
GRAD_ROWS = HIDDEN // N_BLK
AWAY = (0, -1, 1, -2, 2, -3, 3, 4)
VMEM_BYTES = 56 * 2**20
bf16 = jnp.bfloat16
f32 = jnp.float32

ANY = pl.BlockSpec(memory_space=pl.ANY)
HBM = pl.BlockSpec(memory_space=pltpu.HBM)
VMEM = pl.BlockSpec(memory_space=pltpu.VMEM)
SMEM = pl.BlockSpec(memory_space=pltpu.SMEM)


def swap(axis):
    return lambda v: lax.ppermute(v, axis, [(0, 1), (1, 0)])


def turn(v, step):
    return lax.ppermute(v, "z", [(i, (i + step) % Z) for i in range(Z)])


def max_groups(nears):
    return min(K // GROUP + XH * len(nears), XH * len(nears) * SPAN * TR // GROUP)


def plan_groups(starts_ref, z_ref, nears, adj_hbm, adj, sem, base_ref, first_ref, end_ref):
    count = jnp.int32(0)
    for near in nears:
        there = lax.rem(z_ref[0] + AWAY[near] + Z, Z)
        for xh in range(XH):
            low = starts_ref[xh * Z + there]
            high = starts_ref[xh * Z + there + 1]
            size = (high - low + GROUP - 1) // GROUP

            def begin(g, carry, low=low, high=high, count=count):
                first = low + g * GROUP
                base = jnp.minimum(first, K - GROUP)
                base_ref[count + g] = base
                first_ref[count + g] = first
                end_ref[count + g] = high
                pltpu.make_async_copy(
                    adj_hbm.at[pl.ds(base, GROUP)], adj.at[count + g], sem.at[count + g]
                ).start()
                return carry

            lax.fori_loop(0, size, begin, 0)
            count = count + size
    base_ref[count] = 0
    first_ref[count] = 0
    end_ref[count] = 0
    return count


def for_pairs(count, adj_hbm, adj, sem, base_ref, first_ref, end_ref, work):
    def wait(g):
        pltpu.make_async_copy(adj_hbm.at[pl.ds(0, GROUP)], adj.at[g], sem.at[g]).wait()

    def step(i, carry):
        wait(2 * i)

        @pl.when(2 * i + 1 < count)
        def _():
            wait(2 * i + 1)

        for g in (2 * i, 2 * i + 1):
            for u in range(GROUP):
                k = base_ref[g] + u
                work(g, u, k, (k >= first_ref[g]) & (k < end_ref[g]))
        return carry

    lax.fori_loop(0, (count + 1) // 2, step, 0)


def group_scratch(nears):
    groups = max_groups(nears) + 1
    return [
        pltpu.VMEM((groups, GROUP, TILE, TILE), bf16),
        pltpu.SemaphoreType.DMA((groups,)),
        pltpu.SMEM((groups,), jnp.int32),
        pltpu.SMEM((groups,), jnp.int32),
        pltpu.SMEM((groups,), jnp.int32),
    ]


def forward_kernel(
    nears, total, final, starts_ref, z_ref, row_ref, pos_ref, adj_hbm, before_hbm, *refs
):
    pieces = refs[:total]
    refs = refs[total:]
    if final:
        out_ref, slab, piece_sem, adj, adj_sem, base_ref, first_ref, end_ref, acc = refs
    else:
        acc, zero_ref, slab, piece_sem, adj, adj_sem, base_ref, first_ref, end_ref = refs
        zero_ref[0] = 0
    copies = []
    at = 0
    for n, piece in enumerate(pieces):
        size = piece.shape[0]
        copies.append(pltpu.make_async_copy(piece, slab.at[pl.ds(at, size)], piece_sem.at[n]))
        at += size
    if nears[0] > 0:
        copies.append(pltpu.make_async_copy(before_hbm, acc, piece_sem.at[total]))
    for copy in copies:
        copy.start()
    count = plan_groups(
        starts_ref, z_ref, nears, adj_hbm, adj, adj_sem, base_ref, first_ref, end_ref
    )
    if nears[0] == 0:
        acc[...] = jnp.zeros_like(acc)
    for copy in copies:
        copy.wait()

    def work(g, u, k, live):
        row = jnp.where(live, row_ref[k], TR)
        pos = jnp.where(live, pos_ref[k] - nears[0] * NEAR_TILES, 0)
        acc[row] += jnp.dot(adj[g, u], slab[pos], preferred_element_type=f32)

    for_pairs(count, adj_hbm, adj, adj_sem, base_ref, first_ref, end_ref, work)
    if final:
        out_ref[...] = acc[:TR].astype(bf16)


def tile_cost(nears):
    tiles = K * len(nears) // Z
    return pl.CostEstimate(
        flops=tiles * 2 * TILE * TILE * HIDDEN, bytes_accessed=tiles * 6 * TILE * TILE, transcendentals=0
    )


def forward_tiles(scalars, adj, before, pieces, nears, final):
    acc_shape = (TR + 1, TILE, HIDDEN)
    if before is None:
        before = scalars[0]
    if final:
        out_shape, out_specs = jax.ShapeDtypeStruct((TR, TILE, HIDDEN), bf16), VMEM
    else:
        out_shape = [jax.ShapeDtypeStruct(acc_shape, f32), jax.ShapeDtypeStruct((1,), jnp.int32)]
        out_specs = [VMEM, SMEM]
    return pl.pallas_call(
        functools.partial(forward_kernel, nears, len(pieces), final),
        out_shape=out_shape,
        grid_spec=pltpu.PrefetchScalarGridSpec(
            num_scalar_prefetch=4,
            grid=(),
            in_specs=[HBM] + [ANY] * (1 + len(pieces)),
            out_specs=out_specs,
            scratch_shapes=[
                pltpu.VMEM((len(nears) * NEAR_TILES, TILE, HIDDEN), bf16),
                pltpu.SemaphoreType.DMA((len(pieces) + 1,)),
            ]
            + group_scratch(nears)
            + ([pltpu.VMEM(acc_shape, f32)] if final else []),
        ),
        compiler_params=pltpu.CompilerParams(
            vmem_limit_bytes=VMEM_BYTES
        ),
        cost_estimate=tile_cost(nears),
        name="forward_tiles",
    )(*scalars, adj, before, *pieces)


def backward_kernel(nears, ignored, starts_ref, z_ref, row_ref, pos_ref, adj_hbm, err_hbm, *refs):
    refs = refs[ignored:]
    outs = refs[: 2 * len(nears)]
    err, err_sem, adj, adj_sem, base_ref, first_ref, end_ref, acc = refs[2 * len(nears) :]
    copies = [
        pltpu.make_async_copy(
            err_hbm.at[i // PER, pl.ds(i % PER * TILE, TILE)], err.at[i], err_sem.at[i]
        )
        for i in range(TR)
    ]
    for copy in copies:
        copy.start()
    count = plan_groups(
        starts_ref, z_ref, nears, adj_hbm, adj, adj_sem, base_ref, first_ref, end_ref
    )
    acc[...] = jnp.zeros_like(acc)
    for copy in copies:
        copy.wait()

    def work(g, u, k, live):
        pos = jnp.where(live, pos_ref[k] - nears[0] * NEAR_TILES, len(nears) * NEAR_TILES)
        acc[pos] += lax.dot_general(
            adj[g, u], err[row_ref[k]], (((0,), (0,)), ((), ())), preferred_element_type=f32
        )

    for_pairs(count, adj_hbm, adj, adj_sem, base_ref, first_ref, end_ref, work)
    for i, out in enumerate(outs):
        out[...] = acc[i * XH * PER : (i + 1) * XH * PER].astype(bf16)


def backward_tiles(scalars, adj, err, nears, after):
    return pl.pallas_call(
        functools.partial(backward_kernel, nears, len(after)),
        out_shape=[jax.ShapeDtypeStruct((XH * PER, TILE, HIDDEN), bf16)] * (2 * len(nears)),
        grid_spec=pltpu.PrefetchScalarGridSpec(
            num_scalar_prefetch=4,
            grid=(),
            in_specs=[HBM] + [ANY] * (1 + len(after)),
            out_specs=[VMEM] * (2 * len(nears)),
            scratch_shapes=[
                pltpu.VMEM((TR, TILE, HIDDEN), bf16),
                pltpu.SemaphoreType.DMA((TR,)),
            ]
            + group_scratch(nears)
            + [pltpu.VMEM((len(nears) * NEAR_TILES + 1, TILE, HIDDEN), f32)],
        ),
        compiler_params=pltpu.CompilerParams(
            vmem_limit_bytes=VMEM_BYTES
        ),
        cost_estimate=tile_cost(nears),
        name="backward_tiles",
    )(*scalars, adj, err, *after)


def dense_kernel(scale, parts_ref, weight_ref, bias_ref, cot_ref, act_ref, back_ref):
    summed = parts_ref[0].astype(f32)
    for b in range(1, N_BLK):
        summed = summed + parts_ref[b].astype(f32)
    agg = summed.astype(bf16)
    weight = weight_ref[...]
    v = jnp.dot(agg, weight, preferred_element_type=f32) + bias_ref[...]
    c = math.sqrt(2.0 / math.pi)
    t = jnp.tanh(c * (v + 0.044715 * (v * v * v)))
    act_ref[...] = (0.5 * v * (1.0 + t)).astype(bf16)
    slope = 0.5 * (1.0 + t) + 0.5 * v * (1.0 - t * t) * (c * (1.0 + 3.0 * 0.044715 * (v * v)))
    delta = (cot_ref[...].astype(f32) * slope).astype(bf16)
    back = lax.dot_general(
        delta, weight, (((1,), (1,)), ((), ())), preferred_element_type=f32
    ).astype(bf16)
    over_nodes = (((0,), (0,)), ((), ()))
    grad_w = lax.dot_general(agg, delta, over_nodes, preferred_element_type=f32) * scale
    grad_b = jnp.sum(delta.astype(f32), axis=0, keepdims=True) * scale
    grad_b = jnp.broadcast_to(grad_b, (EXTRA - GRAD_ROWS, HIDDEN)).astype(bf16)
    for b in range(N_BLK):
        back_ref[b, :NB] = back
        back_ref[b, NB : NB + GRAD_ROWS] = grad_w[b * GRAD_ROWS : (b + 1) * GRAD_ROWS].astype(bf16)
        back_ref[b, NB + GRAD_ROWS :] = grad_b


def dense_block(parts, weight, bias, cot, scale):
    return pl.pallas_call(
        functools.partial(dense_kernel, scale),
        out_shape=[
            jax.ShapeDtypeStruct((NB, HIDDEN), bf16),
            jax.ShapeDtypeStruct((N_BLK, NB + EXTRA, HIDDEN), bf16),
        ],
        in_specs=[VMEM] * 4,
        out_specs=[VMEM] * 2,
        compiler_params=pltpu.CompilerParams(vmem_limit_bytes=VMEM_BYTES),
        name="dense_block",
    )(parts, weight, bias, cot)


def by_z_kernel(z_ref, *refs):
    total_ref, rows = refs[Z:]
    for away in range(Z):
        rows[away] = refs[away][...]
    total = jnp.zeros((EXTRA, HIDDEN), f32)
    for there in range(Z):
        total += rows[lax.rem(there - z_ref[0] + Z, Z)].astype(f32)
    total_ref[...] = total


def sum_by_z(z, parts):
    return pl.pallas_call(
        by_z_kernel,
        out_shape=jax.ShapeDtypeStruct((EXTRA, HIDDEN), f32),
        grid_spec=pltpu.PrefetchScalarGridSpec(
            num_scalar_prefetch=1,
            grid=(),
            in_specs=[VMEM] * Z,
            out_specs=VMEM,
            scratch_shapes=[pltpu.VMEM((Z, EXTRA, HIDDEN), bf16)],
        ),
        compiler_params=pltpu.CompilerParams(vmem_limit_bytes=4 * 2**20),
        name="sum_by_z",
    )(z, *parts)


def gather_forward(scalars, adj, own):
    def pair(piece):
        return [piece, swap("core")(piece)]

    both = jnp.concatenate([own, swap("xh")(own)], axis=0)
    right1, left1 = turn(both, 1), turn(both, -1)
    right2, left2 = turn(right1, 1), turn(left1, -1)
    near = pair(both) + pair(right1) + pair(left1)
    partial, zero = forward_tiles(scalars, adj, None, near, (0, 1, 2), False)
    right3, left3 = turn(right2, 1), turn(left2, -1)
    last = [
        turn(lax.dynamic_slice_in_dim(right3, zero[0], PER), 1),
        turn(lax.dynamic_slice_in_dim(left3, zero[0] + PER, PER), -1),
    ]
    middle = pair(right2) + pair(left2) + pair(right3) + pair(left3)
    partial, _ = forward_tiles(scalars, adj, partial, middle, (3, 4, 5, 6), False)
    last += [swap("core")(piece) for piece in last]
    return forward_tiles(scalars, adj, partial, last, (7,), True)


def place_of(cols, xh, z, core):
    owner = cols // PER
    away = ((owner // CORE) % Z - z) % Z
    near = jnp.where(away <= 3, 2 * away, 15 - 2 * away)
    return ((near * CORE + (owner % CORE ^ core)) * XH + (owner // (CORE * Z) ^ xh)) * PER + cols % PER


def backward_scatter(scalars, adj, err, grads):
    rows = XH * NB
    sums = [None] * Z

    def tiles(nears, after):
        outs = backward_tiles(scalars, adj, err, nears, after)
        for i, near in enumerate(nears):
            keep, send = outs[2 * i], swap("core")(outs[2 * i + 1])
            sums[near] = (keep.astype(f32) + send.astype(f32)).reshape(rows, HIDDEN)

    tiles((5, 6, 7), [])
    far = sums[7].astype(bf16)
    right = jnp.concatenate([far[:NB], grads], axis=0)
    left = jnp.concatenate([far[NB:], grads], axis=0)
    from_left, from_right = [], []
    for step in range(4):
        if step == 0:
            tiles((3, 4), [right, left])
        if step == 1:
            tiles((0, 1, 2), [right, left])
        right, left = turn(right, 1), turn(left, -1)
        size = rows if step > 0 else NB
        from_left.append(right[size:])
        if step < 3:
            from_right.append(left[size:])
        right, left = right[:size].astype(f32), left[:size].astype(f32)
        if step == 0:
            right = jnp.concatenate([sums[6][:NB] + right, sums[6][NB:]], axis=0)
            left = jnp.concatenate([sums[5][:NB], sums[5][NB:] + left], axis=0)
        else:
            right = right + sums[6 - 2 * step]
            left = left + sums[5 - 2 * step] if step < 3 else left
        if step < 3:
            right = jnp.concatenate([right.astype(bf16), from_left[-1]], axis=0)
        if step < 2:
            left = jnp.concatenate([left.astype(bf16), from_right[-1]], axis=0)
        if step == 2:
            left = left.astype(bf16)
    here = right + left
    across = swap("xh")(here[NB:].astype(bf16))
    grad_x = (here[:NB] + across.astype(f32)).astype(bf16)
    return grad_x, [grads] + from_right + from_left[::-1]


def both_sides(rows, axis):
    rows = rows.astype(bf16)
    return rows.astype(f32) + swap(axis)(rows).astype(f32)


def shards(features, adj_tiles, tile_row, tile_col, weight, bias_vec, cotangent):
    adj = adj_tiles[0]
    rows = tile_row[0]
    cols = tile_col[0]
    xh, z, core = (lax.axis_index(axis) for axis in ("xh", "z", "core"))
    edges = jnp.arange(SPANS + 1, dtype=jnp.int32) * SPAN
    starts = jnp.sum((cols[None, :] < edges[:, None]).astype(jnp.int32), axis=1)
    pos = place_of(jnp.minimum(cols, TC - 1), xh, z, core)
    scalars = (starts, z.reshape(1).astype(jnp.int32), rows, pos)

    partial = gather_forward(scalars, adj, features.reshape(PER, TILE, HIDDEN))
    parts = lax.all_to_all(
        partial.reshape(N_BLK, NB, HIDDEN), BLK, split_axis=0, concat_axis=0, tiled=True
    )
    scale = 1.0 / math.sqrt(NB * XH * Z * CORE * N_BLK)
    activated, back = dense_block(parts, weight, bias_vec.reshape(1, HIDDEN), cotangent, scale)
    back = lax.all_to_all(back, BLK, split_axis=0, concat_axis=0, tiled=True)

    grads = jnp.sum(back[:, NB:].astype(f32), axis=0)
    grads = both_sides(both_sides(grads, "core"), "xh").astype(bf16)
    grad_x, by_z = backward_scatter(scalars, adj, back, grads)
    grads = sum_by_z(scalars[1], by_z)
    grad_w = lax.all_to_all(
        jnp.tile(grads[:GRAD_ROWS], (N_BLK, 1)), BLK, split_axis=0, concat_axis=0, tiled=True
    )
    return (activated, grad_x, grad_w, grads[GRAD_ROWS])


def solution(mesh):
    cut = Mesh(mesh.devices.reshape(XH, Z, CORE, Y, XL), AXES)
    row = ("xh", "z", "core")
    return jax.shard_map(
        shards,
        mesh=cut,
        in_specs=(
            P(AXES, None),
            P(row, BLK, None, None),
            P(row, BLK),
            P(row, BLK),
            P(),
            P(),
            P(AXES, None),
        ),
        out_specs=(P(AXES, None), P(AXES, None), P(), P()),
        check_vma=False,
    )
```

time: 245 us -> 219 us (0.89); the launches traced: 245 us -> 217 us
  waiting for transfers between devices: 94.5 us -> 55 us
  Pallas kernels: 23.3 us -> 40.5 us
  starting transfers between devices: 53.3 us -> 45.1 us
  other arithmetic: 14.4 us -> 7.6 us
  between operations: 1.07 us -> 4.53 us
  blocking collectives: 53.6 us -> 56.7 us
    ppermute x16, waiting for transfers between devices: 70.7 us -> 38 us  [turn(): return lax.ppermute(v, 'z', [(i, (i + step) % Z) for i in range(Z)])]
    pallas_call x2 -> x7, Pallas kernels: 19.9 us -> 37 us  [the longest x3 19.2 us: forward_tiles(): pl.pallas_call(functools.partial(forward_kernel, nears, len(pieces), fina...]
    all_to_all x2 -> x1, starting transfers between devices: 15.7 us -> 6.26 us  [shards(): lax.all_to_all(jnp.tile(grads[:GRAD_ROWS], (N_BLK, 1)), BLK, split_axis=0...]
    all_to_all x2 -> x1, waiting for transfers between devices: 10.4 us -> 5.4 us  [shards(): lax.all_to_all(jnp.tile(grads[:GRAD_ROWS], (N_BLK, 1)), BLK, split_axis=0...]
    convert_element_type x5 -> x8, other arithmetic: 6.14 us -> 1.25 us  [the longest x1 0.72 us: backward_scatter(): grad_x = (here[:NB] + across.astype(f32)).astype(bf16)]
    unnamed x43 -> x59, local copies, waits for them, and re-layouts: 1.67 us -> 5.73 us
    ppermute x19 -> x21, starting transfers between devices: 8.11 us -> 11.9 us  [swap(): return lambda v: lax.ppermute(v, axis, [(0, 1), (1, 0)])]
    ppermute x16, starting transfers between devices: 29.4 us -> 26.9 us  [turn(): return lax.ppermute(v, 'z', [(i, (i + step) % Z) for i in range(Z)])]
  transfers between devices with their start and end apart: 37 -> 38, of which waited for: 16 -> 11; matrix products, arithmetic and copies ran while one was open for 6% -> 4% of each run, Pallas kernels for 0% -> 15%
where the time goes in v2:
time: 219 us; the launch traced here: 217 us
  blocking collectives  56.7 us (26%)
  waiting for transfers between devices  55 us (25%)
  starting transfers between devices  45.1 us (21%)
  Pallas kernels  40.5 us (18%)
  other arithmetic  7.6 us (3%)
  local copies, waits for them, and re-layouts  7.2 us (3%)
  between operations  4.53 us (2%)
    ppermute x16, waiting for transfers between devices, turn(): return lax.ppermute(v, 'z', [(i, (i + step) % Z) for i in range(Z)])  38 us
    all_to_all x1, blocking collectives, shards(): lax.all_to_all(partial.reshape(N_BLK, NB, HIDDEN), BLK, split_axis=0, con...  30.3 us
    ppermute x16, starting transfers between devices, turn(): return lax.ppermute(v, 'z', [(i, (i + step) % Z) for i in range(Z)])  26.9 us
    all_to_all x1, blocking collectives, shards(): back = lax.all_to_all(back, BLK, split_axis=0, concat_axis=0, tiled=True)  26.4 us
    pallas_call x3, Pallas kernels, forward_tiles(): pl.pallas_call(functools.partial(forward_kernel, nears, len(pieces), fina...  19.2 us
    pallas_call x3, Pallas kernels, backward_tiles(): pl.pallas_call(functools.partial(backward_kernel, nears, len(after)), out...  17.7 us
    ppermute x21, starting transfers between devices, swap(): return lambda v: lax.ppermute(v, axis, [(0, 1), (1, 0)])  11.9 us
    ppermute x21, waiting for transfers between devices, swap(): return lambda v: lax.ppermute(v, axis, [(0, 1), (1, 0)])  11.6 us
  transfers between devices with their start and end apart: 38, of which 11 were waited for; matrix products, arithmetic and copies ran while one was open for 4% of the time, Pallas kernels for 15%

profile of v2, /device:TPU:2, one launch (start us, length us, event | category | flops | bytes accessed | tf_op | source)
XLA Modules:
  0.0 216.6 jit_solution(13137153548751063780)
XLA Ops:
  0.6 2.2 %collective-permute-start = (bf16[3,128,256]{2,1,0:T(8,128)(2,1)}, bf16[3,128,256]{2,1,0:T(8,128)(2,1)S(1)}, u32[]{:S(2)}, u32[]{:S(2)}) collective-permute-start(bf16[3,128,256]{2,1,0:T(8,128)(2,1)} %bitcast.52), channel_id=1, source_target_pairs={{0,128},{128,0},{1,129},{129,1},{2,130},{130,2},{3,131},{131,3},{4... | collective-permute-start | bytes 589832 | tf_op jit(solution)/shard_map/ppermute | solution.py:40
  2.8 6.2 %collective-permute-done = bf16[3,128,256]{2,1,0:T(8,128)(2,1)S(1)} collective-permute-done((bf16[3,128,256]{2,1,0:T(8,128)(2,1)}, bf16[3,128,256]{2,1,0:T(8,128)(2,1)S(1)}, u32[]{:S(2)}, u32[]{:S(2)}) %collective-permute-start) | collective-permute-done | bytes 196640 | tf_op jit(solution)/shard_map/ppermute | solution.py:40
  9.1 1.0 pad_maximum_fusion.5.refs_0_
  10.0 2.0 collective-permute-start.2
  12.0 4.0 %collective-permute-start.4 = (bf16[6,128,256]{2,1,0:T(8,128)(2,1)S(1)}, bf16[6,128,256]{2,1,0:T(8,128)(2,1)S(1)}, u32[]{:S(2)}, u32[]{:S(2)}) collective-permute-start(bf16[6,128,256]{2,1,0:T(8,128)(2,1)S(1)} %pad_maximum_fusion.5.refs_0_), channel_id=1, source_target_pairs={{0,112},{16,0},{32,16},{48,32},{64,48},{80,64},{96,80},{112,96},{1... | collective-permute-start | bytes 1179656 | tf_op jit(solution)/shard_map/ppermute | solution.py:44
  16.1 8.2 %collective-permute-done.2.refs_2_ = bf16[6,128,256]{2,1,0:T(8,128)(2,1)S(1)} collective-permute-done((bf16[6,128,256]{2,1,0:T(8,128)(2,1)S(1)}, bf16[6,128,256]{2,1,0:T(8,128)(2,1)S(1)}, u32[]{:S(2)}, u32[]{:S(2)}) %collective-permute-start.2) | collective-permute-done | bytes 393248 | tf_op jit(solution)/shard_map/ppermute | solution.py:44
  24.2 3.2 %collective-permute-start.8 = (bf16[6,128,256]{2,1,0:T(8,128)(2,1)S(1)}, bf16[6,128,256]{2,1,0:T(8,128)(2,1)}, u32[]{:S(2)}, u32[]{:S(2)}) collective-permute-start(bf16[6,128,256]{2,1,0:T(8,128)(2,1)S(1)} %collective-permute-done.4.refs_4_), channel_id=1, source_target_pairs={{0,112},{16,0},{32,16},{48,32},{64,48},{80,64},{96,80},{112,96},{1... | collective-permute-start | bytes 1179656 | tf_op jit(solution)/shard_map/ppermute | solution.py:44
  27.5 0.7 reduce.1
  28.2 0.6 collective-permute-start.3
  28.9 5.9 %collective-permute-done.6.refs_0_ = bf16[6,128,256]{2,1,0:T(8,128)(2,1)S(1)} collective-permute-done((bf16[6,128,256]{2,1,0:T(8,128)(2,1)S(1)}, bf16[6,128,256]{2,1,0:T(8,128)(2,1)S(1)}, u32[]{:S(2)}, u32[]{:S(2)}) %collective-permute-start.6) | collective-permute-done | bytes 393248 | tf_op jit(solution)/shard_map/ppermute | solution.py:44
  34.8 0.7 fusion.16.pos_ref
  35.5 1.3 reduce.2.row_ref
  36.8 3.1 %collective-permute-start.12 = (bf16[6,128,256]{2,1,0:T(8,128)(2,1)}, bf16[6,128,256]{2,1,0:T(8,128)(2,1)S(1)}, u32[]{:S(2)}, u32[]{:S(2)}) collective-permute-start(bf16[6,128,256]{2,1,0:T(8,128)(2,1)} %collective-permute-done.8.refs_2_), channel_id=1, source_target_pairs={{0,112},{16,0},{32,16},{48,32},{64,48},{80,64},{96,80},{112,96},{1... | collective-permute-start | bytes 1179656 | tf_op jit(solution)/shard_map/ppermute | solution.py:44
  40.0 0.7 convert_reduce_fusion.starts_ref.before_hbm
  40.8 0.7 copy-done.12
  41.5 0.2 copy-done.13
  41.6 5.9 %forward_tiles.3 = (f32[25,128,256]{2,1,0:T(8,128)}, s32[1]{0:T(128)}) custom-call(s32[17]{0:T(128)} %convert_reduce_fusion.starts_ref.before_hbm, s32[1]{0:T(128)} %bitcast.z_ref, s32[288]{0:T(512)} %reduce.2.row_ref, s32[288]{0:T(512)} %fusion.16.pos_ref, bf16[288,128,128]{2,1,0:T(8,128)(2,1)} %bitcast.40, s32[17]{0:T(128)} %convert_reduce_fusion.starts_ref.before_hbm, ...), custom_call_target="tpu_custom_call" | custom-call | flops 905969664 | bytes 10616832 | tf_op jit(solution)/shard_map/forward_tiles/pallas_call | solution.py:164
  50.8 1.5 collective-permute-start.9
  52.4 0.1 collective-permute-start.11
  52.5 0.5 collective-permute-start.13
  53.0 3.2 %collective-permute-start.15 = (bf16[3,128,256]{2,1,0:T(8,128)(2,1)S(1)}, bf16[3,128,256]{2,1,0:T(8,128)(2,1)S(1)}, u32[]{:S(2)}, u32[]{:S(2)}) collective-permute-start(bf16[3,128,256]{2,1,0:T(8,128)(2,1)S(1)} %constant_dynamic-slice_fusion), channel_id=1, source_target_pairs={{0,112},{16,0},{32,16},{48,32},{64,48},{80,64},{96,80},{112,96},{1... | collective-permute-start | bytes 589832 | tf_op jit(solution)/shard_map/ppermute | solution.py:44
  56.2 4.2 %collective-permute-done.14.refs_0_ = bf16[3,128,256]{2,1,0:T(8,128)(2,1)S(1)} collective-permute-done((bf16[3,128,256]{2,1,0:T(8,128)(2,1)S(1)}, bf16[3,128,256]{2,1,0:T(8,128)(2,1)S(1)}, u32[]{:S(2)}, u32[]{:S(2)}) %collective-permute-start.14) | collective-permute-done | bytes 196640 | tf_op jit(solution)/shard_map/ppermute | solution.py:44
  60.4 0.2 collective-permute-done.15.refs_1_
  60.6 0.3 collective-permute-start.17
  61.0 0.7 copy-done.22
  61.7 0.1 copy-done.23
  61.9 0.2 copy-done.24
  62.0 8.1 %forward_tiles.4 = (f32[25,128,256]{2,1,0:T(8,128)}, s32[1]{0:T(128)}) custom-call(s32[17]{0:T(128)} %convert_reduce_fusion.starts_ref.before_hbm, s32[1]{0:T(128)} %bitcast.z_ref, s32[288]{0:T(512)} %reduce.2.row_ref, s32[288]{0:T(512)} %fusion.16.pos_ref, bf16[288,128,128]{2,1,0:T(8,128)(2,1)} %bitcast.41, f32[25,128,256]{2,1,0:T(8,128)} %get-tuple-element.25.before_hbm, ...), custom_call_target="tpu_custom_call" | custom-call | flops 1207959552 | bytes 14155776 | tf_op jit(solution)/shard_map/forward_tiles/pallas_call | solution.py:164
  70.2 0.6 copy-done.27
  70.9 5.2 %forward_tiles.5 = bf16[24,128,256]{2,1,0:T(8,128)(2,1)} custom-call(s32[17]{0:T(128)} %convert_reduce_fusion.starts_ref.before_hbm, s32[1]{0:T(128)} %bitcast.z_ref, s32[288]{0:T(512)} %reduce.2.row_ref, s32[288]{0:T(512)} %fusion.16.pos_ref, bf16[288,128,128]{2,1,0:T(8,128)(2,1)} %bitcast.42, f32[25,128,256]{2,1,0:T(8,128)} %get-tuple-element.26.before_hbm, ...), custom_call_target="tpu_custom_call" | custom-call | flops 301989888 | bytes 3538944 | tf_op jit(solution)/shard_map/forward_tiles/pallas_call | solution.py:164
  76.1 30.3 %all_to_all.19.parts_ref = bf16[8,384,256]{2,1,0:T(8,128)(2,1)} all-to-all(bf16[8,384,256]{2,1,0:T(8,128)(2,1)} %bitcast.46), channel_id=1, replica_groups=mesh['xh'=2,'z'=8,'core'=2,'y'=4,'xl'=2] {'y','xl'}, dimensions={0} | all-to-all | bytes 3145728 | tf_op jit(solution)/shard_map/all_to_all | solution.py:393
  106.4 3.5 %dense_block.1 = (bf16[384,256]{1,0:T(8,128)(2,1)}, bf16[8,432,256]{2,1,0:T(8,128)(2,1)}) custom-call(bf16[8,384,256]{2,1,0:T(8,128)(2,1)} %all_to_all.19.parts_ref, bf16[256,256]{1,0:T(8,128)(2,1)} %weight_ref.1, f32[1,256]{1,0:T(1,128)} %bitcast.54, bf16[384,256]{1,0:T(8,128)(2,1)} %cot_ref.1), custom_call_target="tpu_custom_call" | custom-call | tf_op jit(solution)/shard_map/dense_block/pallas_call | solution.py:267
  109.9 26.4 %all_to_all.20.err_hbm = bf16[8,432,256]{2,1,0:T(8,128)(2,1)S(1)} all-to-all(bf16[8,432,256]{2,1,0:T(8,128)(2,1)} %get-tuple-element.29), channel_id=1, replica_groups=mesh['xh'=2,'z'=8,'core'=2,'y'=4,'xl'=2] {'y','xl'}, dimensions={0} | all-to-all | bytes 3538944 | tf_op jit(solution)/shard_map/all_to_all | solution.py:398
  136.5 1.1 copy-done
  137.6 6.3 %backward_tiles.3 = (bf16[6,128,256]{2,1,0:T(8,128)(2,1)}, bf16[6,128,256]{2,1,0:T(8,128)(2,1)}, bf16[6,128,256]{2,1,0:T(8,128)(2,1)}, bf16[6,128,256]{2,1,0:T(8...) custom-call(s32[17]{0:T(128)} %convert_reduce_fusion.starts_ref.before_hbm, s32[1]{0:T(128)} %bitcast.z_ref, ...), custom_call_target="tpu_custom_call" | custom-call | flops 905969664 | bytes 10616832 | tf_op jit(solution)/shard_map/backward_tiles/pallas_call | solution.py:218
  144.0 0.9 collective-permute-start.21
  145.0 0.5 collective-permute-start.26
  145.5 4.0 %collective-permute-done.21 = bf16[48,256]{1,0:T(8,128)(2,1)S(1)} collective-permute-done((bf16[48,256]{1,0:T(8,128)(2,1)S(1)}, bf16[48,256]{1,0:T(8,128)(2,1)S(1)}, u32[]{:S(2)}, u32[]{:S(2)}) %collective-permute-start.21) | collective-permute-done | bytes 24608 | tf_op jit(solution)/shard_map/ppermute | solution.py:40
  149.5 1.1 convert_add_fusion.6
  150.8 0.6 copy-done.1
  151.4 1.2 collective-permute-start.27
  152.8 0.9 collective-permute-start.22
  153.7 5.6 %backward_tiles.4 = (bf16[6,128,256]{2,1,0:T(8,128)(2,1)}, bf16[6,128,256]{2,1,0:T(8,128)(2,1)}, bf16[6,128,256]{2,1,0:T(8,128)(2,1)}, bf16[6,128,256]{2,1,0:T(8,128)(2,1)}) custom-call(s32[17]{0:T(128)} %convert_reduce_fusion.starts_ref.before_hbm, s32[1]{0:T(128)} %bitcast.z_ref, s32[288]{0:T(512)} %reduce.2.row_ref, s32[288]{0:T(512)} %fusion.16.pos_ref, ...), custom_call_target="tpu_custom_call" | custom-call | flops 603979776 | bytes 7077888 | tf_op jit(solution)/shard_map/backward_tiles/pallas_call | solution.py:218
  159.4 0.5 collective-permute-start.24
  160.1 2.3 %collective-permute-start.31 = (bf16[816,256]{1,0:T(8,128)(2,1)S(1)}, bf16[816,256]{1,0:T(8,128)(2,1)S(1)}, u32[]{:S(2)}, u32[]{:S(2)}) collective-permute-start(bf16[816,256]{1,0:T(8,128)(2,1)S(1)} %pad_maximum_fusion.2.refs_1_), channel_id=1, source_target_pairs={{0,112},{16,0},{32,16},{48,32},{64,48},{80,64},{96,80},{112,96},{1... | collective-permute-start | bytes 1253384 | tf_op jit(solution)/shard_map/ppermute | solution.py:44
  162.4 0.1 collective-permute-start.23
  162.6 0.6 copy-done.3
  163.2 5.8 %backward_tiles.5 = (bf16[6,128,256]{2,1,0:T(8,128)(2,1)}, bf16[6,128,256]{2,1,0:T(8,128)(2,1)}, bf16[6,128,256]{2,1,0:T(8,128)(2,1)}, bf16[6,128,256]{2,1,0:T(8...) custom-call(s32[17]{0:T(128)} %convert_reduce_fusion.starts_ref.before_hbm, s32[1]{0:T(128)} %bitcast.z_ref, ...), custom_call_target="tpu_custom_call" | custom-call | flops 905969664 | bytes 10616832 | tf_op jit(solution)/shard_map/backward_tiles/pallas_call | solution.py:218
  169.0 0.9 collective-permute-start.30
  170.1 0.5 collective-permute-start.28
  170.7 1.3 collective-permute-done.34
  172.1 3.0 %collective-permute-done.23 = bf16[816,256]{1,0:T(8,128)(2,1)S(1)} collective-permute-done((bf16[816,256]{1,0:T(8,128)(2,1)S(1)}, bf16[816,256]{1,0:T(8,128)(2,1)S(1)}, u32[]{:S(2)}, u32[]{:S(2)}) %collective-permute-start.23) | collective-permute-done | bytes 417824 | tf_op jit(solution)/shard_map/ppermute | solution.py:44
  175.5 3.3 %collective-permute-start.33 = (bf16[816,256]{1,0:T(8,128)(2,1)S(1)}, bf16[816,256]{1,0:T(8,128)(2,1)S(1)}, u32[]{:S(2)}, u32[]{:S(2)}) collective-permute-start(bf16[816,256]{1,0:T(8,128)(2,1)S(1)} %pad_maximum_fusion.4), channel_id=1, source_target_pairs={{0,112},{16,0},{32,16},{48,32},{64,48},{80,64},{96,80},{112,96},{1... | collective-permute-start | bytes 1253384 | tf_op jit(solution)/shard_map/ppermute | solution.py:44
  178.9 8.1 %collective-permute-done.25 = bf16[816,256]{1,0:T(8,128)(2,1)S(1)} collective-permute-done((bf16[816,256]{1,0:T(8,128)(2,1)S(1)}, bf16[816,256]{1,0:T(8,128)(2,1)S(1)}, u32[]{:S(2)}, u32[]{:S(2)}) %collective-permute-start.25) | collective-permute-done | bytes 417824 | tf_op jit(solution)/shard_map/ppermute | solution.py:44
  187.3 0.1 fusion
  187.4 3.3 %collective-permute-start.35 = (bf16[768,256]{1,0:T(8,128)(2,1)S(1)}, bf16[768,256]{1,0:T(8,128)(2,1)S(1)}, u32[]{:S(2)}, u32[]{:S(2)}) collective-permute-start(bf16[768,256]{1,0:T(8,128)(2,1)S(1)} %fusion), channel_id=1, source_target_pairs={{0,112},{16,0},{32,16},{48,32},{64,48},{80,64},{96,80},{112,96},{1... | collective-permute-start | bytes 1179656 | tf_op jit(solution)/shard_map/ppermute | solution.py:44
  190.8 8.4 %collective-permute-done.35 = bf16[768,256]{1,0:T(8,128)(2,1)S(1)} collective-permute-done((bf16[768,256]{1,0:T(8,128)(2,1)S(1)}, bf16[768,256]{1,0:T(8,128)(2,1)S(1)}, u32[]{:S(2)}, u32[]{:S(2)}) %collective-permute-start.35) | collective-permute-done | bytes 393248 | tf_op jit(solution)/shard_map/ppermute | solution.py:44
  199.3 2.9 %collective-permute-start.36 = (bf16[384,256]{1,0:T(8,128)(2,1)S(1)}, bf16[384,256]{1,0:T(8,128)(2,1)S(1)}, u32[]{:S(2)}, u32[]{:S(2)}) collective-permute-start(bf16[384,256]{1,0:T(8,128)(2,1)S(1)} %slice.166), channel_id=1, source_target_pairs={{0,128},{128,0},{1,129},{129,1},{2,130},{130,2},{3,131},{131,3},{4... | collective-permute-start | bytes 589832 | tf_op jit(solution)/shard_map/ppermute | solution.py:40
  202.3 0.6 slice.151
  202.8 0.7 tile.2
  203.5 6.3 %all-to-all-start.2 = ((f32[8,32,256]{2,1,0:T(8,128)}), f32[8,32,256]{2,1,0:T(8,128)S(1)}, u32[]{:S(2)}, u32[]{:S(2)}) async-start(f32[8,32,256]{2,1,0:T(8,128)} %tile.2), calls=%async_computation.2 | async-start | bytes 524288 | tf_op jit(solution)/shard_map/all_to_all | solution.py:404
  209.8 0.7 fusion.5
  210.5 5.4 %all-to-all-done.2 = f32[8,32,256]{2,1,0:T(8,128)S(1)} async-done(((f32[8,32,256]{2,1,0:T(8,128)}), f32[8,32,256]{2,1,0:T(8,128)S(1)}, u32[]{:S(2)}, u32[]{:S(2)}) %all-to-all-start.2) | async-done | bytes 262176 | tf_op jit(solution)/shard_map/all_to_all | solution.py:404
  215.9 0.7 copy.12
  (131 shorter events, 2.7 us)
Async XLA Ops:
  0.6 8.4 %collective-permute-start = (bf16[3,128,256]{2,1,0:T(8,128)(2,1)}, bf16[3,128,256]{2,1,0:T(8,128)(2,1)S(1)}, u32[]{:S(2)}, u32[]{:S(2)}) collective-permute-start(bf16[3,128,256]{2,1,0:T(8,128)(2,1)} %bitcast.52), channel_id=1, source_target_pairs={{0,128},{128,0},{1,129},{129,1},{2,130},{130,2},{3,131},{131,3},{4... | collective-permute-start | bytes 589832 | tf_op jit(solution)/shard_map/ppermute | solution.py:40
  10.0 30.7 %copy-start.4 = (bf16[6,128,256]{2,1,0:T(8,128)(2,1)}, bf16[6,128,256]{2,1,0:T(8,128)(2,1)S(1)}, u32[]{:S(2)}) copy-start(bf16[6,128,256]{2,1,0:T(8,128)(2,1)S(1)} %pad_maximum_fusion.5.refs_0_) | copy-start | bytes 1179652
  10.0 14.2 %collective-permute-start.2 = (bf16[6,128,256]{2,1,0:T(8,128)(2,1)S(1)}, bf16[6,128,256]{2,1,0:T(8,128)(2,1)S(1)}, u32[]{:S(2)}, u32[]{:S(2)}) collective-permute-start(bf16[6,128,256]{2,1,0:T(8,128)(2,1)S(1)} %pad_maximum_fusion.5.refs_0_), channel_id=1, source_target_pairs={{0,16},{16,32},{32,48},{48,64},{64,80},{80,96},{96,112},{112,0},{1... | collective-permute-start | bytes 1179656 | tf_op jit(solution)/shard_map/ppermute | solution.py:44
  12.0 12.2 %collective-permute-start.4 = (bf16[6,128,256]{2,1,0:T(8,128)(2,1)S(1)}, bf16[6,128,256]{2,1,0:T(8,128)(2,1)S(1)}, u32[]{:S(2)}, u32[]{:S(2)}) collective-permute-start(bf16[6,128,256]{2,1,0:T(8,128)(2,1)S(1)} %pad_maximum_fusion.5.refs_0_), channel_id=1, source_target_pairs={{0,112},{16,0},{32,16},{48,32},{64,48},{80,64},{96,80},{112,96},{1... | collective-permute-start | bytes 1179656 | tf_op jit(solution)/shard_map/ppermute | solution.py:44
  24.2 16.5 %copy-start.9 = (bf16[6,128,256]{2,1,0:T(8,128)(2,1)}, bf16[6,128,256]{2,1,0:T(8,128)(2,1)S(1)}, u32[]{:S(2)}) copy-start(bf16[6,128,256]{2,1,0:T(8,128)(2,1)S(1)} %collective-permute-done.2.refs_2_) | copy-start | bytes 1179652
  24.2 10.6 %collective-permute-start.6 = (bf16[6,128,256]{2,1,0:T(8,128)(2,1)S(1)}, bf16[6,128,256]{2,1,0:T(8,128)(2,1)S(1)}, u32[]{:S(2)}, u32[]{:S(2)}) collective-permute-start(bf16[6,128,256]{2,1,0:T(8,128)(2,1)S(1)} %collective-permute-done.2.refs_2_), channel_id=1, source_target_pairs={{0,16},{16,32},{32,48},{48,64},{64,80},{80,96},{96,112},{112,0},{1... | collective-permute-start | bytes 1179656 | tf_op jit(solution)/shard_map/ppermute | solution.py:44
  24.2 16.5 %copy-start.10 = (bf16[6,128,256]{2,1,0:T(8,128)(2,1)}, bf16[6,128,256]{2,1,0:T(8,128)(2,1)S(1)}, u32[]{:S(2)}) copy-start(bf16[6,128,256]{2,1,0:T(8,128)(2,1)S(1)} %collective-permute-done.4.refs_4_) | copy-start | bytes 1179652
  24.2 12.5 %collective-permute-start.8 = (bf16[6,128,256]{2,1,0:T(8,128)(2,1)S(1)}, bf16[6,128,256]{2,1,0:T(8,128)(2,1)}, u32[]{:S(2)}, u32[]{:S(2)}) collective-permute-start(bf16[6,128,256]{2,1,0:T(8,128)(2,1)S(1)} %collective-permute-done.4.refs_4_), channel_id=1, source_target_pairs={{0,112},{16,0},{32,16},{48,32},{64,48},{80,64},{96,80},{112,96},{1... | collective-permute-start | bytes 1179656 | tf_op jit(solution)/shard_map/ppermute | solution.py:44
  27.5 12.4 %collective-permute-start.1 = (bf16[6,128,256]{2,1,0:T(8,128)(2,1)S(1)}, bf16[6,128,256]{2,1,0:T(8,128)(2,1)S(1)}, u32[]{:S(2)}, u32[]{:S(2)}) collective-permute-start(bf16[6,128,256]{2,1,0:T(8,128)(2,1)S(1)} %pad_maximum_fusion.5.refs_0_), channel_id=1, source_target_pairs={{0,8},{8,0},{1,9},{9,1},{2,10},{10,2},{3,11},{11,3},{4,12},{12,4},... | collective-permute-start | bytes 1179656 | tf_op jit(solution)/shard_map/ppermute | solution.py:40
  28.2 12.5 %collective-permute-start.3 = (bf16[6,128,256]{2,1,0:T(8,128)(2,1)S(1)}, bf16[6,128,256]{2,1,0:T(8,128)(2,1)S(1)}, u32[]{:S(2)}, u32[]{:S(2)}) collective-permute-start(bf16[6,128,256]{2,1,0:T(8,128)(2,1)S(1)} %collective-permute-done.2.refs_2_), channel_id=1, source_target_pairs={{0,8},{8,0},{1,9},{9,1},{2,10},{10,2},{3,11},{11,3},{4,12},{12,4},... | collective-permute-start | bytes 1179656 | tf_op jit(solution)/shard_map/ppermute | solution.py:40
  28.8 11.9 %collective-permute-start.5 = (bf16[6,128,256]{2,1,0:T(8,128)(2,1)S(1)}, bf16[6,128,256]{2,1,0:T(8,128)(2,1)S(1)}, u32[]{:S(2)}, u32[]{:S(2)}) collective-permute-start(bf16[6,128,256]{2,1,0:T(8,128)(2,1)S(1)} %collective-permute-done.4.refs_4_), channel_id=1, source_target_pairs={{0,8},{8,0},{1,9},{9,1},{2,10},{10,2},{3,11},{11,3},{4,12},{12,4},... | collective-permute-start | bytes 1179656 | tf_op jit(solution)/shard_map/ppermute | solution.py:40
  34.8 12.8 %copy-start.21 = (bf16[6,128,256]{2,1,0:T(8,128)(2,1)}, bf16[6,128,256]{2,1,0:T(8,128)(2,1)S(1)}, u32[]{:S(2)}) copy-start(bf16[6,128,256]{2,1,0:T(8,128)(2,1)S(1)} %collective-permute-done.6.refs_0_) | copy-start | bytes 1179652
  34.8 17.5 %collective-permute-start.10 = (bf16[6,128,256]{2,1,0:T(8,128)(2,1)S(1)}, bf16[6,128,256]{2,1,0:T(8,128)(2,1)S(1)}, u32[]{:S(2)}, u32[]{:S(2)}) collective-permute-start(bf16[6,128,256]{2,1,0:T(8,128)(2,1)S(1)} %collective-permute-done.6.refs_0_), channel_id=1, source_target_pairs={{0,16},{16,32},{32,48},{48,64},{64,80},{80,96},{96,112},{112,0},{1... | collective-permute-start | bytes 1179656 | tf_op jit(solution)/shard_map/ppermute | solution.py:44
  36.8 15.7 %collective-permute-start.12 = (bf16[6,128,256]{2,1,0:T(8,128)(2,1)}, bf16[6,128,256]{2,1,0:T(8,128)(2,1)S(1)}, u32[]{:S(2)}, u32[]{:S(2)}) collective-permute-start(bf16[6,128,256]{2,1,0:T(8,128)(2,1)} %collective-permute-done.8.refs_2_), channel_id=1, source_target_pairs={{0,112},{16,0},{32,16},{48,32},{64,48},{80,64},{96,80},{112,96},{1... | collective-permute-start | bytes 1179656 | tf_op jit(solution)/shard_map/ppermute | solution.py:44
  39.9 0.8 copy-start.11
  39.9 13.1 %collective-permute-start.7 = (bf16[6,128,256]{2,1,0:T(8,128)(2,1)S(1)}, bf16[6,128,256]{2,1,0:T(8,128)(2,1)}, u32[]{:S(2)}, u32[]{:S(2)}) collective-permute-start(bf16[6,128,256]{2,1,0:T(8,128)(2,1)S(1)} %collective-permute-done.6.refs_0_), channel_id=1, source_target_pairs={{0,8},{8,0},{1,9},{9,1},{2,10},{10,2},{3,11},{11,3},{4,12},{12,4},... | collective-permute-start | bytes 1179656 | tf_op jit(solution)/shard_map/ppermute | solution.py:40
  40.7 0.9 copy-start.13
  50.8 10.2 %collective-permute-start.9 = (bf16[6,128,256]{2,1,0:T(8,128)(2,1)}, bf16[6,128,256]{2,1,0:T(8,128)(2,1)S(1)}, u32[]{:S(2)}, u32[]{:S(2)}) collective-permute-start(bf16[6,128,256]{2,1,0:T(8,128)(2,1)} %collective-permute-done.8.refs_2_), channel_id=1, source_target_pairs={{0,8},{8,0},{1,9},{9,1},{2,10},{10,2},{3,11},{11,3},{4,12},{12,4},... | collective-permute-start | bytes 1179656 | tf_op jit(solution)/shard_map/ppermute | solution.py:40
  52.3 8.7 %copy-start.7 = (bf16[6,128,256]{2,1,0:T(8,128)(2,1)}, bf16[6,128,256]{2,1,0:T(8,128)(2,1)S(1)}, u32[]{:S(2)}) copy-start(bf16[6,128,256]{2,1,0:T(8,128)(2,1)S(1)} %collective-permute-done.10.refs_4_) | copy-start | bytes 1179652
  52.3 8.1 %collective-permute-start.14 = (bf16[3,128,256]{2,1,0:T(8,128)(2,1)S(1)}, bf16[3,128,256]{2,1,0:T(8,128)(2,1)S(1)}, u32[]{:S(2)}, u32[]{:S(2)}) collective-permute-start(bf16[3,128,256]{2,1,0:T(8,128)(2,1)S(1)} %constant_dynamic-slice_fusion.1), channel_id=1, source_target_pairs={{0,16},{16,32},{32,48},{48,64},{64,80},{80,96},{96,112},{112,0},{1... | collective-permute-start | bytes 589832 | tf_op jit(solution)/shard_map/ppermute | solution.py:44
  52.4 8.6 %collective-permute-start.11 = (bf16[6,128,256]{2,1,0:T(8,128)(2,1)S(1)}, bf16[6,128,256]{2,1,0:T(8,128)(2,1)S(1)}, u32[]{:S(2)}, u32[]{:S(2)}) collective-permute-start(bf16[6,128,256]{2,1,0:T(8,128)(2,1)S(1)} %collective-permute-done.10.refs_4_), channel_id=1, source_target_pairs={{0,8},{8,0},{1,9},{9,1},{2,10},{10,2},{3,11},{11,3},{4,12},{12,4},... | collective-permute-start | bytes 1179656 | tf_op jit(solution)/shard_map/ppermute | solution.py:40
  52.5 8.5 %copy-start.8 = (bf16[6,128,256]{2,1,0:T(8,128)(2,1)}, bf16[6,128,256]{2,1,0:T(8,128)(2,1)S(1)}, u32[]{:S(2)}) copy-start(bf16[6,128,256]{2,1,0:T(8,128)(2,1)S(1)} %collective-permute-done.12.refs_6_) | copy-start | bytes 1179652
  52.5 8.5 %collective-permute-start.13 = (bf16[6,128,256]{2,1,0:T(8,128)(2,1)S(1)}, bf16[6,128,256]{2,1,0:T(8,128)(2,1)S(1)}, u32[]{:S(2)}, u32[]{:S(2)}) collective-permute-start(bf16[6,128,256]{2,1,0:T(8,128)(2,1)S(1)} %collective-permute-done.12.refs_6_), channel_id=1, source_target_pairs={{0,8},{8,0},{1,9},{9,1},{2,10},{10,2},{3,11},{11,3},{4,12},{12,4},... | collective-permute-start | bytes 1179656 | tf_op jit(solution)/shard_map/ppermute | solution.py:40
  53.0 7.6 %collective-permute-start.15 = (bf16[3,128,256]{2,1,0:T(8,128)(2,1)S(1)}, bf16[3,128,256]{2,1,0:T(8,128)(2,1)S(1)}, u32[]{:S(2)}, u32[]{:S(2)}) collective-permute-start(bf16[3,128,256]{2,1,0:T(8,128)(2,1)S(1)} %constant_dynamic-slice_fusion), channel_id=1, source_target_pairs={{0,112},{16,0},{32,16},{48,32},{64,48},{80,64},{96,80},{112,96},{1... | collective-permute-start | bytes 589832 | tf_op jit(solution)/shard_map/ppermute | solution.py:44
  60.4 9.7 %copy-start.25 = (bf16[3,128,256]{2,1,0:T(8,128)(2,1)}, bf16[3,128,256]{2,1,0:T(8,128)(2,1)S(1)}, u32[]{:S(2)}) copy-start(bf16[3,128,256]{2,1,0:T(8,128)(2,1)S(1)} %collective-permute-done.14.refs_0_) | copy-start | bytes 589828
  60.4 9.7 %collective-permute-start.16 = (bf16[3,128,256]{2,1,0:T(8,128)(2,1)S(1)}, bf16[3,128,256]{2,1,0:T(8,128)(2,1)S(1)}, u32[]{:S(2)}, u32[]{:S(2)}) collective-permute-start(bf16[3,128,256]{2,1,0:T(8,128)(2,1)S(1)} %collective-permute-done.14.refs_0_), channel_id=1, source_target_pairs={{0,8},{8,0},{1,9},{9,1},{2,10},{10,2},{3,11},{11,3},{4,12},{12,4},... | collective-permute-start | bytes 589832 | tf_op jit(solution)/shard_map/ppermute | solution.py:40
  60.6 9.5 %copy-start.26 = (bf16[3,128,256]{2,1,0:T(8,128)(2,1)}, bf16[3,128,256]{2,1,0:T(8,128)(2,1)S(1)}, u32[]{:S(2)}) copy-start(bf16[3,128,256]{2,1,0:T(8,128)(2,1)S(1)} %collective-permute-done.15.refs_1_) | copy-start | bytes 589828
  60.6 9.5 %collective-permute-start.17 = (bf16[3,128,256]{2,1,0:T(8,128)(2,1)S(1)}, bf16[3,128,256]{2,1,0:T(8,128)(2,1)S(1)}, u32[]{:S(2)}, u32[]{:S(2)}) collective-permute-start(bf16[3,128,256]{2,1,0:T(8,128)(2,1)S(1)} %collective-permute-done.15.refs_1_), channel_id=1, source_target_pairs={{0,8},{8,0},{1,9},{9,1},{2,10},{10,2},{3,11},{11,3},{4,12},{12,4},... | collective-permute-start | bytes 589832 | tf_op jit(solution)/shard_map/ppermute | solution.py:40
  60.9 0.8 copy-start.22
  60.9 0.9 copy-start.23
  61.0 1.0 copy-start.24
  136.4 1.2 copy-start
  136.4 7.6 %collective-permute-start.20 = (bf16[48,256]{1,0:T(8,128)(2,1)S(1)}, bf16[48,256]{1,0:T(8,128)(2,1)S(1)}, u32[]{:S(2)}, u32[]{:S(2)}) collective-permute-start(bf16[48,256]{1,0:T(8,128)(2,1)S(1)} %slice_reduce_fusion), channel_id=1, source_target_pairs={{0,8},{8,0},{1,9},{9,1},{2,10},{10,2},{3,11},{11,3},{4,12},{12,4},... | collective-permute-start | bytes 73736 | tf_op jit(solution)/shard_map/ppermute | solution.py:40
  143.9 6.7 %copy-start.19 = (bf16[6,128,256]{2,1,0:T(8,128)(2,1)S(1)}, bf16[6,128,256]{2,1,0:T(8,128)(2,1)}, u32[]{:S(2)}) copy-start(bf16[6,128,256]{2,1,0:T(8,128)(2,1)} %get-tuple-element.32) | copy-start | bytes 1179652
  143.9 5.6 %collective-permute-start.18 = (bf16[6,128,256]{2,1,0:T(8,128)(2,1)}, bf16[6,128,256]{2,1,0:T(8,128)(2,1)S(1)}, u32[]{:S(2)}, u32[]{:S(2)}) collective-permute-start(bf16[6,128,256]{2,1,0:T(8,128)(2,1)} %get-tuple-element.31), channel_id=1, source_target_pairs={{0,8},{8,0},{1,9},{9,1},{2,10},{10,2},{3,11},{11,3},{4,12},{12,4},... | collective-permute-start | bytes 1179656 | tf_op jit(solution)/shard_map/ppermute | solution.py:40
  144.0 5.4 %collective-permute-start.21 = (bf16[48,256]{1,0:T(8,128)(2,1)S(1)}, bf16[48,256]{1,0:T(8,128)(2,1)S(1)}, u32[]{:S(2)}, u32[]{:S(2)}) collective-permute-start(bf16[48,256]{1,0:T(8,128)(2,1)S(1)} %add_convert_fusion.2), channel_id=1, source_target_pairs={{0,128},{128,0},{1,129},{129,1},{2,130},{130,2},{3,131},{131,3},{4... | collective-permute-start | bytes 73736 | tf_op jit(solution)/shard_map/ppermute | solution.py:40
  145.0 5.6 %collective-permute-start.19 = (bf16[6,128,256]{2,1,0:T(8,128)(2,1)}, bf16[6,128,256]{2,1,0:T(8,128)(2,1)S(1)}, u32[]{:S(2)}, u32[]{:S(2)}) collective-permute-start(bf16[6,128,256]{2,1,0:T(8,128)(2,1)} %get-tuple-element.33), channel_id=1, source_target_pairs={{0,8},{8,0},{1,9},{9,1},{2,10},{10,2},{3,11},{11,3},{4,12},{12,4},... | collective-permute-start | bytes 1179656 | tf_op jit(solution)/shard_map/ppermute | solution.py:40
  145.0 7.7 %collective-permute-start.26 = (bf16[6,128,256]{2,1,0:T(8,128)(2,1)}, bf16[6,128,256]{2,1,0:T(8,128)(2,1)S(1)}, u32[]{:S(2)}, u32[]{:S(2)}) collective-permute-start(bf16[6,128,256]{2,1,0:T(8,128)(2,1)} %get-tuple-element.37), channel_id=1, source_target_pairs={{0,8},{8,0},{1,9},{9,1},{2,10},{10,2},{3,11},{11,3},{4,12},{12,4},... | collective-permute-start | bytes 1179656 | tf_op jit(solution)/shard_map/ppermute | solution.py:40
  150.6 0.9 copy-start.1
  150.6 2.1 copy-start.17
  151.4 2.3 %copy-start.5 = (bf16[432,256]{1,0:T(8,128)(2,1)}, bf16[432,256]{1,0:T(8,128)(2,1)S(1)}, u32[]{:S(2)}) copy-start(bf16[432,256]{1,0:T(8,128)(2,1)S(1)} %get-tuple-element.49.refs_0_) | copy-start | bytes 663556
  151.4 2.3 %copy-start.6 = (bf16[432,256]{1,0:T(8,128)(2,1)}, bf16[432,256]{1,0:T(8,128)(2,1)S(1)}, u32[]{:S(2)}) copy-start(bf16[432,256]{1,0:T(8,128)(2,1)S(1)} %get-tuple-element.48.refs_1_) | copy-start | bytes 663556
  151.4 8.5 %collective-permute-start.27 = (bf16[432,256]{1,0:T(8,128)(2,1)S(1)}, bf16[432,256]{1,0:T(8,128)(2,1)S(1)}, u32[]{:S(2)}, u32[]{:S(2)}) collective-permute-start(bf16[432,256]{1,0:T(8,128)(2,1)S(1)} %get-tuple-element.48.refs_1_), channel_id=1, source_target_pairs={{0,112},{16,0},{32,16},{48,32},{64,48},{80,64},{96,80},{112,96},{1... | collective-permute-start | bytes 663560 | tf_op jit(solution)/shard_map/ppermute | solution.py:44
  152.8 9.5 %collective-permute-start.22 = (bf16[432,256]{1,0:T(8,128)(2,1)S(1)}, bf16[432,256]{1,0:T(8,128)(2,1)S(1)}, u32[]{:S(2)}, u32[]{:S(2)}) collective-permute-start(bf16[432,256]{1,0:T(8,128)(2,1)S(1)} %get-tuple-element.49.refs_0_), channel_id=1, source_target_pairs={{0,16},{16,32},{32,48},{48,64},{64,80},{80,96},{96,112},{112,0},{1... | collective-permute-start | bytes 663560 | tf_op jit(solution)/shard_map/ppermute | solution.py:44
  159.3 3.0 %slice-start = ((f32[6,128,256]{2,1,0:T(8,128)}), f32[3,128,256]{2,1,0:T(8,128)S(1)}, s32[]{:S(2)}) async-start(f32[6,128,256]{2,1,0:T(8,128)} %copy-done.1), calls=%async_computation.3 | async-start | bytes 786432 | tf_op jit(solution)/shard_map/slice | solution.py:360
  159.3 10.5 %collective-permute-start.32 = (bf16[6,128,256]{2,1,0:T(8,128)(2,1)}, bf16[6,128,256]{2,1,0:T(8,128)(2,1)S(1)}, u32[]{:S(2)}, u32[]{:S(2)}) collective-permute-start(bf16[6,128,256]{2,1,0:T(8,128)(2,1)} %get-tuple-element.43), channel_id=1, source_target_pairs={{0,8},{8,0},{1,9},{9,1},{2,10},{10,2},{3,11},{11,3},{4,12},{12,4},... | collective-permute-start | bytes 1179656 | tf_op jit(solution)/shard_map/ppermute | solution.py:40
  159.4 10.6 %collective-permute-start.24 = (bf16[6,128,256]{2,1,0:T(8,128)(2,1)}, bf16[6,128,256]{2,1,0:T(8,128)(2,1)S(1)}, u32[]{:S(2)}, u32[]{:S(2)}) collective-permute-start(bf16[6,128,256]{2,1,0:T(8,128)(2,1)} %get-tuple-element.35), channel_id=1, source_target_pairs={{0,8},{8,0},{1,9},{9,1},{2,10},{10,2},{3,11},{11,3},{4,12},{12,4},... | collective-permute-start | bytes 1179656 | tf_op jit(solution)/shard_map/ppermute | solution.py:40
  160.0 2.5 %copy-start.2 = (bf16[816,256]{1,0:T(8,128)(2,1)}, bf16[816,256]{1,0:T(8,128)(2,1)S(1)}, u32[]{:S(2)}) copy-start(bf16[816,256]{1,0:T(8,128)(2,1)S(1)} %pad_maximum_fusion.2.refs_1_) | copy-start | bytes 1253380
  160.1 15.3 %collective-permute-start.31 = (bf16[816,256]{1,0:T(8,128)(2,1)S(1)}, bf16[816,256]{1,0:T(8,128)(2,1)S(1)}, u32[]{:S(2)}, u32[]{:S(2)}) collective-permute-start(bf16[816,256]{1,0:T(8,128)(2,1)S(1)} %pad_maximum_fusion.2.refs_1_), channel_id=1, source_target_pairs={{0,112},{16,0},{32,16},{48,32},{64,48},{80,64},{96,80},{112,96},{1... | collective-permute-start | bytes 1253384 | tf_op jit(solution)/shard_map/ppermute | solution.py:44
  162.4 7.6 %copy-start.18 = (bf16[6,128,256]{2,1,0:T(8,128)(2,1)S(1)}, bf16[6,128,256]{2,1,0:T(8,128)(2,1)}, u32[]{:S(2)}) copy-start(bf16[6,128,256]{2,1,0:T(8,128)(2,1)} %get-tuple-element.42) | copy-start | bytes 1179652
  162.4 12.7 %collective-permute-start.23 = (bf16[816,256]{1,0:T(8,128)(2,1)S(1)}, bf16[816,256]{1,0:T(8,128)(2,1)S(1)}, u32[]{:S(2)}, u32[]{:S(2)}) collective-permute-start(bf16[816,256]{1,0:T(8,128)(2,1)S(1)} %pad_maximum_fusion.refs_0_), channel_id=1, source_target_pairs={{0,16},{16,32},{32,48},{48,64},{64,80},{80,96},{96,112},{112,0},{1... | collective-permute-start | bytes 1253384 | tf_op jit(solution)/shard_map/ppermute | solution.py:44
  169.0 1.6 copy-start.15
  169.0 3.0 %copy-start.20 = (bf16[6,128,256]{2,1,0:T(8,128)(2,1)S(1)}, bf16[6,128,256]{2,1,0:T(8,128)(2,1)}, u32[]{:S(2)}) copy-start(bf16[6,128,256]{2,1,0:T(8,128)(2,1)} %get-tuple-element.44) | copy-start | bytes 1179652
  169.0 21.7 %collective-permute-start.30 = (bf16[6,128,256]{2,1,0:T(8,128)(2,1)}, bf16[6,128,256]{2,1,0:T(8,128)(2,1)S(1)}, u32[]{:S(2)}, u32[]{:S(2)}) collective-permute-start(bf16[6,128,256]{2,1,0:T(8,128)(2,1)} %get-tuple-element.41), channel_id=1, source_target_pairs={{0,8},{8,0},{1,9},{9,1},{2,10},{10,2},{3,11},{11,3},{4,12},{12,4},... | collective-permute-start | bytes 1179656 | tf_op jit(solution)/shard_map/ppermute | solution.py:40
  169.9 2.1 collective-permute-start.34
  170.1 8.7 %collective-permute-start.28 = (bf16[6,128,256]{2,1,0:T(8,128)(2,1)}, bf16[6,128,256]{2,1,0:T(8,128)(2,1)S(1)}, u32[]{:S(2)}, u32[]{:S(2)}) collective-permute-start(bf16[6,128,256]{2,1,0:T(8,128)(2,1)} %get-tuple-element.39), channel_id=1, source_target_pairs={{0,8},{8,0},{1,9},{9,1},{2,10},{10,2},{3,11},{11,3},{4,12},{12,4},... | collective-permute-start | bytes 1179656 | tf_op jit(solution)/shard_map/ppermute | solution.py:40
  175.2 3.6 %copy-start.16 = (bf16[6,128,256]{2,1,0:T(8,128)(2,1)S(1)}, bf16[6,128,256]{2,1,0:T(8,128)(2,1)}, u32[]{:S(2)}) copy-start(bf16[6,128,256]{2,1,0:T(8,128)(2,1)} %get-tuple-element.38) | copy-start | bytes 1179652
  175.2 11.8 %collective-permute-start.25 = (bf16[816,256]{1,0:T(8,128)(2,1)S(1)}, bf16[816,256]{1,0:T(8,128)(2,1)S(1)}, u32[]{:S(2)}, u32[]{:S(2)}) collective-permute-start(bf16[816,256]{1,0:T(8,128)(2,1)S(1)} %pad_maximum_fusion.1), channel_id=1, source_target_pairs={{0,16},{16,32},{32,48},{48,64},{64,80},{80,96},{96,112},{112,0},{1... | collective-permute-start | bytes 1253384 | tf_op jit(solution)/shard_map/ppermute | solution.py:44
  175.5 11.8 %collective-permute-start.33 = (bf16[816,256]{1,0:T(8,128)(2,1)S(1)}, bf16[816,256]{1,0:T(8,128)(2,1)S(1)}, u32[]{:S(2)}, u32[]{:S(2)}) collective-permute-start(bf16[816,256]{1,0:T(8,128)(2,1)S(1)} %pad_maximum_fusion.4), channel_id=1, source_target_pairs={{0,112},{16,0},{32,16},{48,32},{64,48},{80,64},{96,80},{112,96},{1... | collective-permute-start | bytes 1253384 | tf_op jit(solution)/shard_map/ppermute | solution.py:44
  187.0 3.7 %copy-start.14 = (bf16[6,128,256]{2,1,0:T(8,128)(2,1)S(1)}, bf16[6,128,256]{2,1,0:T(8,128)(2,1)}, u32[]{:S(2)}) copy-start(bf16[6,128,256]{2,1,0:T(8,128)(2,1)} %get-tuple-element.40) | copy-start | bytes 1179652
  187.2 12.0 %collective-permute-start.29 = (bf16[816,256]{1,0:T(8,128)(2,1)S(1)}, bf16[816,256]{1,0:T(8,128)(2,1)S(1)}, u32[]{:S(2)}, u32[]{:S(2)}) collective-permute-start(bf16[816,256]{1,0:T(8,128)(2,1)S(1)} %pad_maximum_fusion.3), channel_id=1, source_target_pairs={{0,16},{16,32},{32,48},{48,64},{64,80},{80,96},{96,112},{112,0},{1... | collective-permute-start | bytes 1253384 | tf_op jit(solution)/shard_map/ppermute | solution.py:44
  187.4 11.8 %collective-permute-start.35 = (bf16[768,256]{1,0:T(8,128)(2,1)S(1)}, bf16[768,256]{1,0:T(8,128)(2,1)S(1)}, u32[]{:S(2)}, u32[]{:S(2)}) collective-permute-start(bf16[768,256]{1,0:T(8,128)(2,1)S(1)} %fusion), channel_id=1, source_target_pairs={{0,112},{16,0},{32,16},{48,32},{64,48},{80,64},{96,80},{112,96},{1... | collective-permute-start | bytes 1179656 | tf_op jit(solution)/shard_map/ppermute | solution.py:44
  199.3 10.5 %collective-permute-start.36 = (bf16[384,256]{1,0:T(8,128)(2,1)S(1)}, bf16[384,256]{1,0:T(8,128)(2,1)S(1)}, u32[]{:S(2)}, u32[]{:S(2)}) collective-permute-start(bf16[384,256]{1,0:T(8,128)(2,1)S(1)} %slice.166), channel_id=1, source_target_pairs={{0,128},{128,0},{1,129},{129,1},{2,130},{130,2},{3,131},{131,3},{4... | collective-permute-start | bytes 589832 | tf_op jit(solution)/shard_map/ppermute | solution.py:40
  203.5 12.4 %all-to-all-start.2 = ((f32[8,32,256]{2,1,0:T(8,128)}), f32[8,32,256]{2,1,0:T(8,128)S(1)}, u32[]{:S(2)}, u32[]{:S(2)}) async-start(f32[8,32,256]{2,1,0:T(8,128)} %tile.2), calls=%async_computation.2 | async-start | bytes 524288 | tf_op jit(solution)/shard_map/all_to_all | solution.py:404
  (4 other events, 2.9 us)

commit v3 on v2

--- a/solution.py
+++ b/solution.py
@@ -184,10 +184,16 @@
     )(*scalars, adj, before, *pieces)
 
 
-def backward_kernel(nears, ignored, starts_ref, z_ref, row_ref, pos_ref, adj_hbm, err_hbm, *refs):
+def backward_kernel(nears, ignored, with_grads, starts_ref, z_ref, row_ref, pos_ref, adj_hbm, err_hbm, *refs):
     refs = refs[ignored:]
     outs = refs[: 2 * len(nears)]
-    err, err_sem, adj, adj_sem, base_ref, first_ref, end_ref, acc = refs[2 * len(nears) :]
+    refs = refs[2 * len(nears) :]
+    if with_grads:
+        grad_ref, extra, extra_sem = refs[0], *refs[-2:]
+        refs = refs[1:-2]
+        extra_copy = pltpu.make_async_copy(err_hbm.at[:, pl.ds(NB, EXTRA)], extra, extra_sem)
+        extra_copy.start()
+    err, err_sem, adj, adj_sem, base_ref, first_ref, end_ref, acc = refs
     copies = [
         pltpu.make_async_copy(
             err_hbm.at[i // PER, pl.ds(i % PER * TILE, TILE)], err.at[i], err_sem.at[i]
@@ -210,25 +216,35 @@
         )
 
     for_pairs(count, adj_hbm, adj, adj_sem, base_ref, first_ref, end_ref, work)
+    if with_grads:
+        extra_copy.wait()
+        total = extra[0].astype(f32)
+        for b in range(1, N_BLK):
+            total += extra[b].astype(f32)
+        grad_ref[...] = total.astype(bf16)
     for i, out in enumerate(outs):
         out[...] = acc[i * XH * PER : (i + 1) * XH * PER].astype(bf16)
 
 
-def backward_tiles(scalars, adj, err, nears, after):
+def backward_tiles(scalars, adj, err, nears, after, with_grads):
+    grad_shape = [jax.ShapeDtypeStruct((EXTRA, HIDDEN), bf16)] if with_grads else []
+    grad_scratch = [pltpu.VMEM((N_BLK, EXTRA, HIDDEN), bf16), pltpu.SemaphoreType.DMA]
     return pl.pallas_call(
-        functools.partial(backward_kernel, nears, len(after)),
-        out_shape=[jax.ShapeDtypeStruct((XH * PER, TILE, HIDDEN), bf16)] * (2 * len(nears)),
+        functools.partial(backward_kernel, nears, len(after), with_grads),
+        out_shape=[jax.ShapeDtypeStruct((XH * PER, TILE, HIDDEN), bf16)] * (2 * len(nears))
+        + grad_shape,
         grid_spec=pltpu.PrefetchScalarGridSpec(
             num_scalar_prefetch=4,
             grid=(),
             in_specs=[HBM] + [ANY] * (1 + len(after)),
-            out_specs=[VMEM] * (2 * len(nears)),
+            out_specs=[VMEM] * (2 * len(nears) + len(grad_shape)),
             scratch_shapes=[
                 pltpu.VMEM((TR, TILE, HIDDEN), bf16),
                 pltpu.SemaphoreType.DMA((TR,)),
             ]
             + group_scratch(nears)
-            + [pltpu.VMEM((len(nears) * NEAR_TILES + 1, TILE, HIDDEN), f32)],
+            + [pltpu.VMEM((len(nears) * NEAR_TILES + 1, TILE, HIDDEN), f32)]
+            + (grad_scratch if with_grads else []),
         ),
         compiler_params=pltpu.CompilerParams(
             vmem_limit_bytes=VMEM_BYTES
@@ -277,49 +293,29 @@
     )(parts, weight, bias, cot)
 
 
-def by_z_kernel(z_ref, *refs):
-    total_ref, rows = refs[Z:]
-    for away in range(Z):
-        rows[away] = refs[away][...]
-    total = jnp.zeros((EXTRA, HIDDEN), f32)
-    for there in range(Z):
-        total += rows[lax.rem(there - z_ref[0] + Z, Z)].astype(f32)
-    total_ref[...] = total
-
-
-def sum_by_z(z, parts):
-    return pl.pallas_call(
-        by_z_kernel,
-        out_shape=jax.ShapeDtypeStruct((EXTRA, HIDDEN), f32),
-        grid_spec=pltpu.PrefetchScalarGridSpec(
-            num_scalar_prefetch=1,
-            grid=(),
-            in_specs=[VMEM] * Z,
-            out_specs=VMEM,
-            scratch_shapes=[pltpu.VMEM((Z, EXTRA, HIDDEN), bf16)],
-        ),
-        compiler_params=pltpu.CompilerParams(vmem_limit_bytes=4 * 2**20),
-        name="sum_by_z",
-    )(z, *parts)
-
-
 def gather_forward(scalars, adj, own):
     def pair(piece):
         return [piece, swap("core")(piece)]
+
+    def after(zero, one, two):
+        ran = zero[0] == 0
+        return jnp.where(ran, one, two), jnp.where(ran, two, one)
 
     both = jnp.concatenate([own, swap("xh")(own)], axis=0)
     right1, left1 = turn(both, 1), turn(both, -1)
     right2, left2 = turn(right1, 1), turn(left1, -1)
     near = pair(both) + pair(right1) + pair(left1)
     partial, zero = forward_tiles(scalars, adj, None, near, (0, 1, 2), False)
+    right2, left2 = after(zero, right2, left2)
     right3, left3 = turn(right2, 1), turn(left2, -1)
-    last = [
-        turn(lax.dynamic_slice_in_dim(right3, zero[0], PER), 1),
-        turn(lax.dynamic_slice_in_dim(left3, zero[0] + PER, PER), -1),
-    ]
-    middle = pair(right2) + pair(left2) + pair(right3) + pair(left3)
-    partial, _ = forward_tiles(scalars, adj, partial, middle, (3, 4, 5, 6), False)
-    last += [swap("core")(piece) for piece in last]
+    near = pair(right2) + pair(left2)
+    partial, zero = forward_tiles(scalars, adj, partial, near, (3, 4), False)
+    right4 = turn(lax.dynamic_slice_in_dim(right3, zero[0], PER), 1)
+    left4 = turn(lax.dynamic_slice_in_dim(left3, zero[0] + PER, PER), -1)
+    near = pair(right3) + pair(left3)
+    partial, zero = forward_tiles(scalars, adj, partial, near, (5, 6), False)
+    right4, left4 = after(zero, right4, left4)
+    last = [right4, left4] + [swap("core")(piece) for piece in (right4, left4)]
     return forward_tiles(scalars, adj, partial, last, (7,), True)
 
 
@@ -330,48 +326,30 @@
     return ((near * CORE + (owner % CORE ^ core)) * XH + (owner // (CORE * Z) ^ xh)) * PER + cols % PER
 
 
-def backward_scatter(scalars, adj, err, grads):
+def backward_scatter(scalars, adj, err):
     rows = XH * NB
     sums = [None] * Z
 
-    def tiles(nears, after):
-        outs = backward_tiles(scalars, adj, err, nears, after)
+    def tiles(nears, after=(), with_grads=False):
+        outs = backward_tiles(scalars, adj, err, nears, after, with_grads)
         for i, near in enumerate(nears):
             keep, send = outs[2 * i], swap("core")(outs[2 * i + 1])
             sums[near] = (keep.astype(f32) + send.astype(f32)).reshape(rows, HIDDEN)
-
-    tiles((5, 6, 7), [])
+        return outs[-1]
+
+    tiles((3, 4, 5, 6, 7))
     far = sums[7].astype(bf16)
-    right = jnp.concatenate([far[:NB], grads], axis=0)
-    left = jnp.concatenate([far[NB:], grads], axis=0)
-    from_left, from_right = [], []
-    for step in range(4):
-        if step == 0:
-            tiles((3, 4), [right, left])
-        if step == 1:
-            tiles((0, 1, 2), [right, left])
-        right, left = turn(right, 1), turn(left, -1)
-        size = rows if step > 0 else NB
-        from_left.append(right[size:])
-        if step < 3:
-            from_right.append(left[size:])
-        right, left = right[:size].astype(f32), left[:size].astype(f32)
-        if step == 0:
-            right = jnp.concatenate([sums[6][:NB] + right, sums[6][NB:]], axis=0)
-            left = jnp.concatenate([sums[5][:NB], sums[5][NB:] + left], axis=0)
-        else:
-            right = right + sums[6 - 2 * step]
-            left = left + sums[5 - 2 * step] if step < 3 else left
-        if step < 3:
-            right = jnp.concatenate([right.astype(bf16), from_left[-1]], axis=0)
-        if step < 2:
-            left = jnp.concatenate([left.astype(bf16), from_right[-1]], axis=0)
-        if step == 2:
-            left = left.astype(bf16)
-    here = right + left
+    right, left = far[:NB], far[NB:]
+    right, left = turn(right, 1).astype(f32), turn(left, -1).astype(f32)
+    right = jnp.concatenate([sums[6][:NB] + right, sums[6][NB:]], axis=0).astype(bf16)
+    left = jnp.concatenate([sums[5][:NB], sums[5][NB:] + left], axis=0).astype(bf16)
+    grads = tiles((0, 1, 2), (right, left), True)
+    for near in (4, 2):
+        right = (sums[near] + turn(right, 1).astype(f32)).astype(bf16)
+        left = (sums[near - 1] + turn(left, -1).astype(f32)).astype(bf16)
+    here = sums[0] + turn(right, 1).astype(f32) + turn(left, -1).astype(f32)
     across = swap("xh")(here[NB:].astype(bf16))
-    grad_x = (here[:NB] + across.astype(f32)).astype(bf16)
-    return grad_x, [grads] + from_right + from_left[::-1]
+    return (here[:NB] + across.astype(f32)).astype(bf16), grads
 
 
 def both_sides(rows, axis):
@@ -397,10 +375,10 @@
     activated, back = dense_block(parts, weight, bias_vec.reshape(1, HIDDEN), cotangent, scale)
     back = lax.all_to_all(back, BLK, split_axis=0, concat_axis=0, tiled=True)
 
-    grads = jnp.sum(back[:, NB:].astype(f32), axis=0)
+    grad_x, grads = backward_scatter(scalars, adj, back)
     grads = both_sides(both_sides(grads, "core"), "xh").astype(bf16)
-    grad_x, by_z = backward_scatter(scalars, adj, back, grads)
-    grads = sum_by_z(scalars[1], by_z)
+    by_z = lax.all_to_all(jnp.tile(grads, (Z, 1)), "z", split_axis=0, concat_axis=0, tiled=True)
+    grads = jnp.sum(by_z.reshape(Z, EXTRA, HIDDEN).astype(f32), axis=0)
     grad_w = lax.all_to_all(
         jnp.tile(grads[:GRAD_ROWS], (N_BLK, 1)), BLK, split_axis=0, concat_axis=0, tiled=True
     )

time: 219 us -> 233 us (1.064)
  other arithmetic: 7.6 us -> 14.9 us
  starting transfers between devices: 45.1 us -> 51.1 us
  waiting for transfers between devices: 55 us -> 52.5 us
    pallas_call x3 -> x4, Pallas kernels: 19.2 us -> 24.9 us  [forward_tiles(): pl.pallas_call(functools.partial(forward_kernel, nears, len(pieces), fina...]
    ppermute x21, waiting for transfers between devices: 11.6 us -> 16.4 us  [swap(): return lambda v: lax.ppermute(v, axis, [(0, 1), (1, 0)])]
    all_to_all x1, waiting for transfers between devices: 5.4 us -> 0.69 us  [shards(): lax.all_to_all(jnp.tile(grads[:GRAD_ROWS], (N_BLK, 1)), BLK, split_axis=0...]
    ppermute x16, starting transfers between devices: 26.9 us -> 31.6 us  [turn(): return lax.ppermute(v, 'z', [(i, (i + step) % Z) for i in range(Z)])]
    pallas_call x4 -> x2, Pallas kernels: 17.7 us -> 14.3 us  [backward_tiles(): pl.pallas_call(functools.partial(backward_kernel, nears, len(after), with...]
    all_to_all x0 -> x1, starting transfers between devices: none -> 3.39 us  [shards(): lax.all_to_all(jnp.tile(grads, (Z, 1)), 'z', split_axis=0, concat_axis=0,...]
    ppermute x21, starting transfers between devices: 11.9 us -> 8.89 us  [swap(): return lambda v: lax.ppermute(v, axis, [(0, 1), (1, 0)])]
    all_to_all x1, blocking collectives: 30.3 us -> 27.5 us  [shards(): lax.all_to_all(partial.reshape(N_BLK, NB, HIDDEN), BLK, split_axis=0, con...]
  transfers between devices with their start and end apart: 38 -> 39, of which waited for: 11 -> 15; matrix products, arithmetic and copies ran while one was open for 4% -> 7% of each run, Pallas kernels for 15% -> 11%
where the time goes in v3:
time: 233 us; the launch traced here: 228 us
  blocking collectives  55 us (24%)
  waiting for transfers between devices  52.5 us (23%)
  starting transfers between devices  51.1 us (22%)
  Pallas kernels  42.7 us (18%)
  other arithmetic  14.9 us (6%)
  local copies, waits for them, and re-layouts  6.38 us (3%)
  between operations  5.86 us (3%)
    ppermute x16, waiting for transfers between devices, turn(): return lax.ppermute(v, 'z', [(i, (i + step) % Z) for i in range(Z)])  35.4 us
    ppermute x16, starting transfers between devices, turn(): return lax.ppermute(v, 'z', [(i, (i + step) % Z) for i in range(Z)])  31.6 us
    all_to_all x1, blocking collectives, shards(): back = lax.all_to_all(back, BLK, split_axis=0, concat_axis=0, tiled=True)  27.6 us
    all_to_all x1, blocking collectives, shards(): lax.all_to_all(partial.reshape(N_BLK, NB, HIDDEN), BLK, split_axis=0, con...  27.5 us
    pallas_call x4, Pallas kernels, forward_tiles(): pl.pallas_call(functools.partial(forward_kernel, nears, len(pieces), fina...  24.9 us
    ppermute x21, waiting for transfers between devices, swap(): return lambda v: lax.ppermute(v, axis, [(0, 1), (1, 0)])  16.4 us
    pallas_call x2, Pallas kernels, backward_tiles(): pl.pallas_call(functools.partial(backward_kernel, nears, len(after), with...  14.3 us
    ppermute x21, starting transfers between devices, swap(): return lambda v: lax.ppermute(v, axis, [(0, 1), (1, 0)])  8.89 us
  transfers between devices with their start and end apart: 39, of which 15 were waited for; matrix products, arithmetic and copies ran while one was open for 7% of the time, Pallas kernels for 11%

profile of v3, /device:TPU:2, one launch (start us, length us, event | category | flops | bytes accessed | tf_op | source)
XLA Modules:
  0.0 228.4 jit_solution(9154691028778640278)
XLA Ops:
  0.6 2.2 collective-permute-start
  2.8 6.2 %collective-permute-done = bf16[3,128,256]{2,1,0:T(8,128)(2,1)S(1)} collective-permute-done((bf16[3,128,256]{2,1,0:T(8,128)(2,1)}, bf16[3,128,256]{2,1,0:T(8,128)(2,1)S(1)}, u32[]{:S(2)}, u32[]{:S(2)}) %collective-permute-start) | collective-permute-done | bytes 196640 | tf_op jit(solution)/shard_map/ppermute | solution.py:40
  9.1 1.0 pad_maximum_fusion.refs_0_
  10.0 2.0 collective-permute-start.2
  12.0 4.0 %collective-permute-start.4 = (bf16[6,128,256]{2,1,0:T(8,128)(2,1)S(1)}, bf16[6,128,256]{2,1,0:T(8,128)(2,1)S(1)}, u32[]{:S(2)}, u32[]{:S(2)}) collective-permute-start(bf16[6,128,256]{2,1,0:T(8,128)(2,1)S(1)} %pad_maximum_fusion.refs_0_), channel_id=1, source_target_pairs={{0,112},{16,0},{32,16},{48,32},{64,48},{80,64},{96,80},{112,96},{1... | collective-permute-start | bytes 1179656 | tf_op jit(solution)/shard_map/ppermute | solution.py:44
  16.1 8.1 %collective-permute-done.2.refs_2_ = bf16[6,128,256]{2,1,0:T(8,128)(2,1)S(1)} collective-permute-done((bf16[6,128,256]{2,1,0:T(8,128)(2,1)S(1)}, bf16[6,128,256]{2,1,0:T(8,128)(2,1)S(1)}, u32[]{:S(2)}, u32[]{:S(2)}) %collective-permute-start.2) | collective-permute-done | bytes 393248 | tf_op jit(solution)/shard_map/ppermute | solution.py:44
  24.2 0.5 collective-permute-start.5
  24.7 0.7 reduce
  25.4 1.3 reduce.1.row_ref
  26.7 2.6 %collective-permute-start.7 = (bf16[6,128,256]{2,1,0:T(8,128)(2,1)S(1)}, bf16[6,128,256]{2,1,0:T(8,128)(2,1)S(1)}, u32[]{:S(2)}, u32[]{:S(2)}) collective-permute-start(bf16[6,128,256]{2,1,0:T(8,128)(2,1)S(1)} %collective-permute-done.4.refs_4_), channel_id=1, source_target_pairs={{0,112},{16,0},{32,16},{48,32},{64,48},{80,64},{96,80},{112,96},{1... | collective-permute-start | bytes 1179656 | tf_op jit(solution)/shard_map/ppermute | solution.py:44
  29.3 0.7 convert_reduce_fusion.1.starts_ref.before_hbm
  30.0 0.6 fusion.16.pos_ref
  30.7 0.7 copy-done.11
  31.7 6.4 %forward_tiles.4 = (f32[25,128,256]{2,1,0:T(8,128)}, s32[1]{0:T(128)}) custom-call(s32[17]{0:T(128)} %convert_reduce_fusion.1.starts_ref.before_hbm, s32[1]{0:T(128)} %bitcast.z_ref, s32[288]{0:T(512)} %reduce.1.row_ref, s32[288]{0:T(512)} %fusion.16.pos_ref, bf16[288,128,128]{2,1,0:T(8,128)(2,1)} %bitcast.42, s32[17]{0:T(128)} %convert_reduce_fusion.1.starts_ref.before_hbm, ...), custom_call_target="tpu_custom_call" | custom-call | flops 905969664 | bytes 10616832 | tf_op jit(solution)/shard_map/forward_tiles/pallas_call | solution.py:164
  38.7 3.0 %collective-permute-done.6 = bf16[6,128,256]{2,1,0:T(8,128)(2,1)S(1)} collective-permute-done((bf16[6,128,256]{2,1,0:T(8,128)(2,1)S(1)}, bf16[6,128,256]{2,1,0:T(8,128)(2,1)S(1)}, u32[]{:S(2)}, u32[]{:S(2)}) %collective-permute-start.6) | collective-permute-done | bytes 393248 | tf_op jit(solution)/shard_map/ppermute | solution.py:44
  41.9 3.2 %collective-permute-start.12 = (bf16[6,128,256]{2,1,0:T(8,128)(2,1)S(1)}, bf16[6,128,256]{2,1,0:T(8,128)(2,1)S(1)}, u32[]{:S(2)}, u32[]{:S(2)}) collective-permute-start(bf16[6,128,256]{2,1,0:T(8,128)(2,1)S(1)} %get-tuple-element.54.refs_2_), channel_id=1, source_target_pairs={{0,112},{16,0},{32,16},{48,32},{64,48},{80,64},{96,80},{112,96},{1... | collective-permute-start | bytes 1179656 | tf_op jit(solution)/shard_map/ppermute | solution.py:44
  45.1 0.5 collective-permute-start.9
  45.6 7.8 %collective-permute-done.10.refs_0_ = bf16[6,128,256]{2,1,0:T(8,128)(2,1)S(1)} collective-permute-done((bf16[6,128,256]{2,1,0:T(8,128)(2,1)S(1)}, bf16[6,128,256]{2,1,0:T(8,128)(2,1)S(1)}, u32[]{:S(2)}, u32[]{:S(2)}) %collective-permute-start.10) | collective-permute-done | bytes 393248 | tf_op jit(solution)/shard_map/ppermute | solution.py:44
  53.5 0.5 collective-permute-start.13
  54.0 0.7 copy-done.16
  54.9 6.7 %forward_tiles.5 = (f32[25,128,256]{2,1,0:T(8,128)}, s32[1]{0:T(128)}) custom-call(s32[17]{0:T(128)} %convert_reduce_fusion.1.starts_ref.before_hbm, s32[1]{0:T(128)} %bitcast.z_ref, s32[288]{0:T(512)} %reduce.1.row_ref, s32[288]{0:T(512)} %fusion.16.pos_ref, bf16[288,128,128]{2,1,0:T(8,128)(2,1)} %bitcast.43, f32[25,128,256]{2,1,0:T(8,128)} %get-tuple-element.29.before_hbm, ...), custom_call_target="tpu_custom_call" | custom-call | flops 603979776 | bytes 7077888 | tf_op jit(solution)/shard_map/forward_tiles/pallas_call | solution.py:164
  63.5 4.0 %collective-permute-start.15 = (bf16[3,128,256]{2,1,0:T(8,128)(2,1)S(1)}, bf16[3,128,256]{2,1,0:T(8,128)(2,1)S(1)}, u32[]{:S(2)}, u32[]{:S(2)}) collective-permute-start(bf16[3,128,256]{2,1,0:T(8,128)(2,1)S(1)} %constant_dynamic-slice_fusion), channel_id=1, source_target_pairs={{0,112},{16,0},{32,16},{48,32},{64,48},{80,64},{96,80},{112,96},{1... | collective-permute-start | bytes 589832 | tf_op jit(solution)/shard_map/ppermute | solution.py:44
  69.1 0.8 copy-done.12
  70.1 6.6 %forward_tiles.6 = (f32[25,128,256]{2,1,0:T(8,128)}, s32[1]{0:T(128)}) custom-call(s32[17]{0:T(128)} %convert_reduce_fusion.1.starts_ref.before_hbm, s32[1]{0:T(128)} %bitcast.z_ref, s32[288]{0:T(512)} %reduce.1.row_ref, s32[288]{0:T(512)} %fusion.16.pos_ref, bf16[288,128,128]{2,1,0:T(8,128)(2,1)} %bitcast.44, f32[25,128,256]{2,1,0:T(8,128)} %get-tuple-element.31.before_hbm, ...), custom_call_target="tpu_custom_call" | custom-call | flops 603979776 | bytes 7077888 | tf_op jit(solution)/shard_map/forward_tiles/pallas_call | solution.py:164
  77.5 0.5 collective-permute-start.17
  78.0 0.9 collective-permute-done.16.refs_2_
  79.9 5.2 %forward_tiles.7 = bf16[24,128,256]{2,1,0:T(8,128)(2,1)} custom-call(s32[17]{0:T(128)} %convert_reduce_fusion.1.starts_ref.before_hbm, s32[1]{0:T(128)} %bitcast.z_ref, s32[288]{0:T(512)} %reduce.1.row_ref, s32[288]{0:T(512)} %fusion.16.pos_ref, bf16[288,128,128]{2,1,0:T(8,128)(2,1)} %bitcast.45, f32[25,128,256]{2,1,0:T(8,128)} %get-tuple-element.32.before_hbm, ...), custom_call_target="tpu_custom_call" | custom-call | flops 301989888 | bytes 3538944 | tf_op jit(solution)/shard_map/forward_tiles/pallas_call | solution.py:164
  85.1 27.5 %all_to_all.25.parts_ref = bf16[8,384,256]{2,1,0:T(8,128)(2,1)} all-to-all(bf16[8,384,256]{2,1,0:T(8,128)(2,1)} %bitcast.48), channel_id=1, replica_groups=mesh['xh'=2,'z'=8,'core'=2,'y'=4,'xl'=2] {'y','xl'}, dimensions={0} | all-to-all | bytes 3145728 | tf_op jit(solution)/shard_map/all_to_all | solution.py:371
  112.6 3.5 %dense_block.1 = (bf16[384,256]{1,0:T(8,128)(2,1)}, bf16[8,432,256]{2,1,0:T(8,128)(2,1)}) custom-call(bf16[8,384,256]{2,1,0:T(8,128)(2,1)} %all_to_all.25.parts_ref, bf16[256,256]{1,0:T(8,128)(2,1)} %weight_ref.1, f32[1,256]{1,0:T(1,128)} %bitcast.56, bf16[384,256]{1,0:T(8,128)(2,1)} %cot_ref.1), custom_call_target="tpu_custom_call" | custom-call | tf_op jit(solution)/shard_map/dense_block/pallas_call | solution.py:283
  116.1 27.6 %all_to_all.26.err_hbm = bf16[8,432,256]{2,1,0:T(8,128)(2,1)} all-to-all(bf16[8,432,256]{2,1,0:T(8,128)(2,1)} %get-tuple-element.36), channel_id=1, replica_groups=mesh['xh'=2,'z'=8,'core'=2,'y'=4,'xl'=2] {'y','xl'}, dimensions={0} | all-to-all | bytes 3538944 | tf_op jit(solution)/shard_map/all_to_all | solution.py:376
  143.6 7.8 %backward_tiles.2 = (bf16[6,128,256]{2,1,0:T(8,128)(2,1)}, bf16[6,128,256]{2,1,0:T(8,128)(2,1)}, bf16[6,128,256]{2,1,0:T(8,128)(2,1)}, bf16[6,128,256]{2,1,0:T(8...) custom-call(s32[17]{0:T(128)} %convert_reduce_fusion.1.starts_ref.be, ...), custom_call_target="tpu_custom_call" | custom-call | flops 1509949440 | bytes 17694720 | tf_op jit(solution)/shard_map/backward_tiles/pallas_call | solution.py:232
  151.5 0.5 collective-permute-start.19
  152.1 0.4 collective-permute-start.30
  152.6 0.8 collective-permute-done.18
  153.5 1.1 convert_add_fusion.6
  154.6 1.1 add_convert_fusion
  156.0 5.2 %collective-permute-start.22 = (bf16[384,256]{1,0:T(8,128)(2,1)S(1)}, bf16[384,256]{1,0:T(8,128)(2,1)S(1)}, u32[]{:S(2)}, u32[]{:S(2)}) collective-permute-start(bf16[384,256]{1,0:T(8,128)(2,1)S(1)} %bitcast.54), channel_id=1, source_target_pairs={{0,112},{16,0},{32,16},{48,32},{64,48},{80,64},{96,80},{112,96},{1... | collective-permute-start | bytes 589832 | tf_op jit(solution)/shard_map/ppermute | solution.py:44
  161.3 4.9 %collective-permute-done.20 = bf16[384,256]{1,0:T(8,128)(2,1)S(1)} collective-permute-done((bf16[384,256]{1,0:T(8,128)(2,1)S(1)}, bf16[384,256]{1,0:T(8,128)(2,1)S(1)}, u32[]{:S(2)}, u32[]{:S(2)}) %collective-permute-start.20) | collective-permute-done | bytes 196640 | tf_op jit(solution)/shard_map/ppermute | solution.py:44
  166.3 0.8 pad_maximum_fusion.1.refs_0_
  167.1 0.8 pad_maximum_fusion.2.refs_1_
  167.9 6.5 %backward_tiles.3 = (bf16[6,128,256]{2,1,0:T(8,128)(2,1)}, bf16[6,128,256]{2,1,0:T(8,128)(2,1)}, bf16[6,128,256]{2,1,0:T(8,128)(2,1)}, bf16[6,128,256]{2,1,0:T(8...) custom-call(s32[17]{0:T(128)} %convert_reduce_fusion.1.starts_ref.before_hbm, ...), custom_call_target="tpu_custom_call" | custom-call | flops 905969664 | bytes 10616832 | tf_op jit(solution)/shard_map/backward_tiles/pallas_call | solution.py:232
  174.9 4.4 %collective-permute-start.31 = (bf16[768,256]{1,0:T(8,128)(2,1)S(1)}, bf16[768,256]{1,0:T(8,128)(2,1)}, u32[]{:S(2)}, u32[]{:S(2)}) collective-permute-start(bf16[768,256]{1,0:T(8,128)(2,1)S(1)} %copy-done.2), channel_id=1, source_target_pairs={{0,112},{16,0},{32,16},{48,32},{64,48},{80,64},{96,80},{112,96},{1... | collective-permute-start | bytes 1179656 | tf_op jit(solution)/shard_map/ppermute | solution.py:44
  179.2 0.7 add_convert_fusion.2
  180.0 1.2 collective-permute-start.36
  181.5 0.5 collective-permute-start.29
  182.0 3.4 %collective-permute-done.36 = bf16[48,256]{1,0:T(8,128)(2,1)S(1)} collective-permute-done((bf16[48,256]{1,0:T(8,128)(2,1)S(1)}, bf16[48,256]{1,0:T(8,128)(2,1)S(1)}, u32[]{:S(2)}, u32[]{:S(2)}) %collective-permute-start.36) | collective-permute-done | bytes 24608 | tf_op jit(solution)/shard_map/ppermute | solution.py:40
  185.4 0.7 tile.4
  186.1 3.4 %all-to-all-start.2 = ((bf16[8,48,256]{2,1,0:T(8,128)(2,1)}), bf16[8,48,256]{2,1,0:T(8,128)(2,1)S(1)}, u32[]{:S(2)}, u32[]{:S(2)}) async-start(bf16[8,48,256]{2,1,0:T(8,128)(2,1)} %tile.4), calls=%async_computation.2 | async-start | bytes 393216 | tf_op jit(solution)/shard_map/all_to_all | solution.py:380
  189.5 1.2 fusion
  190.7 3.2 %collective-permute-start.32 = (bf16[768,256]{1,0:T(8,128)(2,1)S(1)}, bf16[768,256]{1,0:T(8,128)(2,1)S(1)}, u32[]{:S(2)}, u32[]{:S(2)}) collective-permute-start(bf16[768,256]{1,0:T(8,128)(2,1)S(1)} %fusion), channel_id=1, source_target_pairs={{0,112},{16,0},{32,16},{48,32},{64,48},{80,64},{96,80},{112,96},{1... | collective-permute-start | bytes 1179656 | tf_op jit(solution)/shard_map/ppermute | solution.py:44
  193.9 1.1 fusion.2
  195.2 1.1 convert_add_fusion.1
  196.3 1.1 convert_add_fusion.3
  197.4 7.9 %collective-permute-done.32 = bf16[768,256]{1,0:T(8,128)(2,1)S(1)} collective-permute-done((bf16[768,256]{1,0:T(8,128)(2,1)S(1)}, bf16[768,256]{1,0:T(8,128)(2,1)S(1)}, u32[]{:S(2)}, u32[]{:S(2)}) %collective-permute-start.32) | collective-permute-done | bytes 393248 | tf_op jit(solution)/shard_map/ppermute | solution.py:44
  205.4 2.3 %collective-permute-start.33 = (bf16[768,256]{1,0:T(8,128)(2,1)S(1)}, bf16[768,256]{1,0:T(8,128)(2,1)S(1)}, u32[]{:S(2)}, u32[]{:S(2)}) collective-permute-start(bf16[768,256]{1,0:T(8,128)(2,1)S(1)} %fusion.1), channel_id=1, source_target_pairs={{0,112},{16,0},{32,16},{48,32},{64,48},{80,64},{96,80},{112,96},{1... | collective-permute-start | bytes 1179656 | tf_op jit(solution)/shard_map/ppermute | solution.py:44
  208.1 0.7 tile.5
  208.8 7.2 %all-to-all-start.3 = ((f32[8,32,256]{2,1,0:T(8,128)}), f32[8,32,256]{2,1,0:T(8,128)S(1)}, u32[]{:S(2)}, u32[]{:S(2)}) async-start(f32[8,32,256]{2,1,0:T(8,128)} %tile.5), calls=%async_computation.3 | async-start | bytes 524288 | tf_op jit(solution)/shard_map/all_to_all | solution.py:382
  216.2 3.3 %collective-permute-done.28 = bf16[768,256]{1,0:T(8,128)(2,1)S(1)} collective-permute-done((bf16[768,256]{1,0:T(8,128)(2,1)S(1)}, bf16[768,256]{1,0:T(8,128)(2,1)S(1)}, u32[]{:S(2)}, u32[]{:S(2)}) %collective-permute-start.28) | collective-permute-done | bytes 393248 | tf_op jit(solution)/shard_map/ppermute | solution.py:44
  219.7 1.2 collective-permute-start.34
  220.9 0.6 slice.76
  221.5 0.7 all-to-all-done.3
  222.2 4.8 %collective-permute-done.34 = bf16[384,256]{1,0:T(8,128)(2,1)S(1)} collective-permute-done((bf16[384,256]{1,0:T(8,128)(2,1)S(1)}, bf16[384,256]{1,0:T(8,128)(2,1)S(1)}, u32[]{:S(2)}, u32[]{:S(2)}) %collective-permute-start.34) | collective-permute-done | bytes 196640 | tf_op jit(solution)/shard_map/ppermute | solution.py:40
  227.0 0.7 fusion.5
  227.7 0.7 copy.12
  (117 shorter events, 4.4 us)
Async XLA Ops:
  0.6 8.4 %collective-permute-start = (bf16[3,128,256]{2,1,0:T(8,128)(2,1)}, bf16[3,128,256]{2,1,0:T(8,128)(2,1)S(1)}, u32[]{:S(2)}, u32[]{:S(2)}) collective-permute-start(bf16[3,128,256]{2,1,0:T(8,128)(2,1)} %bitcast.52), channel_id=1, source_target_pairs={{0,128},{128,0},{1,129},{129,1},{2,130},{130,2},{3,131},{131,3},{4... | collective-permute-start | bytes 589832 | tf_op jit(solution)/shard_map/ppermute | solution.py:40
  10.0 20.7 %copy-start.1 = (bf16[6,128,256]{2,1,0:T(8,128)(2,1)}, bf16[6,128,256]{2,1,0:T(8,128)(2,1)S(1)}, u32[]{:S(2)}) copy-start(bf16[6,128,256]{2,1,0:T(8,128)(2,1)S(1)} %pad_maximum_fusion.refs_0_) | copy-start | bytes 1179652
  10.0 14.2 %collective-permute-start.2 = (bf16[6,128,256]{2,1,0:T(8,128)(2,1)S(1)}, bf16[6,128,256]{2,1,0:T(8,128)(2,1)S(1)}, u32[]{:S(2)}, u32[]{:S(2)}) collective-permute-start(bf16[6,128,256]{2,1,0:T(8,128)(2,1)S(1)} %pad_maximum_fusion.refs_0_), channel_id=1, source_target_pairs={{0,16},{16,32},{32,48},{48,64},{64,80},{80,96},{96,112},{112,0},{1... | collective-permute-start | bytes 1179656 | tf_op jit(solution)/shard_map/ppermute | solution.py:44
  12.0 12.2 %collective-permute-start.4 = (bf16[6,128,256]{2,1,0:T(8,128)(2,1)S(1)}, bf16[6,128,256]{2,1,0:T(8,128)(2,1)S(1)}, u32[]{:S(2)}, u32[]{:S(2)}) collective-permute-start(bf16[6,128,256]{2,1,0:T(8,128)(2,1)S(1)} %pad_maximum_fusion.refs_0_), channel_id=1, source_target_pairs={{0,112},{16,0},{32,16},{48,32},{64,48},{80,64},{96,80},{112,96},{1... | collective-permute-start | bytes 1179656 | tf_op jit(solution)/shard_map/ppermute | solution.py:44
  16.1 14.6 %collective-permute-start.1 = (bf16[6,128,256]{2,1,0:T(8,128)(2,1)S(1)}, bf16[6,128,256]{2,1,0:T(8,128)(2,1)S(1)}, u32[]{:S(2)}, u32[]{:S(2)}) collective-permute-start(bf16[6,128,256]{2,1,0:T(8,128)(2,1)S(1)} %pad_maximum_fusion.refs_0_), channel_id=1, source_target_pairs={{0,8},{8,0},{1,9},{9,1},{2,10},{10,2},{3,11},{11,3},{4,12},{12,4},... | collective-permute-start | bytes 1179656 | tf_op jit(solution)/shard_map/ppermute | solution.py:40
  24.2 6.5 %copy-start.9 = (bf16[6,128,256]{2,1,0:T(8,128)(2,1)}, bf16[6,128,256]{2,1,0:T(8,128)(2,1)S(1)}, u32[]{:S(2)}) copy-start(bf16[6,128,256]{2,1,0:T(8,128)(2,1)S(1)} %collective-permute-done.2.refs_2_) | copy-start | bytes 1179652
  24.2 6.4 %collective-permute-start.3 = (bf16[6,128,256]{2,1,0:T(8,128)(2,1)S(1)}, bf16[6,128,256]{2,1,0:T(8,128)(2,1)S(1)}, u32[]{:S(2)}, u32[]{:S(2)}) collective-permute-start(bf16[6,128,256]{2,1,0:T(8,128)(2,1)S(1)} %collective-permute-done.2.refs_2_), channel_id=1, source_target_pairs={{0,8},{8,0},{1,9},{9,1},{2,10},{10,2},{3,11},{11,3},{4,12},{12,4},... | collective-permute-start | bytes 1179656 | tf_op jit(solution)/shard_map/ppermute | solution.py:40
  24.2 6.5 %copy-start.10 = (bf16[6,128,256]{2,1,0:T(8,128)(2,1)}, bf16[6,128,256]{2,1,0:T(8,128)(2,1)S(1)}, u32[]{:S(2)}) copy-start(bf16[6,128,256]{2,1,0:T(8,128)(2,1)S(1)} %collective-permute-done.4.refs_4_) | copy-start | bytes 1179652
  24.2 6.4 %collective-permute-start.5 = (bf16[6,128,256]{2,1,0:T(8,128)(2,1)S(1)}, bf16[6,128,256]{2,1,0:T(8,128)(2,1)S(1)}, u32[]{:S(2)}, u32[]{:S(2)}) collective-permute-start(bf16[6,128,256]{2,1,0:T(8,128)(2,1)S(1)} %collective-permute-done.4.refs_4_), channel_id=1, source_target_pairs={{0,8},{8,0},{1,9},{9,1},{2,10},{10,2},{3,11},{11,3},{4,12},{12,4},... | collective-permute-start | bytes 1179656 | tf_op jit(solution)/shard_map/ppermute | solution.py:40
  26.7 12.0 %collective-permute-start.7 = (bf16[6,128,256]{2,1,0:T(8,128)(2,1)S(1)}, bf16[6,128,256]{2,1,0:T(8,128)(2,1)S(1)}, u32[]{:S(2)}, u32[]{:S(2)}) collective-permute-start(bf16[6,128,256]{2,1,0:T(8,128)(2,1)S(1)} %collective-permute-done.4.refs_4_), channel_id=1, source_target_pairs={{0,112},{16,0},{32,16},{48,32},{64,48},{80,64},{96,80},{112,96},{1... | collective-permute-start | bytes 1179656 | tf_op jit(solution)/shard_map/ppermute | solution.py:44
  29.3 12.4 %collective-permute-start.6 = (bf16[6,128,256]{2,1,0:T(8,128)(2,1)S(1)}, bf16[6,128,256]{2,1,0:T(8,128)(2,1)S(1)}, u32[]{:S(2)}, u32[]{:S(2)}) collective-permute-start(bf16[6,128,256]{2,1,0:T(8,128)(2,1)S(1)} %collective-permute-done.2.refs_2_), channel_id=1, source_target_pairs={{0,16},{16,32},{32,48},{48,64},{64,80},{80,96},{96,112},{112,0},{1... | collective-permute-start | bytes 1179656 | tf_op jit(solution)/shard_map/ppermute | solution.py:44
  30.7 0.8 copy-start.11
  30.7 0.9 copy-start.13
  30.7 1.0 copy-start.15
  41.8 12.2 %copy-start.3 = (bf16[6,128,256]{2,1,0:T(8,128)(2,1)}, bf16[6,128,256]{2,1,0:T(8,128)(2,1)S(1)}, u32[]{:S(2)}) copy-start(bf16[6,128,256]{2,1,0:T(8,128)(2,1)S(1)} %get-tuple-element.54.refs_2_) | copy-start | bytes 1179652
  41.8 12.2 %copy-start.4 = (bf16[6,128,256]{2,1,0:T(8,128)(2,1)}, bf16[6,128,256]{2,1,0:T(8,128)(2,1)S(1)}, u32[]{:S(2)}) copy-start(bf16[6,128,256]{2,1,0:T(8,128)(2,1)S(1)} %get-tuple-element.55.refs_0_) | copy-start | bytes 1179652
  41.8 11.7 %collective-permute-start.10 = (bf16[6,128,256]{2,1,0:T(8,128)(2,1)S(1)}, bf16[6,128,256]{2,1,0:T(8,128)(2,1)S(1)}, u32[]{:S(2)}, u32[]{:S(2)}) collective-permute-start(bf16[6,128,256]{2,1,0:T(8,128)(2,1)S(1)} %get-tuple-element.55.refs_0_), channel_id=1, source_target_pairs={{0,16},{16,32},{32,48},{48,64},{64,80},{80,96},{96,112},{112,0},{1... | collective-permute-start | bytes 1179656 | tf_op jit(solution)/shard_map/ppermute | solution.py:44
  41.9 11.6 %collective-permute-start.12 = (bf16[6,128,256]{2,1,0:T(8,128)(2,1)S(1)}, bf16[6,128,256]{2,1,0:T(8,128)(2,1)S(1)}, u32[]{:S(2)}, u32[]{:S(2)}) collective-permute-start(bf16[6,128,256]{2,1,0:T(8,128)(2,1)S(1)} %get-tuple-element.54.refs_2_), channel_id=1, source_target_pairs={{0,112},{16,0},{32,16},{48,32},{64,48},{80,64},{96,80},{112,96},{1... | collective-permute-start | bytes 1179656 | tf_op jit(solution)/shard_map/ppermute | solution.py:44
  45.1 8.9 %collective-permute-start.8 = (bf16[6,128,256]{2,1,0:T(8,128)(2,1)S(1)}, bf16[6,128,256]{2,1,0:T(8,128)(2,1)S(1)}, u32[]{:S(2)}, u32[]{:S(2)}) collective-permute-start(bf16[6,128,256]{2,1,0:T(8,128)(2,1)S(1)} %get-tuple-element.55.refs_0_), channel_id=1, source_target_pairs={{0,8},{8,0},{1,9},{9,1},{2,10},{10,2},{3,11},{11,3},{4,12},{12,4},... | collective-permute-start | bytes 1179656 | tf_op jit(solution)/shard_map/ppermute | solution.py:40
  45.1 8.9 %collective-permute-start.9 = (bf16[6,128,256]{2,1,0:T(8,128)(2,1)S(1)}, bf16[6,128,256]{2,1,0:T(8,128)(2,1)S(1)}, u32[]{:S(2)}, u32[]{:S(2)}) collective-permute-start(bf16[6,128,256]{2,1,0:T(8,128)(2,1)S(1)} %get-tuple-element.54.refs_2_), channel_id=1, source_target_pairs={{0,8},{8,0},{1,9},{9,1},{2,10},{10,2},{3,11},{11,3},{4,12},{12,4},... | collective-permute-start | bytes 1179656 | tf_op jit(solution)/shard_map/ppermute | solution.py:40
  53.5 15.3 %copy-start.5 = (bf16[6,128,256]{2,1,0:T(8,128)(2,1)}, bf16[6,128,256]{2,1,0:T(8,128)(2,1)S(1)}, u32[]{:S(2)}) copy-start(bf16[6,128,256]{2,1,0:T(8,128)(2,1)S(1)} %collective-permute-done.10.refs_0_) | copy-start | bytes 1179652
  53.5 15.7 %collective-permute-start.11 = (bf16[6,128,256]{2,1,0:T(8,128)(2,1)S(1)}, bf16[6,128,256]{2,1,0:T(8,128)(2,1)S(1)}, u32[]{:S(2)}, u32[]{:S(2)}) collective-permute-start(bf16[6,128,256]{2,1,0:T(8,128)(2,1)S(1)} %collective-permute-done.10.refs_0_), channel_id=1, source_target_pairs={{0,8},{8,0},{1,9},{9,1},{2,10},{10,2},{3,11},{11,3},{4,12},{12,4},... | collective-permute-start | bytes 1179656 | tf_op jit(solution)/shard_map/ppermute | solution.py:40
  53.5 10.0 %copy-start.6 = (bf16[6,128,256]{2,1,0:T(8,128)(2,1)}, bf16[6,128,256]{2,1,0:T(8,128)(2,1)S(1)}, u32[]{:S(2)}) copy-start(bf16[6,128,256]{2,1,0:T(8,128)(2,1)S(1)} %collective-permute-done.12.refs_2_) | copy-start | bytes 1179652
  53.5 15.7 %collective-permute-start.13 = (bf16[6,128,256]{2,1,0:T(8,128)(2,1)S(1)}, bf16[6,128,256]{2,1,0:T(8,128)(2,1)S(1)}, u32[]{:S(2)}, u32[]{:S(2)}) collective-permute-start(bf16[6,128,256]{2,1,0:T(8,128)(2,1)S(1)} %collective-permute-done.12.refs_2_), channel_id=1, source_target_pairs={{0,8},{8,0},{1,9},{9,1},{2,10},{10,2},{3,11},{11,3},{4,12},{12,4},... | collective-permute-start | bytes 1179656 | tf_op jit(solution)/shard_map/ppermute | solution.py:40
  54.0 0.8 copy-start.16
  54.0 0.9 copy-start.17
  63.5 13.8 %collective-permute-start.15 = (bf16[3,128,256]{2,1,0:T(8,128)(2,1)S(1)}, bf16[3,128,256]{2,1,0:T(8,128)(2,1)S(1)}, u32[]{:S(2)}, u32[]{:S(2)}) collective-permute-start(bf16[3,128,256]{2,1,0:T(8,128)(2,1)S(1)} %constant_dynamic-slice_fusion), channel_id=1, source_target_pairs={{0,112},{16,0},{32,16},{48,32},{64,48},{80,64},{96,80},{112,96},{1... | collective-permute-start | bytes 589832 | tf_op jit(solution)/shard_map/ppermute | solution.py:44
  68.8 8.5 %collective-permute-start.14 = (bf16[3,128,256]{2,1,0:T(8,128)(2,1)S(1)}, bf16[3,128,256]{2,1,0:T(8,128)(2,1)S(1)}, u32[]{:S(2)}, u32[]{:S(2)}) collective-permute-start(bf16[3,128,256]{2,1,0:T(8,128)(2,1)S(1)} %constant_dynamic-slice_fusion.1), channel_id=1, source_target_pairs={{0,16},{16,32},{32,48},{48,64},{64,80},{80,96},{96,112},{112,0},{1... | collective-permute-start | bytes 589832 | tf_op jit(solution)/shard_map/ppermute | solution.py:44
  69.1 0.8 copy-start.12
  69.1 0.9 copy-start.14
  77.4 1.8 copy-start.7
  77.4 1.8 copy-start.8
  77.4 1.5 collective-permute-start.16
  77.5 1.7 collective-permute-start.17
  79.2 0.7 copy-start.25
  151.4 4.4 %copy-start.23 = (bf16[6,128,256]{2,1,0:T(8,128)(2,1)S(1)}, bf16[6,128,256]{2,1,0:T(8,128)(2,1)}, u32[]{:S(2)}) copy-start(bf16[6,128,256]{2,1,0:T(8,128)(2,1)} %get-tuple-element.41) | copy-start | bytes 1179652
  151.4 2.0 collective-permute-start.18
  151.5 3.1 %collective-permute-start.19 = (bf16[6,128,256]{2,1,0:T(8,128)(2,1)}, bf16[6,128,256]{2,1,0:T(8,128)(2,1)S(1)}, u32[]{:S(2)}, u32[]{:S(2)}) collective-permute-start(bf16[6,128,256]{2,1,0:T(8,128)(2,1)} %get-tuple-element.40), channel_id=1, source_target_pairs={{0,8},{8,0},{1,9},{9,1},{2,10},{10,2},{3,11},{11,3},{4,12},{12,4},... | collective-permute-start | bytes 1179656 | tf_op jit(solution)/shard_map/ppermute | solution.py:40
  152.0 3.8 %collective-permute-start.21 = (bf16[6,128,256]{2,1,0:T(8,128)(2,1)}, bf16[6,128,256]{2,1,0:T(8,128)(2,1)S(1)}, u32[]{:S(2)}, u32[]{:S(2)}) collective-permute-start(bf16[6,128,256]{2,1,0:T(8,128)(2,1)} %get-tuple-element.42), channel_id=1, source_target_pairs={{0,8},{8,0},{1,9},{9,1},{2,10},{10,2},{3,11},{11,3},{4,12},{12,4},... | collective-permute-start | bytes 1179656 | tf_op jit(solution)/shard_map/ppermute | solution.py:40
  152.1 22.6 %collective-permute-start.30 = (bf16[6,128,256]{2,1,0:T(8,128)(2,1)}, bf16[6,128,256]{2,1,0:T(8,128)(2,1)S(1)}, u32[]{:S(2)}, u32[]{:S(2)}) collective-permute-start(bf16[6,128,256]{2,1,0:T(8,128)(2,1)} %get-tuple-element.52), channel_id=1, source_target_pairs={{0,8},{8,0},{1,9},{9,1},{2,10},{10,2},{3,11},{11,3},{4,12},{12,4},... | collective-permute-start | bytes 1179656 | tf_op jit(solution)/shard_map/ppermute | solution.py:40
  152.5 28.7 %collective-permute-start.25 = (bf16[6,128,256]{2,1,0:T(8,128)(2,1)}, bf16[6,128,256]{2,1,0:T(8,128)(2,1)S(1)}, u32[]{:S(2)}, u32[]{:S(2)}) collective-permute-start(bf16[6,128,256]{2,1,0:T(8,128)(2,1)} %get-tuple-element.48), channel_id=1, source_target_pairs={{0,8},{8,0},{1,9},{9,1},{2,10},{10,2},{3,11},{11,3},{4,12},{12,4},... | collective-permute-start | bytes 1179656 | tf_op jit(solution)/shard_map/ppermute | solution.py:40
  155.7 10.5 %collective-permute-start.20 = (bf16[384,256]{1,0:T(8,128)(2,1)S(1)}, bf16[384,256]{1,0:T(8,128)(2,1)S(1)}, u32[]{:S(2)}, u32[]{:S(2)}) collective-permute-start(bf16[384,256]{1,0:T(8,128)(2,1)S(1)} %bitcast.55), channel_id=1, source_target_pairs={{0,16},{16,32},{32,48},{48,64},{64,80},{80,96},{96,112},{112,0},{1... | collective-permute-start | bytes 589832 | tf_op jit(solution)/shard_map/ppermute | solution.py:44
  156.0 11.0 %collective-permute-start.22 = (bf16[384,256]{1,0:T(8,128)(2,1)S(1)}, bf16[384,256]{1,0:T(8,128)(2,1)S(1)}, u32[]{:S(2)}, u32[]{:S(2)}) collective-permute-start(bf16[384,256]{1,0:T(8,128)(2,1)S(1)} %bitcast.54), channel_id=1, source_target_pairs={{0,112},{16,0},{32,16},{48,32},{64,48},{80,64},{96,80},{112,96},{1... | collective-permute-start | bytes 589832 | tf_op jit(solution)/shard_map/ppermute | solution.py:44
  167.9 6.9 %copy-start.20 = (bf16[6,128,256]{2,1,0:T(8,128)(2,1)S(1)}, bf16[6,128,256]{2,1,0:T(8,128)(2,1)}, u32[]{:S(2)}) copy-start(bf16[6,128,256]{2,1,0:T(8,128)(2,1)} %get-tuple-element.51) | copy-start | bytes 1179652
  167.9 7.0 %copy-start.2 = (bf16[768,256]{1,0:T(8,128)(2,1)S(1)}, bf16[768,256]{1,0:T(8,128)(2,1)}, u32[]{:S(2)}) copy-start(bf16[768,256]{1,0:T(8,128)(2,1)} %pad_maximum_fusion.2.refs_1_) | copy-start | bytes 1179652
  167.9 13.3 %copy-start.19 = (bf16[6,128,256]{2,1,0:T(8,128)(2,1)S(1)}, bf16[6,128,256]{2,1,0:T(8,128)(2,1)}, u32[]{:S(2)}) copy-start(bf16[6,128,256]{2,1,0:T(8,128)(2,1)} %get-tuple-element.47) | copy-start | bytes 1179652
  167.9 13.4 %copy-start = (bf16[768,256]{1,0:T(8,128)(2,1)S(1)}, bf16[768,256]{1,0:T(8,128)(2,1)}, u32[]{:S(2)}) copy-start(bf16[768,256]{1,0:T(8,128)(2,1)} %pad_maximum_fusion.1.refs_0_) | copy-start | bytes 1179652
  174.4 4.8 %collective-permute-start.35 = (bf16[48,256]{1,0:T(8,128)(2,1)}, bf16[48,256]{1,0:T(8,128)(2,1)S(1)}, u32[]{:S(2)}, u32[]{:S(2)}) collective-permute-start(bf16[48,256]{1,0:T(8,128)(2,1)} %get-tuple-element.53), channel_id=1, source_target_pairs={{0,8},{8,0},{1,9},{9,1},{2,10},{10,2},{3,11},{11,3},{4,12},{12,4},... | collective-permute-start | bytes 73736 | tf_op jit(solution)/shard_map/ppermute | solution.py:40
  174.9 14.6 %collective-permute-start.31 = (bf16[768,256]{1,0:T(8,128)(2,1)S(1)}, bf16[768,256]{1,0:T(8,128)(2,1)}, u32[]{:S(2)}, u32[]{:S(2)}) collective-permute-start(bf16[768,256]{1,0:T(8,128)(2,1)S(1)} %copy-done.2), channel_id=1, source_target_pairs={{0,112},{16,0},{32,16},{48,32},{64,48},{80,64},{96,80},{112,96},{1... | collective-permute-start | bytes 1179656 | tf_op jit(solution)/shard_map/ppermute | solution.py:44
  180.0 5.4 %collective-permute-start.36 = (bf16[48,256]{1,0:T(8,128)(2,1)S(1)}, bf16[48,256]{1,0:T(8,128)(2,1)S(1)}, u32[]{:S(2)}, u32[]{:S(2)}) collective-permute-start(bf16[48,256]{1,0:T(8,128)(2,1)S(1)} %add_convert_fusion.2), channel_id=1, source_target_pairs={{0,128},{128,0},{1,129},{129,1},{2,130},{130,2},{3,131},{131,3},{4... | collective-permute-start | bytes 73736 | tf_op jit(solution)/shard_map/ppermute | solution.py:40
  181.2 15.1 %copy-start.21 = (bf16[6,128,256]{2,1,0:T(8,128)(2,1)S(1)}, bf16[6,128,256]{2,1,0:T(8,128)(2,1)}, u32[]{:S(2)}) copy-start(bf16[6,128,256]{2,1,0:T(8,128)(2,1)} %get-tuple-element.45) | copy-start | bytes 1179652
  181.3 12.6 %collective-permute-start.26 = (bf16[768,256]{1,0:T(8,128)(2,1)S(1)}, bf16[768,256]{1,0:T(8,128)(2,1)}, u32[]{:S(2)}, u32[]{:S(2)}) collective-permute-start(bf16[768,256]{1,0:T(8,128)(2,1)S(1)} %copy-done), channel_id=1, source_target_pairs={{0,16},{16,32},{32,48},{48,64},{64,80},{80,96},{96,112},{112,0},{1... | collective-permute-start | bytes 1179656 | tf_op jit(solution)/shard_map/ppermute | solution.py:44
  181.4 34.6 %collective-permute-start.23 = (bf16[6,128,256]{2,1,0:T(8,128)(2,1)}, bf16[6,128,256]{2,1,0:T(8,128)(2,1)S(1)}, u32[]{:S(2)}, u32[]{:S(2)}) collective-permute-start(bf16[6,128,256]{2,1,0:T(8,128)(2,1)} %get-tuple-element.44), channel_id=1, source_target_pairs={{0,8},{8,0},{1,9},{9,1},{2,10},{10,2},{3,11},{11,3},{4,12},{12,4},... | collective-permute-start | bytes 1179656 | tf_op jit(solution)/shard_map/ppermute | solution.py:40
  181.5 13.7 %collective-permute-start.29 = (bf16[6,128,256]{2,1,0:T(8,128)(2,1)}, bf16[6,128,256]{2,1,0:T(8,128)(2,1)}, u32[]{:S(2)}, u32[]{:S(2)}) collective-permute-start(bf16[6,128,256]{2,1,0:T(8,128)(2,1)} %get-tuple-element.50), channel_id=1, source_target_pairs={{0,8},{8,0},{1,9},{9,1},{2,10},{10,2},{3,11},{11,3},{4,12},{12,4},... | collective-permute-start | bytes 1179656 | tf_op jit(solution)/shard_map/ppermute | solution.py:40
  185.4 10.9 %collective-permute-start.24 = (bf16[6,128,256]{2,1,0:T(8,128)(2,1)}, bf16[6,128,256]{2,1,0:T(8,128)(2,1)}, u32[]{:S(2)}, u32[]{:S(2)}) collective-permute-start(bf16[6,128,256]{2,1,0:T(8,128)(2,1)} %get-tuple-element.46), channel_id=1, source_target_pairs={{0,8},{8,0},{1,9},{9,1},{2,10},{10,2},{3,11},{11,3},{4,12},{12,4},... | collective-permute-start | bytes 1179656 | tf_op jit(solution)/shard_map/ppermute | solution.py:40
  186.1 22.0 %all-to-all-start.2 = ((bf16[8,48,256]{2,1,0:T(8,128)(2,1)}), bf16[8,48,256]{2,1,0:T(8,128)(2,1)S(1)}, u32[]{:S(2)}, u32[]{:S(2)}) async-start(bf16[8,48,256]{2,1,0:T(8,128)(2,1)} %tile.4), calls=%async_computation.2 | async-start | bytes 393216 | tf_op jit(solution)/shard_map/all_to_all | solution.py:380
  189.5 5.7 %copy-start.22 = (bf16[6,128,256]{2,1,0:T(8,128)(2,1)S(1)}, bf16[6,128,256]{2,1,0:T(8,128)(2,1)}, u32[]{:S(2)}) copy-start(bf16[6,128,256]{2,1,0:T(8,128)(2,1)} %get-tuple-element.49) | copy-start | bytes 1179652
  190.7 14.6 %collective-permute-start.32 = (bf16[768,256]{1,0:T(8,128)(2,1)S(1)}, bf16[768,256]{1,0:T(8,128)(2,1)S(1)}, u32[]{:S(2)}, u32[]{:S(2)}) collective-permute-start(bf16[768,256]{1,0:T(8,128)(2,1)S(1)} %fusion), channel_id=1, source_target_pairs={{0,112},{16,0},{32,16},{48,32},{64,48},{80,64},{96,80},{112,96},{1... | collective-permute-start | bytes 1179656 | tf_op jit(solution)/shard_map/ppermute | solution.py:44
  195.1 12.8 %collective-permute-start.27 = (bf16[768,256]{1,0:T(8,128)(2,1)S(1)}, bf16[768,256]{1,0:T(8,128)(2,1)S(1)}, u32[]{:S(2)}, u32[]{:S(2)}) collective-permute-start(bf16[768,256]{1,0:T(8,128)(2,1)S(1)} %fusion.2), channel_id=1, source_target_pairs={{0,16},{16,32},{32,48},{48,64},{64,80},{80,96},{96,112},{112,0},{1... | collective-permute-start | bytes 1179656 | tf_op jit(solution)/shard_map/ppermute | solution.py:44
  196.3 19.8 %copy-start.18 = (bf16[6,128,256]{2,1,0:T(8,128)(2,1)S(1)}, bf16[6,128,256]{2,1,0:T(8,128)(2,1)}, u32[]{:S(2)}) copy-start(bf16[6,128,256]{2,1,0:T(8,128)(2,1)} %get-tuple-element.43) | copy-start | bytes 1179652
  205.4 10.8 %collective-permute-start.33 = (bf16[768,256]{1,0:T(8,128)(2,1)S(1)}, bf16[768,256]{1,0:T(8,128)(2,1)S(1)}, u32[]{:S(2)}, u32[]{:S(2)}) collective-permute-start(bf16[768,256]{1,0:T(8,128)(2,1)S(1)} %fusion.1), channel_id=1, source_target_pairs={{0,112},{16,0},{32,16},{48,32},{64,48},{80,64},{96,80},{112,96},{1... | collective-permute-start | bytes 1179656 | tf_op jit(solution)/shard_map/ppermute | solution.py:44
  207.9 11.6 %collective-permute-start.28 = (bf16[768,256]{1,0:T(8,128)(2,1)S(1)}, bf16[768,256]{1,0:T(8,128)(2,1)S(1)}, u32[]{:S(2)}, u32[]{:S(2)}) collective-permute-start(bf16[768,256]{1,0:T(8,128)(2,1)S(1)} %fusion.3), channel_id=1, source_target_pairs={{0,16},{16,32},{32,48},{48,64},{64,80},{80,96},{96,112},{112,0},{1... | collective-permute-start | bytes 1179656 | tf_op jit(solution)/shard_map/ppermute | solution.py:44
  208.8 13.4 %all-to-all-start.3 = ((f32[8,32,256]{2,1,0:T(8,128)}), f32[8,32,256]{2,1,0:T(8,128)S(1)}, u32[]{:S(2)}, u32[]{:S(2)}) async-start(f32[8,32,256]{2,1,0:T(8,128)} %tile.5), calls=%async_computation.3 | async-start | bytes 524288 | tf_op jit(solution)/shard_map/all_to_all | solution.py:382
  219.7 7.3 %collective-permute-start.34 = (bf16[384,256]{1,0:T(8,128)(2,1)S(1)}, bf16[384,256]{1,0:T(8,128)(2,1)S(1)}, u32[]{:S(2)}, u32[]{:S(2)}) collective-permute-start(bf16[384,256]{1,0:T(8,128)(2,1)S(1)} %slice.83), channel_id=1, source_target_pairs={{0,128},{128,0},{1,129},{129,1},{2,130},{130,2},{3,131},{131,3},{4... | collective-permute-start | bytes 589832 | tf_op jit(solution)/shard_map/ppermute | solution.py:40
  (1 other events, 0.7 us)

commit v4 on v2

--- a/solution.py
+++ b/solution.py
@@ -184,16 +184,17 @@
     )(*scalars, adj, before, *pieces)
 
 
-def backward_kernel(nears, ignored, starts_ref, z_ref, row_ref, pos_ref, adj_hbm, err_hbm, *refs):
-    refs = refs[ignored:]
-    outs = refs[: 2 * len(nears)]
-    err, err_sem, adj, adj_sem, base_ref, first_ref, end_ref, acc = refs[2 * len(nears) :]
+def backward_kernel(starts_ref, z_ref, row_ref, pos_ref, adj_hbm, err_hbm, *refs):
+    nears = tuple(range(Z))
+    outs = refs[: 2 * Z]
+    err, err_sem, extra, extra_sem, adj, adj_sem, base_ref, first_ref, end_ref, acc = refs[2 * Z :]
     copies = [
         pltpu.make_async_copy(
             err_hbm.at[i // PER, pl.ds(i % PER * TILE, TILE)], err.at[i], err_sem.at[i]
         )
         for i in range(TR)
     ]
+    copies.append(pltpu.make_async_copy(err_hbm.at[:, pl.ds(NB, EXTRA)], extra, extra_sem))
     for copy in copies:
         copy.start()
     count = plan_groups(
@@ -204,38 +205,49 @@
         copy.wait()
 
     def work(g, u, k, live):
-        pos = jnp.where(live, pos_ref[k] - nears[0] * NEAR_TILES, len(nears) * NEAR_TILES)
+        pos = jnp.where(live, pos_ref[k], TC)
         acc[pos] += lax.dot_general(
             adj[g, u], err[row_ref[k]], (((0,), (0,)), ((), ())), preferred_element_type=f32
         )
 
     for_pairs(count, adj_hbm, adj, adj_sem, base_ref, first_ref, end_ref, work)
+    grads = extra[0].astype(f32)
+    for b in range(1, N_BLK):
+        grads += extra[b].astype(f32)
     for i, out in enumerate(outs):
-        out[...] = acc[i * XH * PER : (i + 1) * XH * PER].astype(bf16)
-
-
-def backward_tiles(scalars, adj, err, nears, after):
+        for tile in range(XH * PER):
+            at = tile * TILE
+            if out.shape[0] > XH * NB and tile >= PER:
+                at += EXTRA
+            out[at : at + TILE] = acc[i * XH * PER + tile].astype(bf16)
+        if out.shape[0] > XH * NB:
+            out[NB : NB + EXTRA] = grads.astype(bf16)
+
+
+def backward_tiles(scalars, adj, err):
+    sizes = [XH * NB] * (2 * Z - 2) + [XH * NB + EXTRA] * 2
+    nears = tuple(range(Z))
     return pl.pallas_call(
-        functools.partial(backward_kernel, nears, len(after)),
-        out_shape=[jax.ShapeDtypeStruct((XH * PER, TILE, HIDDEN), bf16)] * (2 * len(nears)),
+        backward_kernel,
+        out_shape=[jax.ShapeDtypeStruct((size, HIDDEN), bf16) for size in sizes],
         grid_spec=pltpu.PrefetchScalarGridSpec(
             num_scalar_prefetch=4,
             grid=(),
-            in_specs=[HBM] + [ANY] * (1 + len(after)),
-            out_specs=[VMEM] * (2 * len(nears)),
+            in_specs=[HBM, ANY],
+            out_specs=[VMEM] * len(sizes),
             scratch_shapes=[
                 pltpu.VMEM((TR, TILE, HIDDEN), bf16),
                 pltpu.SemaphoreType.DMA((TR,)),
+                pltpu.VMEM((N_BLK, EXTRA, HIDDEN), bf16),
+                pltpu.SemaphoreType.DMA,
             ]
             + group_scratch(nears)
-            + [pltpu.VMEM((len(nears) * NEAR_TILES + 1, TILE, HIDDEN), f32)],
+            + [pltpu.VMEM((TC + 1, TILE, HIDDEN), f32)],
         ),
-        compiler_params=pltpu.CompilerParams(
-            vmem_limit_bytes=VMEM_BYTES
-        ),
+        compiler_params=pltpu.CompilerParams(vmem_limit_bytes=VMEM_BYTES),
         cost_estimate=tile_cost(nears),
         name="backward_tiles",
-    )(*scalars, adj, err, *after)
+    )(*scalars, adj, err)
 
 
 def dense_kernel(scale, parts_ref, weight_ref, bias_ref, cot_ref, act_ref, back_ref):
@@ -310,17 +322,15 @@
     both = jnp.concatenate([own, swap("xh")(own)], axis=0)
     right1, left1 = turn(both, 1), turn(both, -1)
     right2, left2 = turn(right1, 1), turn(left1, -1)
-    near = pair(both) + pair(right1) + pair(left1)
-    partial, zero = forward_tiles(scalars, adj, None, near, (0, 1, 2), False)
     right3, left3 = turn(right2, 1), turn(left2, -1)
-    last = [
-        turn(lax.dynamic_slice_in_dim(right3, zero[0], PER), 1),
-        turn(lax.dynamic_slice_in_dim(left3, zero[0] + PER, PER), -1),
-    ]
-    middle = pair(right2) + pair(left2) + pair(right3) + pair(left3)
-    partial, _ = forward_tiles(scalars, adj, partial, middle, (3, 4, 5, 6), False)
-    last += [swap("core")(piece) for piece in last]
-    return forward_tiles(scalars, adj, partial, last, (7,), True)
+    right4, left4 = turn(right3[:PER], 1), turn(left3[PER:], -1)
+    near = pair(both) + pair(right1) + pair(left1) + pair(right2) + pair(left2)
+    partial, zero = forward_tiles(scalars, adj, None, near, (0, 1, 2, 3, 4), False)
+    ran = zero[0] == 0
+    right4, left4 = jnp.where(ran, right4, left4), jnp.where(ran, left4, right4)
+    far = pair(right3) + pair(left3) + [right4, left4]
+    far += [swap("core")(piece) for piece in (right4, left4)]
+    return forward_tiles(scalars, adj, partial, far, (5, 6, 7), True)
 
 
 def place_of(cols, xh, z, core):
@@ -330,48 +340,36 @@
     return ((near * CORE + (owner % CORE ^ core)) * XH + (owner // (CORE * Z) ^ xh)) * PER + cols % PER
 
 
-def backward_scatter(scalars, adj, err, grads):
+def backward_scatter(scalars, adj, err):
     rows = XH * NB
-    sums = [None] * Z
-
-    def tiles(nears, after):
-        outs = backward_tiles(scalars, adj, err, nears, after)
-        for i, near in enumerate(nears):
-            keep, send = outs[2 * i], swap("core")(outs[2 * i + 1])
-            sums[near] = (keep.astype(f32) + send.astype(f32)).reshape(rows, HIDDEN)
-
-    tiles((5, 6, 7), [])
+    outs = backward_tiles(scalars, adj, err)
+    sums = [outs[2 * i].astype(f32) + swap("core")(outs[2 * i + 1]).astype(f32) for i in range(Z)]
     far = sums[7].astype(bf16)
-    right = jnp.concatenate([far[:NB], grads], axis=0)
-    left = jnp.concatenate([far[NB:], grads], axis=0)
-    from_left, from_right = [], []
-    for step in range(4):
-        if step == 0:
-            tiles((3, 4), [right, left])
-        if step == 1:
-            tiles((0, 1, 2), [right, left])
+    grads = far[NB : NB + EXTRA]
+    opposite = turn(grads, Z // 2)
+    right, left = turn(far[: NB + EXTRA], 1), turn(far[NB:], -1)
+    from_left, from_right = [right[NB:]], [left[:EXTRA]]
+    onto_right = sums[6][:NB] + right[:NB].astype(f32)
+    onto_left = sums[5][NB:] + left[EXTRA:].astype(f32)
+    right = jnp.concatenate(
+        [onto_right.astype(bf16), sums[6][NB:].astype(bf16), from_left[0]], axis=0
+    )
+    left = jnp.concatenate([sums[5][:NB].astype(bf16), onto_left.astype(bf16), from_right[0]], axis=0)
+    for near in (4, 2):
         right, left = turn(right, 1), turn(left, -1)
-        size = rows if step > 0 else NB
-        from_left.append(right[size:])
-        if step < 3:
-            from_right.append(left[size:])
-        right, left = right[:size].astype(f32), left[:size].astype(f32)
-        if step == 0:
-            right = jnp.concatenate([sums[6][:NB] + right, sums[6][NB:]], axis=0)
-            left = jnp.concatenate([sums[5][:NB], sums[5][NB:] + left], axis=0)
-        else:
-            right = right + sums[6 - 2 * step]
-            left = left + sums[5 - 2 * step] if step < 3 else left
-        if step < 3:
-            right = jnp.concatenate([right.astype(bf16), from_left[-1]], axis=0)
-        if step < 2:
-            left = jnp.concatenate([left.astype(bf16), from_right[-1]], axis=0)
-        if step == 2:
-            left = left.astype(bf16)
-    here = right + left
+        from_left.append(right[rows:])
+        from_right.append(left[rows:])
+        onto_right = (sums[near] + right[:rows].astype(f32)).astype(bf16)
+        onto_left = (sums[near - 1] + left[:rows].astype(f32)).astype(bf16)
+        if near == 4:
+            right = lax.dynamic_update_slice(right, onto_right, (0, 0))
+            left = lax.dynamic_update_slice(left, onto_left, (0, 0))
+    right, left = turn(onto_right, 1), turn(onto_left, -1)
+    by_z = [grads] + from_right + [opposite] + from_left[::-1]
+    grads = both_sides(sum_by_z(scalars[1], by_z), "xh")
+    here = sums[0] + right.astype(f32) + left.astype(f32)
     across = swap("xh")(here[NB:].astype(bf16))
-    grad_x = (here[:NB] + across.astype(f32)).astype(bf16)
-    return grad_x, [grads] + from_right + from_left[::-1]
+    return (here[:NB] + across.astype(f32)).astype(bf16), grads
 
 
 def both_sides(rows, axis):
@@ -397,10 +395,7 @@
     activated, back = dense_block(parts, weight, bias_vec.reshape(1, HIDDEN), cotangent, scale)
     back = lax.all_to_all(back, BLK, split_axis=0, concat_axis=0, tiled=True)
 
-    grads = jnp.sum(back[:, NB:].astype(f32), axis=0)
-    grads = both_sides(both_sides(grads, "core"), "xh").astype(bf16)
-    grad_x, by_z = backward_scatter(scalars, adj, back, grads)
-    grads = sum_by_z(scalars[1], by_z)
+    grad_x, grads = backward_scatter(scalars, adj, back)
     grad_w = lax.all_to_all(
         jnp.tile(grads[:GRAD_ROWS], (N_BLK, 1)), BLK, split_axis=0, concat_axis=0, tiled=True
     )

time: 219 us -> 220 us (level)
  Pallas kernels: 40.5 us -> 29.3 us
  starting transfers between devices: 45.1 us -> 56.1 us
  waiting for transfers between devices: 55 us -> 64.7 us
  local copies, waits for them, and re-layouts: 7.2 us -> 4.24 us
  between operations: 4.53 us -> 1.82 us
    ppermute x16 -> x17, waiting for transfers between devices: 38 us -> 50 us  [turn(): return lax.ppermute(v, 'z', [(i, (i + step) % Z) for i in range(Z)])]
    ppermute x16 -> x17, starting transfers between devices: 26.9 us -> 34.2 us  [turn(): return lax.ppermute(v, 'z', [(i, (i + step) % Z) for i in range(Z)])]
    pallas_call x3 -> x1, Pallas kernels: 17.7 us -> 10.6 us  [backward_tiles(): pl.pallas_call(backward_kernel, out_shape=[jax.ShapeDtypeStruct((size, HI...]
    unnamed x59 -> x53, local copies, waits for them, and re-layouts: 5.73 us -> 1.45 us
    pallas_call x3 -> x2, Pallas kernels: 19.2 us -> 15.2 us  [forward_tiles(): pl.pallas_call(functools.partial(forward_kernel, nears, len(pieces), fina...]
    all_to_all x1, waiting for transfers between devices: 5.4 us -> 2.19 us  [shards(): lax.all_to_all(jnp.tile(grads[:GRAD_ROWS], (N_BLK, 1)), BLK, split_axis=0...]
    ppermute x21 -> x20, starting transfers between devices: 11.9 us -> 13.4 us  [swap(): return lambda v: lax.ppermute(v, axis, [(0, 1), (1, 0)])]
    ppermute x21 -> x20, waiting for transfers between devices: 11.6 us -> 12.5 us  [swap(): return lambda v: lax.ppermute(v, axis, [(0, 1), (1, 0)])]
  transfers between devices with their start and end apart: 38 -> 38, of which waited for: 11 -> 14; matrix products, arithmetic and copies ran while one was open for 4% -> 4% of each run, Pallas kernels for 15% -> 4%
where the time goes in v4:
time: 220 us
  waiting for transfers between devices  64.7 us (29%)
  starting transfers between devices  56.1 us (26%)
  blocking collectives  54.8 us (25%)
  Pallas kernels  29.3 us (13%)
  other arithmetic  8.51 us (4%)
  local copies, waits for them, and re-layouts  4.24 us (2%)
    ppermute x17, waiting for transfers between devices, turn(): return lax.ppermute(v, 'z', [(i, (i + step) % Z) for i in range(Z)])  50 us
    ppermute x17, starting transfers between devices, turn(): return lax.ppermute(v, 'z', [(i, (i + step) % Z) for i in range(Z)])  34.2 us
    all_to_all x1, blocking collectives, shards(): lax.all_to_all(partial.reshape(N_BLK, NB, HIDDEN), BLK, split_axis=0, con...  29.3 us
    all_to_all x1, blocking collectives, shards(): back = lax.all_to_all(back, BLK, split_axis=0, concat_axis=0, tiled=True)  25.6 us
    pallas_call x2, Pallas kernels, forward_tiles(): pl.pallas_call(functools.partial(forward_kernel, nears, len(pieces), fina...  15.2 us
    ppermute x20, starting transfers between devices, swap(): return lambda v: lax.ppermute(v, axis, [(0, 1), (1, 0)])  13.4 us
    ppermute x20, waiting for transfers between devices, swap(): return lambda v: lax.ppermute(v, axis, [(0, 1), (1, 0)])  12.5 us
    pallas_call x1, Pallas kernels, backward_tiles(): pl.pallas_call(backward_kernel, out_shape=[jax.ShapeDtypeStruct((size, HI...  10.6 us
  transfers between devices with their start and end apart: 38, of which 14 were waited for; matrix products, arithmetic and copies ran while one was open for 4% of the time, Pallas kernels for 4%

profile of v4, /device:TPU:2, one launch (start us, length us, event | category | flops | bytes accessed | tf_op | source)
XLA Modules:
  0.0 219.5 jit_solution(3376516945553459118)
XLA Ops:
  0.6 2.2 %collective-permute-start = (bf16[3,128,256]{2,1,0:T(8,128)(2,1)}, bf16[3,128,256]{2,1,0:T(8,128)(2,1)S(1)}, u32[]{:S(2)}, u32[]{:S(2)}) collective-permute-start(bf16[3,128,256]{2,1,0:T(8,128)(2,1)} %bitcast.13), channel_id=1, source_target_pairs={{0,128},{128,0},{1,129},{129,1},{2,130},{130,2},{3,131},{131,3},{4... | collective-permute-start | bytes 589832 | tf_op jit(solution)/shard_map/ppermute | solution.py:40
  2.8 6.2 %collective-permute-done = bf16[3,128,256]{2,1,0:T(8,128)(2,1)S(1)} collective-permute-done((bf16[3,128,256]{2,1,0:T(8,128)(2,1)}, bf16[3,128,256]{2,1,0:T(8,128)(2,1)S(1)}, u32[]{:S(2)}, u32[]{:S(2)}) %collective-permute-start) | collective-permute-done | bytes 196640 | tf_op jit(solution)/shard_map/ppermute | solution.py:40
  9.1 1.0 pad_maximum_fusion.2.refs_0_
  10.0 2.0 collective-permute-start.2
  12.0 4.0 %collective-permute-start.4 = (bf16[6,128,256]{2,1,0:T(8,128)(2,1)S(1)}, bf16[6,128,256]{2,1,0:T(8,128)(2,1)S(1)}, u32[]{:S(2)}, u32[]{:S(2)}) collective-permute-start(bf16[6,128,256]{2,1,0:T(8,128)(2,1)S(1)} %pad_maximum_fusion.2.refs_0_), channel_id=1, source_target_pairs={{0,112},{16,0},{32,16},{48,32},{64,48},{80,64},{96,80},{112,96},{1... | collective-permute-start | bytes 1179656 | tf_op jit(solution)/shard_map/ppermute | solution.py:44
  16.1 8.2 %collective-permute-done.2.refs_2_ = bf16[6,128,256]{2,1,0:T(8,128)(2,1)S(1)} collective-permute-done((bf16[6,128,256]{2,1,0:T(8,128)(2,1)S(1)}, bf16[6,128,256]{2,1,0:T(8,128)(2,1)S(1)}, u32[]{:S(2)}, u32[]{:S(2)}) %collective-permute-start.2) | collective-permute-done | bytes 393248 | tf_op jit(solution)/shard_map/ppermute | solution.py:44
  24.2 3.2 %collective-permute-start.8 = (bf16[6,128,256]{2,1,0:T(8,128)(2,1)S(1)}, bf16[6,128,256]{2,1,0:T(8,128)(2,1)S(1)}, u32[]{:S(2)}, u32[]{:S(2)}) collective-permute-start(bf16[6,128,256]{2,1,0:T(8,128)(2,1)S(1)} %collective-permute-done.4.refs_4_), channel_id=1, source_target_pairs={{0,112},{16,0},{32,16},{48,32},{64,48},{80,64},{96,80},{112,96},{1... | collective-permute-start | bytes 1179656 | tf_op jit(solution)/shard_map/ppermute | solution.py:44
  27.5 7.3 %collective-permute-done.6.refs_6_ = bf16[6,128,256]{2,1,0:T(8,128)(2,1)S(1)} collective-permute-done((bf16[6,128,256]{2,1,0:T(8,128)(2,1)S(1)}, bf16[6,128,256]{2,1,0:T(8,128)(2,1)S(1)}, u32[]{:S(2)}, u32[]{:S(2)}) %collective-permute-start.6) | collective-permute-done | bytes 393248 | tf_op jit(solution)/shard_map/ppermute | solution.py:44
  34.8 3.2 %collective-permute-start.12 = (bf16[6,128,256]{2,1,0:T(8,128)(2,1)S(1)}, bf16[6,128,256]{2,1,0:T(8,128)(2,1)S(1)}, u32[]{:S(2)}, u32[]{:S(2)}) collective-permute-start(bf16[6,128,256]{2,1,0:T(8,128)(2,1)S(1)} %collective-permute-done.8.refs_8_), channel_id=1, source_target_pairs={{0,112},{16,0},{32,16},{48,32},{64,48},{80,64},{96,80},{112,96},{1... | collective-permute-start | bytes 1179656 | tf_op jit(solution)/shard_map/ppermute | solution.py:44
  38.0 0.5 collective-permute-start.3
  38.5 5.9 %collective-permute-done.10.refs_0_ = bf16[6,128,256]{2,1,0:T(8,128)(2,1)S(1)} collective-permute-done((bf16[6,128,256]{2,1,0:T(8,128)(2,1)S(1)}, bf16[6,128,256]{2,1,0:T(8,128)(2,1)S(1)}, u32[]{:S(2)}, u32[]{:S(2)}) %collective-permute-start.10) | collective-permute-done | bytes 393248 | tf_op jit(solution)/shard_map/ppermute | solution.py:44
  44.4 0.5 collective-permute-start.9
  44.9 0.7 reduce
  45.6 0.6 fusion.13.pos_ref
  46.3 0.7 slice.104
  47.0 0.7 slice.103
  47.6 2.5 %collective-permute-start.15 = (bf16[3,128,256]{2,1,0:T(8,128)(2,1)}, bf16[3,128,256]{2,1,0:T(8,128)(2,1)}, u32[]{:S(2)}, u32[]{:S(2)}) collective-permute-start(bf16[3,128,256]{2,1,0:T(8,128)(2,1)} %slice.104), channel_id=1, source_target_pairs={{0,112},{16,0},{32,16},{48,32},{64,48},{80,64},{96,80},{112,96},{1... | collective-permute-start | bytes 589832 | tf_op jit(solution)/shard_map/ppermute | solution.py:44
  50.2 0.7 convert_reduce_fusion.starts_ref.before_hbm
  50.9 1.3 reduce.1.row_ref
  52.2 8.2 %forward_tiles.2 = (f32[25,128,256]{2,1,0:T(8,128)}, s32[1]{0:T(128)}) custom-call(s32[17]{0:T(128)} %convert_reduce_fusion.starts_ref.before_hbm, s32[1]{0:T(128)} %bitcast.z_ref, s32[288]{0:T(512)} %reduce.1.row_ref, s32[288]{0:T(512)} %fusion.13.pos_ref, bf16[288,128,128]{2,1,0:T(8,128)(2,1)} %bitcast.8, s32[17]{0:T(128)} %convert_reduce_fusion.starts_ref.before_hbm, ...), custom_call_target="tpu_custom_call" | custom-call | flops 1509949440 | bytes 17694720 | tf_op jit(solution)/shard_map/forward_tiles/pallas_call | solution.py:164
  61.3 0.5 collective-permute-start.13
  61.8 1.1 broadcast_select_fusion
  62.8 0.4 collective-permute-start.16
  63.2 0.4 collective-permute-start.17
  63.6 0.9 collective-permute-done.16.refs_6_
  64.5 0.3 collective-permute-done.17.refs_7_
  64.8 0.4 copy-done.20
  65.2 0.3 copy-done.21
  65.5 7.0 %forward_tiles.3 = bf16[24,128,256]{2,1,0:T(8,128)(2,1)} custom-call(s32[17]{0:T(128)} %convert_reduce_fusion.starts_ref.before_hbm, s32[1]{0:T(128)} %bitcast.z_ref, s32[288]{0:T(512)} %reduce.1.row_ref, s32[288]{0:T(512)} %fusion.13.pos_ref, bf16[288,128,128]{2,1,0:T(8,128)(2,1)} %bitcast.9, f32[25,128,256]{2,1,0:T(8,128)} %get-tuple-element.24.before_hbm, ...), custom_call_target="tpu_custom_call" | custom-call | flops 905969664 | bytes 10616832 | tf_op jit(solution)/shard_map/forward_tiles/pallas_call | solution.py:164
  72.5 29.3 %all_to_all.19.parts_ref = bf16[8,384,256]{2,1,0:T(8,128)(2,1)} all-to-all(bf16[8,384,256]{2,1,0:T(8,128)(2,1)} %bitcast.11), channel_id=1, replica_groups=mesh['xh'=2,'z'=8,'core'=2,'y'=4,'xl'=2] {'y','xl'}, dimensions={0} | all-to-all | bytes 3145728 | tf_op jit(solution)/shard_map/all_to_all | solution.py:391
  101.8 3.5 %dense_block.1 = (bf16[384,256]{1,0:T(8,128)(2,1)}, bf16[8,432,256]{2,1,0:T(8,128)(2,1)}) custom-call(bf16[8,384,256]{2,1,0:T(8,128)(2,1)} %all_to_all.19.parts_ref, bf16[256,256]{1,0:T(8,128)(2,1)} %weight_ref.1, f32[1,256]{1,0:T(1,128)} %bitcast.15, bf16[384,256]{1,0:T(8,128)(2,1)} %cot_ref.1), custom_call_target="tpu_custom_call" | custom-call | tf_op jit(solution)/shard_map/dense_block/pallas_call | solution.py:279
  105.2 25.6 %all_to_all.20.err_hbm = bf16[8,432,256]{2,1,0:T(8,128)(2,1)} all-to-all(bf16[8,432,256]{2,1,0:T(8,128)(2,1)} %get-tuple-element.27), channel_id=1, replica_groups=mesh['xh'=2,'z'=8,'core'=2,'y'=4,'xl'=2] {'y','xl'}, dimensions={0} | all-to-all | bytes 3538944 | tf_op jit(solution)/shard_map/all_to_all | solution.py:396
  130.8 10.6 %backward_tiles.1 = (bf16[768,256]{1,0:T(8,128)(2,1)}, bf16[768,256]{1,0:T(8,128)(2,1)}, bf16[768,256]{1,0:T(8,128)(2,1)}, bf16[768,256]{1,0:T(8,128)(2,1)}, bf1...) custom-call(s32[17]{0:T(128)} %convert_reduce_fusion.starts_ref.befo, ...), custom_call_target="tpu_custom_call" | custom-call | flops 2415919104 | bytes 28311552 | tf_op jit(solution)/shard_map/backward_tiles/pallas_call | solution.py:230
  141.5 0.5 collective-permute-start.21
  142.1 0.4 collective-permute-start.20
  142.5 0.9 collective-permute-done.28
  143.4 1.1 convert_add_fusion.1
  144.8 2.2 collective-permute-start.29
  147.2 5.1 %collective-permute-done.29 = bf16[432,256]{1,0:T(8,128)(2,1)S(1)} collective-permute-done((bf16[432,256]{1,0:T(8,128)(2,1)S(1)}, bf16[432,256]{1,0:T(8,128)(2,1)S(1)}, u32[]{:S(2)}, u32[]{:S(2)}) %collective-permute-start.29) | collective-permute-done | bytes 221216 | tf_op jit(solution)/shard_map/ppermute | solution.py:44
  152.4 3.4 %collective-permute-start.30 = (bf16[816,256]{1,0:T(8,128)(2,1)S(1)}, bf16[816,256]{1,0:T(8,128)(2,1)S(1)}, u32[]{:S(2)}, u32[]{:S(2)}) collective-permute-start(bf16[816,256]{1,0:T(8,128)(2,1)S(1)} %pad_maximum_fusion.1), channel_id=1, source_target_pairs={{0,112},{16,0},{32,16},{48,32},{64,48},{80,64},{96,80},{112,96},{1... | collective-permute-start | bytes 1253384 | tf_op jit(solution)/shard_map/ppermute | solution.py:44
  156.1 0.5 collective-permute-start.27
  156.6 8.4 %collective-permute-done.30 = bf16[816,256]{1,0:T(8,128)(2,1)S(1)} collective-permute-done((bf16[816,256]{1,0:T(8,128)(2,1)S(1)}, bf16[816,256]{1,0:T(8,128)(2,1)S(1)}, u32[]{:S(2)}, u32[]{:S(2)}) %collective-permute-start.30) | collective-permute-done | bytes 417824 | tf_op jit(solution)/shard_map/ppermute | solution.py:44
  165.1 0.2 fusion.1
  165.3 2.9 %collective-permute-start.32 = (bf16[816,256]{1,0:T(8,128)(2,1)S(1)}, bf16[816,256]{1,0:T(8,128)(2,1)S(1)}, u32[]{:S(2)}, u32[]{:S(2)}) collective-permute-start(bf16[816,256]{1,0:T(8,128)(2,1)S(1)} %fusion.1), channel_id=1, source_target_pairs={{0,112},{16,0},{32,16},{48,32},{64,48},{80,64},{96,80},{112,96},{1... | collective-permute-start | bytes 1253384 | tf_op jit(solution)/shard_map/ppermute | solution.py:44
  168.2 0.2 fusion
  168.5 1.0 collective-permute-start.25
  169.5 0.5 collective-permute-start.18
  170.0 8.0 %collective-permute-done.32 = bf16[816,256]{1,0:T(8,128)(2,1)S(1)} collective-permute-done((bf16[816,256]{1,0:T(8,128)(2,1)S(1)}, bf16[816,256]{1,0:T(8,128)(2,1)S(1)}, u32[]{:S(2)}, u32[]{:S(2)}) %collective-permute-start.32) | collective-permute-done | bytes 417824 | tf_op jit(solution)/shard_map/ppermute | solution.py:44
  178.1 1.5 collective-permute-start.33
  179.6 0.2 add_convert_fusion.3
  179.8 1.0 collective-permute-start.26
  180.8 7.2 %collective-permute-start.35 = (bf16[48,256]{1,0:T(8,128)(2,1)S(1)}, bf16[48,256]{1,0:T(8,128)(2,1)S(1)}, u32[]{:S(2)}, u32[]{:S(2)}) collective-permute-start(bf16[48,256]{1,0:T(8,128)(2,1)S(1)} %slice.121.refs_0_), channel_id=1, source_target_pairs={{0,64},{16,80},{32,96},{48,112},{64,0},{80,16},{96,32},{112,48},{1... | collective-permute-start | bytes 73736 | tf_op jit(solution)/shard_map/ppermute | solution.py:44
  188.0 7.1 %collective-permute-done.35.refs_4_ = bf16[48,256]{1,0:T(8,128)(2,1)S(1)} collective-permute-done((bf16[48,256]{1,0:T(8,128)(2,1)S(1)}, bf16[48,256]{1,0:T(8,128)(2,1)S(1)}, u32[]{:S(2)}, u32[]{:S(2)}) %collective-permute-start.35) | collective-permute-done | bytes 24608 | tf_op jit(solution)/shard_map/ppermute | solution.py:44
  195.2 3.5 %collective-permute-start.36 = (bf16[48,256]{1,0:T(8,128)(2,1)S(1)}, bf16[48,256]{1,0:T(8,128)(2,1)S(1)}, u32[]{:S(2)}, u32[]{:S(2)}) collective-permute-start(bf16[48,256]{1,0:T(8,128)(2,1)S(1)} %convert_element_type.148), channel_id=1, source_target_pairs={{0,128},{128,0},{1,129},{129,1},{2,130},{130,2},{3,131},{131,3},{4... | collective-permute-start | bytes 73736 | tf_op jit(solution)/shard_map/ppermute | solution.py:40
  198.7 1.9 collective-permute-done.36
  200.6 0.7 tile.2
  201.4 8.4 %all-to-all-start.2 = ((f32[8,32,256]{2,1,0:T(8,128)}), f32[8,32,256]{2,1,0:T(8,128)S(1)}, u32[]{:S(2)}, u32[]{:S(2)}) async-start(f32[8,32,256]{2,1,0:T(8,128)} %tile.2), calls=%async_computation.2 | async-start | bytes 524288 | tf_op jit(solution)/shard_map/all_to_all | solution.py:399
  209.8 0.2 convert_add_fusion
  210.1 3.1 %collective-permute-start.34 = (bf16[384,256]{1,0:T(8,128)(2,1)S(1)}, bf16[384,256]{1,0:T(8,128)(2,1)S(1)}, u32[]{:S(2)}, u32[]{:S(2)}) collective-permute-start(bf16[384,256]{1,0:T(8,128)(2,1)S(1)} %slice.146), channel_id=1, source_target_pairs={{0,128},{128,0},{1,129},{129,1},{2,130},{130,2},{3,131},{131,3},{4... | collective-permute-start | bytes 589832 | tf_op jit(solution)/shard_map/ppermute | solution.py:40
  213.2 0.6 slice.127
  213.7 2.2 all-to-all-done.2
  215.9 2.2 collective-permute-done.34
  218.1 0.7 fusion.2
  218.8 0.7 copy.14
  (110 shorter events, 1.4 us)
Async XLA Ops:
  0.6 8.4 %collective-permute-start = (bf16[3,128,256]{2,1,0:T(8,128)(2,1)}, bf16[3,128,256]{2,1,0:T(8,128)(2,1)S(1)}, u32[]{:S(2)}, u32[]{:S(2)}) collective-permute-start(bf16[3,128,256]{2,1,0:T(8,128)(2,1)} %bitcast.13), channel_id=1, source_target_pairs={{0,128},{128,0},{1,129},{129,1},{2,130},{130,2},{3,131},{131,3},{4... | collective-permute-start | bytes 589832 | tf_op jit(solution)/shard_map/ppermute | solution.py:40
  10.0 42.1 %copy-start = (bf16[6,128,256]{2,1,0:T(8,128)(2,1)}, bf16[6,128,256]{2,1,0:T(8,128)(2,1)S(1)}, u32[]{:S(2)}) copy-start(bf16[6,128,256]{2,1,0:T(8,128)(2,1)S(1)} %pad_maximum_fusion.2.refs_0_) | copy-start | bytes 1179652
  10.0 14.2 %collective-permute-start.2 = (bf16[6,128,256]{2,1,0:T(8,128)(2,1)S(1)}, bf16[6,128,256]{2,1,0:T(8,128)(2,1)S(1)}, u32[]{:S(2)}, u32[]{:S(2)}) collective-permute-start(bf16[6,128,256]{2,1,0:T(8,128)(2,1)S(1)} %pad_maximum_fusion.2.refs_0_), channel_id=1, source_target_pairs={{0,16},{16,32},{32,48},{48,64},{64,80},{80,96},{96,112},{112,0},{1... | collective-permute-start | bytes 1179656 | tf_op jit(solution)/shard_map/ppermute | solution.py:44
  12.0 12.2 %collective-permute-start.4 = (bf16[6,128,256]{2,1,0:T(8,128)(2,1)S(1)}, bf16[6,128,256]{2,1,0:T(8,128)(2,1)S(1)}, u32[]{:S(2)}, u32[]{:S(2)}) collective-permute-start(bf16[6,128,256]{2,1,0:T(8,128)(2,1)S(1)} %pad_maximum_fusion.2.refs_0_), channel_id=1, source_target_pairs={{0,112},{16,0},{32,16},{48,32},{64,48},{80,64},{96,80},{112,96},{1... | collective-permute-start | bytes 1179656 | tf_op jit(solution)/shard_map/ppermute | solution.py:44
  24.2 27.9 %copy-start.6 = (bf16[6,128,256]{2,1,0:T(8,128)(2,1)}, bf16[6,128,256]{2,1,0:T(8,128)(2,1)S(1)}, u32[]{:S(2)}) copy-start(bf16[6,128,256]{2,1,0:T(8,128)(2,1)S(1)} %collective-permute-done.2.refs_2_) | copy-start | bytes 1179652
  24.2 10.6 %collective-permute-start.6 = (bf16[6,128,256]{2,1,0:T(8,128)(2,1)S(1)}, bf16[6,128,256]{2,1,0:T(8,128)(2,1)S(1)}, u32[]{:S(2)}, u32[]{:S(2)}) collective-permute-start(bf16[6,128,256]{2,1,0:T(8,128)(2,1)S(1)} %collective-permute-done.2.refs_2_), channel_id=1, source_target_pairs={{0,16},{16,32},{32,48},{48,64},{64,80},{80,96},{96,112},{112,0},{1... | collective-permute-start | bytes 1179656 | tf_op jit(solution)/shard_map/ppermute | solution.py:44
  24.2 27.9 %copy-start.7 = (bf16[6,128,256]{2,1,0:T(8,128)(2,1)}, bf16[6,128,256]{2,1,0:T(8,128)(2,1)S(1)}, u32[]{:S(2)}) copy-start(bf16[6,128,256]{2,1,0:T(8,128)(2,1)S(1)} %collective-permute-done.4.refs_4_) | copy-start | bytes 1179652
  24.2 10.5 %collective-permute-start.8 = (bf16[6,128,256]{2,1,0:T(8,128)(2,1)S(1)}, bf16[6,128,256]{2,1,0:T(8,128)(2,1)S(1)}, u32[]{:S(2)}, u32[]{:S(2)}) collective-permute-start(bf16[6,128,256]{2,1,0:T(8,128)(2,1)S(1)} %collective-permute-done.4.refs_4_), channel_id=1, source_target_pairs={{0,112},{16,0},{32,16},{48,32},{64,48},{80,64},{96,80},{112,96},{1... | collective-permute-start | bytes 1179656 | tf_op jit(solution)/shard_map/ppermute | solution.py:44
  34.8 17.4 %copy-start.8 = (bf16[6,128,256]{2,1,0:T(8,128)(2,1)}, bf16[6,128,256]{2,1,0:T(8,128)(2,1)S(1)}, u32[]{:S(2)}) copy-start(bf16[6,128,256]{2,1,0:T(8,128)(2,1)S(1)} %collective-permute-done.6.refs_6_) | copy-start | bytes 1179652
  34.8 9.6 %collective-permute-start.10 = (bf16[6,128,256]{2,1,0:T(8,128)(2,1)S(1)}, bf16[6,128,256]{2,1,0:T(8,128)(2,1)S(1)}, u32[]{:S(2)}, u32[]{:S(2)}) collective-permute-start(bf16[6,128,256]{2,1,0:T(8,128)(2,1)S(1)} %collective-permute-done.6.refs_6_), channel_id=1, source_target_pairs={{0,16},{16,32},{32,48},{48,64},{64,80},{80,96},{96,112},{112,0},{1... | collective-permute-start | bytes 1179656 | tf_op jit(solution)/shard_map/ppermute | solution.py:44
  34.8 17.4 %copy-start.9 = (bf16[6,128,256]{2,1,0:T(8,128)(2,1)}, bf16[6,128,256]{2,1,0:T(8,128)(2,1)S(1)}, u32[]{:S(2)}) copy-start(bf16[6,128,256]{2,1,0:T(8,128)(2,1)S(1)} %collective-permute-done.8.refs_8_) | copy-start | bytes 1179652
  34.8 9.6 %collective-permute-start.12 = (bf16[6,128,256]{2,1,0:T(8,128)(2,1)S(1)}, bf16[6,128,256]{2,1,0:T(8,128)(2,1)S(1)}, u32[]{:S(2)}, u32[]{:S(2)}) collective-permute-start(bf16[6,128,256]{2,1,0:T(8,128)(2,1)S(1)} %collective-permute-done.8.refs_8_), channel_id=1, source_target_pairs={{0,112},{16,0},{32,16},{48,32},{64,48},{80,64},{96,80},{112,96},{1... | collective-permute-start | bytes 1179656 | tf_op jit(solution)/shard_map/ppermute | solution.py:44
  38.0 9.6 %collective-permute-start.1 = (bf16[6,128,256]{2,1,0:T(8,128)(2,1)S(1)}, bf16[6,128,256]{2,1,0:T(8,128)(2,1)S(1)}, u32[]{:S(2)}, u32[]{:S(2)}) collective-permute-start(bf16[6,128,256]{2,1,0:T(8,128)(2,1)S(1)} %pad_maximum_fusion.2.refs_0_), channel_id=1, source_target_pairs={{0,8},{8,0},{1,9},{9,1},{2,10},{10,2},{3,11},{11,3},{4,12},{12,4},... | collective-permute-start | bytes 1179656 | tf_op jit(solution)/shard_map/ppermute | solution.py:40
  38.0 12.1 %collective-permute-start.3 = (bf16[6,128,256]{2,1,0:T(8,128)(2,1)S(1)}, bf16[6,128,256]{2,1,0:T(8,128)(2,1)S(1)}, u32[]{:S(2)}, u32[]{:S(2)}) collective-permute-start(bf16[6,128,256]{2,1,0:T(8,128)(2,1)S(1)} %collective-permute-done.2.refs_2_), channel_id=1, source_target_pairs={{0,8},{8,0},{1,9},{9,1},{2,10},{10,2},{3,11},{11,3},{4,12},{12,4},... | collective-permute-start | bytes 1179656 | tf_op jit(solution)/shard_map/ppermute | solution.py:40
  38.5 13.6 %collective-permute-start.5 = (bf16[6,128,256]{2,1,0:T(8,128)(2,1)S(1)}, bf16[6,128,256]{2,1,0:T(8,128)(2,1)}, u32[]{:S(2)}, u32[]{:S(2)}) collective-permute-start(bf16[6,128,256]{2,1,0:T(8,128)(2,1)S(1)} %collective-permute-done.4.refs_4_), channel_id=1, source_target_pairs={{0,8},{8,0},{1,9},{9,1},{2,10},{10,2},{3,11},{11,3},{4,12},{12,4},... | collective-permute-start | bytes 1179656 | tf_op jit(solution)/shard_map/ppermute | solution.py:40
  44.4 16.7 %copy-start.1 = (bf16[6,128,256]{2,1,0:T(8,128)(2,1)}, bf16[6,128,256]{2,1,0:T(8,128)(2,1)S(1)}, u32[]{:S(2)}) copy-start(bf16[6,128,256]{2,1,0:T(8,128)(2,1)S(1)} %collective-permute-done.10.refs_0_) | copy-start | bytes 1179652
  44.4 7.7 %collective-permute-start.7 = (bf16[6,128,256]{2,1,0:T(8,128)(2,1)S(1)}, bf16[6,128,256]{2,1,0:T(8,128)(2,1)}, u32[]{:S(2)}, u32[]{:S(2)}) collective-permute-start(bf16[6,128,256]{2,1,0:T(8,128)(2,1)S(1)} %collective-permute-done.6.refs_6_), channel_id=1, source_target_pairs={{0,8},{8,0},{1,9},{9,1},{2,10},{10,2},{3,11},{11,3},{4,12},{12,4},... | collective-permute-start | bytes 1179656 | tf_op jit(solution)/shard_map/ppermute | solution.py:40
  44.4 16.8 %copy-start.2 = (bf16[6,128,256]{2,1,0:T(8,128)(2,1)}, bf16[6,128,256]{2,1,0:T(8,128)(2,1)S(1)}, u32[]{:S(2)}) copy-start(bf16[6,128,256]{2,1,0:T(8,128)(2,1)S(1)} %collective-permute-done.12.refs_2_) | copy-start | bytes 1179652
  44.4 7.7 %collective-permute-start.9 = (bf16[6,128,256]{2,1,0:T(8,128)(2,1)S(1)}, bf16[6,128,256]{2,1,0:T(8,128)(2,1)}, u32[]{:S(2)}, u32[]{:S(2)}) collective-permute-start(bf16[6,128,256]{2,1,0:T(8,128)(2,1)S(1)} %collective-permute-done.8.refs_8_), channel_id=1, source_target_pairs={{0,8},{8,0},{1,9},{9,1},{2,10},{10,2},{3,11},{11,3},{4,12},{12,4},... | collective-permute-start | bytes 1179656 | tf_op jit(solution)/shard_map/ppermute | solution.py:40
  47.6 4.6 %copy-start.10 = (bf16[6,128,256]{2,1,0:T(8,128)(2,1)}, bf16[6,128,256]{2,1,0:T(8,128)(2,1)S(1)}, u32[]{:S(2)}) copy-start(bf16[6,128,256]{2,1,0:T(8,128)(2,1)S(1)} %collective-permute-done.1.refs_1_) | copy-start | bytes 1179652
  47.6 14.1 %collective-permute-start.15 = (bf16[3,128,256]{2,1,0:T(8,128)(2,1)}, bf16[3,128,256]{2,1,0:T(8,128)(2,1)}, u32[]{:S(2)}, u32[]{:S(2)}) collective-permute-start(bf16[3,128,256]{2,1,0:T(8,128)(2,1)} %slice.104), channel_id=1, source_target_pairs={{0,112},{16,0},{32,16},{48,32},{64,48},{80,64},{96,80},{112,96},{1... | collective-permute-start | bytes 589832 | tf_op jit(solution)/shard_map/ppermute | solution.py:44
  50.2 2.1 copy-start.11
  50.2 11.6 %collective-permute-start.14 = (bf16[3,128,256]{2,1,0:T(8,128)(2,1)}, bf16[3,128,256]{2,1,0:T(8,128)(2,1)}, u32[]{:S(2)}, u32[]{:S(2)}) collective-permute-start(bf16[3,128,256]{2,1,0:T(8,128)(2,1)} %slice.103), channel_id=1, source_target_pairs={{0,16},{16,32},{32,48},{48,64},{64,80},{80,96},{96,112},{112,0},{1... | collective-permute-start | bytes 589832 | tf_op jit(solution)/shard_map/ppermute | solution.py:44
  61.1 2.5 %collective-permute-start.11 = (bf16[6,128,256]{2,1,0:T(8,128)(2,1)S(1)}, bf16[6,128,256]{2,1,0:T(8,128)(2,1)S(1)}, u32[]{:S(2)}, u32[]{:S(2)}) collective-permute-start(bf16[6,128,256]{2,1,0:T(8,128)(2,1)S(1)} %collective-permute-done.10.refs_0_), channel_id=1, source_target_pairs={{0,8},{8,0},{1,9},{9,1},{2,10},{10,2},{3,11},{11,3},{4,12},{12,4},... | collective-permute-start | bytes 1179656 | tf_op jit(solution)/shard_map/ppermute | solution.py:40
  61.3 2.4 %collective-permute-start.13 = (bf16[6,128,256]{2,1,0:T(8,128)(2,1)S(1)}, bf16[6,128,256]{2,1,0:T(8,128)(2,1)S(1)}, u32[]{:S(2)}, u32[]{:S(2)}) collective-permute-start(bf16[6,128,256]{2,1,0:T(8,128)(2,1)S(1)} %collective-permute-done.12.refs_2_), channel_id=1, source_target_pairs={{0,8},{8,0},{1,9},{9,1},{2,10},{10,2},{3,11},{11,3},{4,12},{12,4},... | collective-permute-start | bytes 1179656 | tf_op jit(solution)/shard_map/ppermute | solution.py:40
  62.8 2.0 copy-start.3
  62.8 2.0 copy-start.4
  62.8 1.7 collective-permute-start.16
  63.2 1.6 collective-permute-start.17
  63.6 1.2 copy-start.18
  63.6 1.2 copy-start.19
  64.5 0.7 copy-start.20
  64.8 0.7 copy-start.21
  141.4 3.2 %copy-start.5 = (bf16[816,256]{1,0:T(8,128)(2,1)S(1)}, bf16[816,256]{1,0:T(8,128)(2,1)}, u32[]{:S(2)}) copy-start(bf16[816,256]{1,0:T(8,128)(2,1)} %get-tuple-element.34) | copy-start | bytes 1253380
  141.4 2.0 collective-permute-start.28
  141.5 3.1 %collective-permute-start.21 = (bf16[816,256]{1,0:T(8,128)(2,1)}, bf16[816,256]{1,0:T(8,128)(2,1)S(1)}, u32[]{:S(2)}, u32[]{:S(2)}) collective-permute-start(bf16[816,256]{1,0:T(8,128)(2,1)} %get-tuple-element.35), channel_id=1, source_target_pairs={{0,8},{8,0},{1,9},{9,1},{2,10},{10,2},{3,11},{11,3},{4,12},{12,4},... | collective-permute-start | bytes 1253384 | tf_op jit(solution)/shard_map/ppermute | solution.py:40
  142.0 23.1 %collective-permute-start.31 = (bf16[768,256]{1,0:T(8,128)(2,1)}, bf16[768,256]{1,0:T(8,128)(2,1)S(1)}, u32[]{:S(2)}, u32[]{:S(2)}) collective-permute-start(bf16[768,256]{1,0:T(8,128)(2,1)} %get-tuple-element.43), channel_id=1, source_target_pairs={{0,8},{8,0},{1,9},{9,1},{2,10},{10,2},{3,11},{11,3},{4,12},{12,4},... | collective-permute-start | bytes 1179656 | tf_op jit(solution)/shard_map/ppermute | solution.py:40
  142.1 4.8 %collective-permute-start.20 = (bf16[768,256]{1,0:T(8,128)(2,1)}, bf16[768,256]{1,0:T(8,128)(2,1)S(1)}, u32[]{:S(2)}, u32[]{:S(2)}) collective-permute-start(bf16[768,256]{1,0:T(8,128)(2,1)} %get-tuple-element.33), channel_id=1, source_target_pairs={{0,8},{8,0},{1,9},{9,1},{2,10},{10,2},{3,11},{11,3},{4,12},{12,4},... | collective-permute-start | bytes 1179656 | tf_op jit(solution)/shard_map/ppermute | solution.py:40
  143.4 3.5 %copy-start.17 = (bf16[768,256]{1,0:T(8,128)(2,1)S(1)}, bf16[768,256]{1,0:T(8,128)(2,1)}, u32[]{:S(2)}) copy-start(bf16[768,256]{1,0:T(8,128)(2,1)} %get-tuple-element.32) | copy-start | bytes 1179652
  144.8 7.5 %collective-permute-start.29 = (bf16[432,256]{1,0:T(8,128)(2,1)S(1)}, bf16[432,256]{1,0:T(8,128)(2,1)S(1)}, u32[]{:S(2)}, u32[]{:S(2)}) collective-permute-start(bf16[432,256]{1,0:T(8,128)(2,1)S(1)} %get-tuple-element.45), channel_id=1, source_target_pairs={{0,112},{16,0},{32,16},{48,32},{64,48},{80,64},{96,80},{112,96},{1... | collective-permute-start | bytes 663560 | tf_op jit(solution)/shard_map/ppermute | solution.py:44
  147.1 9.0 %copy-start.25 = (bf16[768,256]{1,0:T(8,128)(2,1)S(1)}, bf16[768,256]{1,0:T(8,128)(2,1)}, u32[]{:S(2)}) copy-start(bf16[768,256]{1,0:T(8,128)(2,1)} %get-tuple-element.37) | copy-start | bytes 1179652
  147.1 9.1 %copy-start.24 = (bf16[768,256]{1,0:T(8,128)(2,1)S(1)}, bf16[768,256]{1,0:T(8,128)(2,1)}, u32[]{:S(2)}) copy-start(bf16[768,256]{1,0:T(8,128)(2,1)} %get-tuple-element.39) | copy-start | bytes 1179652
  147.1 18.0 %copy-start.16 = (bf16[768,256]{1,0:T(8,128)(2,1)S(1)}, bf16[768,256]{1,0:T(8,128)(2,1)}, u32[]{:S(2)}) copy-start(bf16[768,256]{1,0:T(8,128)(2,1)} %get-tuple-element.42) | copy-start | bytes 1179652
  147.1 8.7 %collective-permute-start.22 = (bf16[432,256]{1,0:T(8,128)(2,1)S(1)}, bf16[432,256]{1,0:T(8,128)(2,1)S(1)}, u32[]{:S(2)}, u32[]{:S(2)}) collective-permute-start(bf16[432,256]{1,0:T(8,128)(2,1)S(1)} %get-tuple-element.44), channel_id=1, source_target_pairs={{0,16},{16,32},{32,48},{48,64},{64,80},{80,96},{96,112},{112,0},{1... | collective-permute-start | bytes 663560 | tf_op jit(solution)/shard_map/ppermute | solution.py:44
  152.4 15.8 %copy-start.15 = (bf16[768,256]{1,0:T(8,128)(2,1)S(1)}, bf16[768,256]{1,0:T(8,128)(2,1)}, u32[]{:S(2)}) copy-start(bf16[768,256]{1,0:T(8,128)(2,1)} %get-tuple-element.36) | copy-start | bytes 1179652
  152.4 12.6 %collective-permute-start.30 = (bf16[816,256]{1,0:T(8,128)(2,1)S(1)}, bf16[816,256]{1,0:T(8,128)(2,1)S(1)}, u32[]{:S(2)}, u32[]{:S(2)}) collective-permute-start(bf16[816,256]{1,0:T(8,128)(2,1)S(1)} %pad_maximum_fusion.1), channel_id=1, source_target_pairs={{0,112},{16,0},{32,16},{48,32},{64,48},{80,64},{96,80},{112,96},{1... | collective-permute-start | bytes 1253384 | tf_op jit(solution)/shard_map/ppermute | solution.py:44
  155.9 13.6 %copy-start.23 = (bf16[768,256]{1,0:T(8,128)(2,1)S(1)}, bf16[768,256]{1,0:T(8,128)(2,1)}, u32[]{:S(2)}) copy-start(bf16[768,256]{1,0:T(8,128)(2,1)} %get-tuple-element.31) | copy-start | bytes 1179652
  155.9 13.6 %copy-start.22 = (bf16[768,256]{1,0:T(8,128)(2,1)S(1)}, bf16[768,256]{1,0:T(8,128)(2,1)}, u32[]{:S(2)}) copy-start(bf16[768,256]{1,0:T(8,128)(2,1)} %get-tuple-element.29) | copy-start | bytes 1179652
  155.9 22.0 %copy-start.14 = (bf16[768,256]{1,0:T(8,128)(2,1)S(1)}, bf16[768,256]{1,0:T(8,128)(2,1)}, u32[]{:S(2)}) copy-start(bf16[768,256]{1,0:T(8,128)(2,1)} %get-tuple-element.38) | copy-start | bytes 1179652
  155.9 12.3 %collective-permute-start.23 = (bf16[816,256]{1,0:T(8,128)(2,1)S(1)}, bf16[816,256]{1,0:T(8,128)(2,1)S(1)}, u32[]{:S(2)}, u32[]{:S(2)}) collective-permute-start(bf16[816,256]{1,0:T(8,128)(2,1)S(1)} %pad_maximum_fusion), channel_id=1, source_target_pairs={{0,16},{16,32},{32,48},{48,64},{64,80},{80,96},{96,112},{112,0},{1... | collective-permute-start | bytes 1253384 | tf_op jit(solution)/shard_map/ppermute | solution.py:44
  156.0 12.2 %collective-permute-start.24 = (bf16[768,256]{1,0:T(8,128)(2,1)S(1)}, bf16[768,256]{1,0:T(8,128)(2,1)S(1)}, u32[]{:S(2)}, u32[]{:S(2)}) collective-permute-start(bf16[768,256]{1,0:T(8,128)(2,1)S(1)} %copy-done.25), channel_id=1, source_target_pairs={{0,8},{8,0},{1,9},{9,1},{2,10},{10,2},{3,11},{11,3},{4,12},{12,4},... | collective-permute-start | bytes 1179656 | tf_op jit(solution)/shard_map/ppermute | solution.py:40
  156.1 13.9 %collective-permute-start.27 = (bf16[768,256]{1,0:T(8,128)(2,1)S(1)}, bf16[768,256]{1,0:T(8,128)(2,1)S(1)}, u32[]{:S(2)}, u32[]{:S(2)}) collective-permute-start(bf16[768,256]{1,0:T(8,128)(2,1)S(1)} %copy-done.24), channel_id=1, source_target_pairs={{0,8},{8,0},{1,9},{9,1},{2,10},{10,2},{3,11},{11,3},{4,12},{12,4},... | collective-permute-start | bytes 1179656 | tf_op jit(solution)/shard_map/ppermute | solution.py:40
  165.3 14.3 %copy-start.13 = (bf16[768,256]{1,0:T(8,128)(2,1)S(1)}, bf16[768,256]{1,0:T(8,128)(2,1)}, u32[]{:S(2)}) copy-start(bf16[768,256]{1,0:T(8,128)(2,1)} %get-tuple-element.30) | copy-start | bytes 1179652
  165.3 12.6 %collective-permute-start.32 = (bf16[816,256]{1,0:T(8,128)(2,1)S(1)}, bf16[816,256]{1,0:T(8,128)(2,1)S(1)}, u32[]{:S(2)}, u32[]{:S(2)}) collective-permute-start(bf16[816,256]{1,0:T(8,128)(2,1)S(1)} %fusion.1), channel_id=1, source_target_pairs={{0,112},{16,0},{32,16},{48,32},{64,48},{80,64},{96,80},{112,96},{1... | collective-permute-start | bytes 1253384 | tf_op jit(solution)/shard_map/ppermute | solution.py:44
  168.5 11.1 %collective-permute-start.25 = (bf16[816,256]{1,0:T(8,128)(2,1)S(1)}, bf16[816,256]{1,0:T(8,128)(2,1)S(1)}, u32[]{:S(2)}, u32[]{:S(2)}) collective-permute-start(bf16[816,256]{1,0:T(8,128)(2,1)S(1)} %fusion), channel_id=1, source_target_pairs={{0,16},{16,32},{32,48},{48,64},{64,80},{80,96},{96,112},{112,0},{1... | collective-permute-start | bytes 1253384 | tf_op jit(solution)/shard_map/ppermute | solution.py:44
  169.5 10.1 %collective-permute-start.19 = (bf16[768,256]{1,0:T(8,128)(2,1)S(1)}, bf16[768,256]{1,0:T(8,128)(2,1)S(1)}, u32[]{:S(2)}, u32[]{:S(2)}) collective-permute-start(bf16[768,256]{1,0:T(8,128)(2,1)S(1)} %copy-done.23), channel_id=1, source_target_pairs={{0,8},{8,0},{1,9},{9,1},{2,10},{10,2},{3,11},{11,3},{4,12},{12,4},... | collective-permute-start | bytes 1179656 | tf_op jit(solution)/shard_map/ppermute | solution.py:40
  169.5 40.3 %collective-permute-start.18 = (bf16[768,256]{1,0:T(8,128)(2,1)S(1)}, bf16[768,256]{1,0:T(8,128)(2,1)S(1)}, u32[]{:S(2)}, u32[]{:S(2)}) collective-permute-start(bf16[768,256]{1,0:T(8,128)(2,1)S(1)} %copy-done.22), channel_id=1, source_target_pairs={{0,8},{8,0},{1,9},{9,1},{2,10},{10,2},{3,11},{11,3},{4,12},{12,4},... | collective-permute-start | bytes 1179656 | tf_op jit(solution)/shard_map/ppermute | solution.py:40
  178.1 31.7 %copy-start.12 = (bf16[768,256]{1,0:T(8,128)(2,1)S(1)}, bf16[768,256]{1,0:T(8,128)(2,1)}, u32[]{:S(2)}) copy-start(bf16[768,256]{1,0:T(8,128)(2,1)} %get-tuple-element.28) | copy-start | bytes 1179652
  178.1 31.7 %collective-permute-start.33 = (bf16[768,256]{1,0:T(8,128)(2,1)S(1)}, bf16[768,256]{1,0:T(8,128)(2,1)S(1)}, u32[]{:S(2)}, u32[]{:S(2)}) collective-permute-start(bf16[768,256]{1,0:T(8,128)(2,1)S(1)} %add_convert_fusion.1), channel_id=1, source_target_pairs={{0,112},{16,0},{32,16},{48,32},{64,48},{80,64},{96,80},{112,96},{1... | collective-permute-start | bytes 1179656 | tf_op jit(solution)/shard_map/ppermute | solution.py:44
  179.8 30.0 %collective-permute-start.26 = (bf16[768,256]{1,0:T(8,128)(2,1)S(1)}, bf16[768,256]{1,0:T(8,128)(2,1)S(1)}, u32[]{:S(2)}, u32[]{:S(2)}) collective-permute-start(bf16[768,256]{1,0:T(8,128)(2,1)S(1)} %add_convert_fusion.3), channel_id=1, source_target_pairs={{0,16},{16,32},{32,48},{48,64},{64,80},{80,96},{96,112},{112,0},{1... | collective-permute-start | bytes 1179656 | tf_op jit(solution)/shard_map/ppermute | solution.py:44
  180.8 14.4 %collective-permute-start.35 = (bf16[48,256]{1,0:T(8,128)(2,1)S(1)}, bf16[48,256]{1,0:T(8,128)(2,1)S(1)}, u32[]{:S(2)}, u32[]{:S(2)}) collective-permute-start(bf16[48,256]{1,0:T(8,128)(2,1)S(1)} %slice.121.refs_0_), channel_id=1, source_target_pairs={{0,64},{16,80},{32,96},{48,112},{64,0},{80,16},{96,32},{112,48},{1... | collective-permute-start | bytes 73736 | tf_op jit(solution)/shard_map/ppermute | solution.py:44
  195.2 5.4 %collective-permute-start.36 = (bf16[48,256]{1,0:T(8,128)(2,1)S(1)}, bf16[48,256]{1,0:T(8,128)(2,1)S(1)}, u32[]{:S(2)}, u32[]{:S(2)}) collective-permute-start(bf16[48,256]{1,0:T(8,128)(2,1)S(1)} %convert_element_type.148), channel_id=1, source_target_pairs={{0,128},{128,0},{1,129},{129,1},{2,130},{130,2},{3,131},{131,3},{4... | collective-permute-start | bytes 73736 | tf_op jit(solution)/shard_map/ppermute | solution.py:40
  201.4 14.6 %all-to-all-start.2 = ((f32[8,32,256]{2,1,0:T(8,128)}), f32[8,32,256]{2,1,0:T(8,128)S(1)}, u32[]{:S(2)}, u32[]{:S(2)}) async-start(f32[8,32,256]{2,1,0:T(8,128)} %tile.2), calls=%async_computation.2 | async-start | bytes 524288 | tf_op jit(solution)/shard_map/all_to_all | solution.py:399
  210.1 8.0 %collective-permute-start.34 = (bf16[384,256]{1,0:T(8,128)(2,1)S(1)}, bf16[384,256]{1,0:T(8,128)(2,1)S(1)}, u32[]{:S(2)}, u32[]{:S(2)}) collective-permute-start(bf16[384,256]{1,0:T(8,128)(2,1)S(1)} %slice.146), channel_id=1, source_target_pairs={{0,128},{128,0},{1,129},{129,1},{2,130},{130,2},{3,131},{131,3},{4... | collective-permute-start | bytes 589832 | tf_op jit(solution)/shard_map/ppermute | solution.py:40
